TPU v7x, 32 devices: a whole 2x2x4 slice. The times are simulated.
32 devices in a mesh: ctx: 8 (over y, x, core), head: 4 (over z).
Axes of the slice: x: 2, y: 2, z: 4, core: 2. Of those that a mesh axis runs over, the one named last changes fastest.
Arguments:
- queries: bfloat16 [1024, 128, 128], P('ctx', 'head'), may hold values from -64 to 64
- key_states: bfloat16 [1024, 8, 128], P('ctx', 'head'), may hold values from -4 to 4
- value_vector_states: bfloat16 [1024, 8, 128], P('ctx', 'head'), may hold values from -6 to 6
- map_query: float32 [128, 128, 64], P('head'), may hold values from -0.5 to 0.5
- map_key: float32 [128, 128, 64], P('head'), may hold values from -0.5 to 0.5
Outputs:
- grad_map_query: float32 [128, 128, 64], P('head')
- grad_map_key: float32 [128, 128, 64], P('head')
All inputs are finite; a program needn't handle non-finite values.
Results may differ from a plain program's by a relative error of at most 0.0012.
Values may be sent and summed in bfloat16 or wider, within the bound.
No kernel may reach another device: no remote copies, remote signals or barrier semaphores. Data moves between devices by JAX's collectives and lax.ppermute only.
A program may use at most 192 MiB of HBM per device.

v0:
```python
import functools
import math

import jax
import jax.numpy as jnp
import numpy as np
from jax import lax
from jax.experimental import pallas as pl
from jax.experimental.pallas import tpu as pltpu
from jax.sharding import PartitionSpec as P

F32 = jnp.float32
BF16 = jnp.bfloat16
F16 = jnp.float16
VMEM_LIMIT = 56 * 1024 * 1024
TAIL = 16


def dot(a, b):
    return lax.dot_general(a, b, (((1,), (0,)), ((), ())), preferred_element_type=F32)


def dot_nt(a, b):
    return lax.dot_general(a, b, (((1,), (1,)), ((), ())), preferred_element_type=F32)


def halves(x):
    high = x.astype(BF16)
    return high, (x - high.astype(F32)).astype(BF16)


def beside(*parts):
    return jnp.concatenate(parts, axis=1)


def below(*parts):
    return jnp.concatenate(parts, axis=0)


def feature_and_slope(logit):
    grown = jnp.exp(jnp.minimum(logit, 0.0))
    positive = logit > 0
    return jnp.where(positive, logit + 1.0, grown), jnp.where(positive, 1.0, grown)


def causal(rows, columns, shift):
    row = lax.broadcasted_iota(jnp.int32, (rows, columns), 0)
    column = lax.broadcasted_iota(jnp.int32, (rows, columns), 1)
    return column <= row + shift


def teacher_kernel(scale, rows, q_ref, k_ref, v_ref, out_ref, energy_ref, scores_ref):
    blocks, _, chunk, dim = q_ref.shape
    per_row = rows // chunk
    steps = blocks // per_row
    power = scale * math.log2(math.e)
    mask = causal(rows, rows, 0)

    def finish(r, weighted, total):
        teacher = weighted / total
        for i in range(per_row):
            out_ref[r * per_row + i, 0] = teacher[i * chunk : (i + 1) * chunk]
        return jnp.sum((teacher * teacher).reshape(rows // 8, 8, dim), axis=0)

    def take(ref, r, count=1):
        return ref[pl.ds(r * per_row, count * per_row), 0].reshape(count * rows, dim)

    if steps <= 8:
        energy = jnp.zeros((8, dim), F32)
        for r in range(steps):
            q = take(q_ref, r)
            keys = take(k_ref, 0, r + 1)
            scores = dot_nt(q, keys)
            last = jnp.where(mask, scores[:, r * rows :], -1e30)
            scores = beside(scores[:, : r * rows], last) if r else last
            top = jnp.max(scores, axis=1, keepdims=True)
            weights = jnp.exp2((scores - top) * power)
            total = jnp.sum(weights, axis=1, keepdims=True)
            weighted = dot(weights.astype(BF16), take(v_ref, 0, r + 1))
            energy = energy + finish(r, weighted, total)
    else:

        def one_row(r, energy):
            q = take(q_ref, r)

            def look(j, top):
                scores = dot_nt(q, take(k_ref, j))
                scores = jnp.where((j < r) | mask, scores, -1e30)
                scores_ref[j] = scores
                return jnp.maximum(top, jnp.max(scores, axis=1, keepdims=True))

            top = lax.fori_loop(0, r + 1, look, jnp.full((rows, 1), -1e30, F32))

            def add(j, state):
                weighted, total = state
                weights = jnp.exp2((scores_ref[j] - top) * power)
                total = total + jnp.sum(weights, axis=1, keepdims=True)
                return weighted + dot(weights.astype(BF16), take(v_ref, j)), total

            weighted, total = lax.fori_loop(
                0, r + 1, add, (jnp.zeros((rows, dim), F32), jnp.zeros((rows, 1), F32))
            )
            return energy + finish(r, weighted, total)

        energy = lax.fori_loop(0, steps, one_row, jnp.zeros((8, dim), F32))
    energy_ref[0] = energy


def teacher_call(x, heads):
    blocks, _, chunk, dim = x.shape
    rows = 2 * chunk if blocks % 2 == 0 else chunk
    steps = blocks * chunk // rows
    held = (steps, rows, rows) if steps > 8 else (1, 8, 128)
    return pl.pallas_call(
        functools.partial(teacher_kernel, 1.0 / math.sqrt(dim), rows),
        grid=(heads,),
        in_specs=[
            pl.BlockSpec((blocks, 1, chunk, dim), lambda h: (0, h, 0, 0)),
            pl.BlockSpec((blocks, 1, chunk, dim), lambda h: (0, heads, 0, 0)),
            pl.BlockSpec((blocks, 1, chunk, dim), lambda h: (0, heads + 1, 0, 0)),
        ],
        out_specs=[
            pl.BlockSpec((blocks, 1, chunk, dim), lambda h: (0, h, 0, 0)),
            pl.BlockSpec((1, 8, dim), lambda h: (h, 0, 0)),
        ],
        out_shape=[
            jax.ShapeDtypeStruct((blocks, heads, chunk, dim), F32),
            jax.ShapeDtypeStruct((heads, 8, dim), F32),
        ],
        scratch_shapes=[pltpu.VMEM(held, F32)],
        compiler_params=pltpu.CompilerParams(vmem_limit_bytes=VMEM_LIMIT),
        cost_estimate=pl.CostEstimate(
            flops=2 * heads * (blocks * chunk) ** 2 * dim,
            bytes_accessed=8 * heads * blocks * chunk * dim,
            transcendentals=heads * (blocks * chunk) ** 2 // 2,
        ),
    )(x, x, x)


def student_kernel(
    heads,
    x_ref,
    teacher_ref,
    mq_ref,
    mk_ref,
    grad_ref,
    top_ref,
    wq_ref,
    wk_ref,
    state_ref,
    local_ref,
    slope_ref,
    back_ref,
    sum_q_ref,
    sum_k_ref,
):
    blocks, _, chunk, dim = x_ref.shape
    features = mq_ref.shape[1]
    both = 2 * features

    for h in range(heads):
        rows = pl.ds(h * both, both)
        for source, target in ((mq_ref, wq_ref), (mk_ref, wk_ref)):
            high, low = halves(source[h])
            target[rows, :] = below(beside(high, low), beside(-high, -low))
    state_ref[...] = jnp.zeros_like(state_ref)
    sum_q_ref[...] = jnp.zeros_like(sum_q_ref)
    sum_k_ref[...] = jnp.zeros_like(sum_k_ref)
    mask = causal(chunk, chunk, 0)
    ones = jnp.ones((chunk, dim), BF16)

    def forward(r, carry):
        k, v = x_ref[r, heads], x_ref[r, heads + 1]
        wide = beside(v, ones)
        wide = below(wide, wide)
        twice = beside(v, v)
        phi_k, slope_k = feature_and_slope(dot_nt(wk_ref[...], beside(k, k)))
        slope_ref[r] = slope_k
        k_high, k_low = halves(phi_k)
        for h in range(heads):
            rows = pl.ds(h * both, both)
            at = slice(h * both, (h + 1) * both)
            q = x_ref[r, h]
            qq = beside(q, q)
            weight = wq_ref[rows, :]
            phi, _ = feature_and_slope(dot_nt(qq, weight))
            phi_t, slope_t = feature_and_slope(dot_nt(weight, qq))
            q_high, q_low = halves(phi)
            t_high, t_low = halves(phi_t)
            q_pair = beside(q_high, q_low)
            kh, kl = k_high[at], k_low[at]
            pair = beside(kh, kl)
            inner = dot(q_pair, below(pair, pair))
            inner = jnp.where(mask, inner[:, :chunk] + inner[:, chunk:], 0.0)
            state = state_ref[rows, :]
            s_high, s_low = halves(state)
            out = (
                dot(beside(*halves(inner)), wide)
                + dot(q_pair, below(s_high, s_high))
                + dot(q_high, s_low)
            )
            inverse = 1.0 / out[:, dim:]
            student = out[:, :dim] * inverse
            error = student - teacher_ref[r, h]
            numer = error * inverse
            denom = -jnp.sum(error * student, axis=1, keepdims=True) * inverse
            n_high, n_low = halves(numer)
            d_high, d_low = halves(denom)
            inner_grad = jnp.where(
                mask, dot_nt(beside(n_high, n_low), twice) + denom[:, :chunk], 0.0
            )
            i_high, i_low = halves(inner_grad)
            back_ref[r, rows, :] = dot(
                beside(t_high, t_high), below(beside(n_high, d_high), beside(n_low, d_low))
            )
            grad_t = (
                dot_nt(pair, beside(i_high, i_high))
                + dot_nt(beside(kh, s_high[:, :dim]), beside(i_low, n_high))
                + dot_nt(
                    beside(s_high[:, :dim], s_high[:, dim:] * (1.0 / dim)), beside(n_low, d_high)
                )
                + dot_nt(
                    beside(s_low[:, :dim], s_low[:, dim:] * (1.0 / dim)), beside(n_high, d_high)
                )
            )
            sum_q_ref[rows, :] += dot(beside(*halves(grad_t * slope_t)), below(q, q))
            local_ref[r, rows, :] = dot(beside(t_high, t_low), below(i_high, i_high)) + dot(
                t_high, i_low
            )
        state_ref[...] += dot(beside(k_high, k_low), wide)
        return carry

    lax.fori_loop(0, blocks, forward, 0)
    state_ref[...] = jnp.zeros_like(state_ref)

    def backward(i, carry):
        r = blocks - 1 - i
        k, v = x_ref[r, heads], x_ref[r, heads + 1]
        later = state_ref[...]
        high, low = halves(later[:, :dim])
        grad_t = local_ref[r] + dot_nt(beside(high, low), beside(v, v)) + later[:, dim:]
        sum_k_ref[...] += dot(beside(*halves(grad_t * slope_ref[r])), below(k, k))
        state_ref[...] = later + back_ref[r]
        return carry

    lax.fori_loop(0, blocks, backward, 0)
    for h in range(heads):
        base = h * both
        for i, total in enumerate((sum_q_ref, sum_k_ref)):
            part = total[pl.ds(base, features), :] - total[pl.ds(base + features, features), :]
            grad_ref[pl.ds(base + i * features, features), :] = part
        top = jnp.max(jnp.abs(grad_ref[pl.ds(base, both), :]), axis=0, keepdims=True)
        top_ref[pl.ds(h, 1), :] = top


def student_call(x, teacher, map_query, map_key):
    blocks, _, chunk, dim = x.shape
    heads, features, _ = map_query.shape
    rows = heads * 2 * features
    whole = pl.BlockSpec(memory_space=pltpu.VMEM)
    return pl.pallas_call(
        functools.partial(student_kernel, heads),
        in_specs=[whole] * 4,
        out_specs=[whole] * 2,
        out_shape=[
            jax.ShapeDtypeStruct((rows, dim), F32),
            jax.ShapeDtypeStruct((heads, dim), F32),
        ],
        scratch_shapes=[
            pltpu.VMEM((rows, 2 * dim), BF16),
            pltpu.VMEM((rows, 2 * dim), BF16),
            pltpu.VMEM((rows, 2 * dim), F32),
            pltpu.VMEM((blocks, rows, chunk), F32),
            pltpu.VMEM((blocks, rows, chunk), F32),
            pltpu.VMEM((blocks, rows, 2 * dim), F32),
            pltpu.VMEM((rows, dim), F32),
            pltpu.VMEM((rows, dim), F32),
        ],
        compiler_params=pltpu.CompilerParams(vmem_limit_bytes=VMEM_LIMIT),
        cost_estimate=pl.CostEstimate(
            flops=40 * rows * blocks * chunk * dim,
            bytes_accessed=12 * heads * blocks * chunk * dim,
            transcendentals=3 * rows * blocks * chunk,
        ),
    )(x, teacher, map_query, map_key)


def on_device(queries, key_states, value_vector_states, map_query, map_key):
    places = lax.axis_size("ctx")
    planes = lax.axis_size("head")
    place = lax.axis_index("ctx")
    tokens, query_heads, dim = queries.shape
    key_heads = key_states.shape[1]
    features = map_query.shape[2]
    group = query_heads // key_heads
    heads = min(d for d in range(1, group + 1) if group % d == 0 and d * places >= query_heads)
    padding = heads * places - query_heads
    key_of = np.minimum(np.arange(places) * heads, query_heads - 1) // group

    def padded(a, axis):
        width = [(0, padding if i == axis else 0) for i in range(a.ndim)]
        return jnp.pad(a, width) if padding else a

    by_head = padded(queries, 1).transpose(1, 0, 2).reshape(places, heads, tokens, dim)
    keys = jnp.stack([key_states[:, g] for g in key_of])[:, None]
    values = jnp.stack([value_vector_states[:, g] for g in key_of])[:, None]
    parts = jnp.concatenate([by_head, keys, values], axis=1)
    x = lax.all_to_all(parts, "ctx", 0, 0)

    def own(weights):
        weights = padded(weights, 0).transpose(0, 2, 1)
        return lax.dynamic_slice_in_dim(weights, place * heads, heads, 0)

    teacher, energy = teacher_call(x, heads)
    live = place * heads + jnp.arange(heads) < query_heads
    energy = jnp.sum(jnp.where(live[:, None, None], energy, 0.0)).reshape(1, 1)
    shifted = [
        lax.ppermute(energy, "head", [(i, (i + k) % planes) for i in range(planes)])
        for k in range(1, planes)
    ]
    energy = sum(shifted, energy)[0, 0]
    grads, top = student_call(x, teacher, own(map_query), own(map_key))

    def exponent(v):
        return jnp.clip(jnp.round(jnp.log2(jnp.maximum(v, 1e-30))), -100.0, 126.0)

    power = exponent(jnp.max(top, axis=1))
    energy_power = exponent(energy)
    near_one = energy * jnp.exp2(-energy_power)
    first = near_one.astype(F16)
    second = ((near_one - first.astype(F32)) * 1024.0).astype(F16)
    tail = jnp.concatenate([power.astype(F16), jnp.stack([energy_power.astype(F16), first, second])])
    tail = jnp.pad(jnp.broadcast_to(tail[:, None], (heads + 3, dim)), ((0, TAIL - heads - 3), (0, 0)))
    rows = heads * 2 * features
    scaled = (grads.reshape(heads, -1, dim) * jnp.exp2(-power)[:, None, None]).astype(F16)
    sent = jnp.concatenate([scaled.reshape(rows, dim), tail])
    gathered = lax.all_gather(sent, "ctx").astype(F32)
    tails = gathered[:, rows:, 0]
    power = tails[:, :heads]
    energies = (tails[:, heads + 1] + tails[:, heads + 2] * (1.0 / 1024.0)) * jnp.exp2(tails[:, heads])
    factor = jnp.exp2(power) * (2.0 * query_heads * planes / jnp.sum(energies))
    result = gathered[:, :rows].reshape(places, heads, 2, features, dim)
    result = result * factor[:, :, None, None, None]
    result = result.reshape(places * heads, 2, features, dim)[:query_heads].transpose(1, 0, 3, 2)
    return (result[0], result[1])


def solution(mesh):
    placed = (
        P("ctx", "head", None),
        P("ctx", "head", None),
        P("ctx", "head", None),
        P("head", None, None),
        P("head", None, None),
    )
    return jax.shard_map(
        on_device,
        mesh=mesh,
        in_specs=placed,
        out_specs=(P("head", None, None), P("head", None, None)),
        check_vma=False,
    )
```

profile of v0, /device:TPU:0, one launch (start us, length us, event | category | flops | bytes accessed | tf_op | source)
XLA Modules:
  0.0 104.0 jit_solution(4093339969922868827)
XLA Ops:
  0.6 0.0 copy-start.1
  0.6 1.1 %fusion.1 = (bf16[128,1,128]{2,1,0:T(2,128)(2,1)S(1)}, bf16[128,1,128]{2,1,0:T(2,128)(2,1)S(1)}) fusion(bf16[128,2,128]{2,1,0:T(2,128)(2,1)} %param.6), kind=kLoop, calls=%fused_computation.41 | loop fusion | bytes 131072 | tf_op jit(solution)/shard_map/slice | solution.py:305
  1.9 1.0 fusion.2
  3.0 0.0 copy-done.1
  3.0 0.4 copy.18
  3.4 1.3 %pad_maximum_fusion = bf16[8,6,128,128]{3,2,1,0:T(8,128)(2,1)} fusion(bf16[8,1,128,128]{3,2,1,0:T(8,128)(2,1)S(1)} %bitcast.41, bf16[8,1,128,128]{3,2,1,0:T(8,128)(2,1)S(1)} %bitcast.40, bf16[8,4,128,128]{3,2,1,0:T(8,128)(2,1)S(1)} %bitcast.38), kind=kLoop, calls=%fused_computation.1 | loop fusion | flops 1572864 | bytes 3145728 | tf_op jit(solution)/shard_map/concatenate | solution.py:307
  4.8 5.2 %all-to-all-start = ((bf16[8,6,128,128]{3,2,1,0:T(8,128)(2,1)}), bf16[8,6,128,128]{3,2,1,0:T(8,128)(2,1)S(1)}, u32[]{:S(2)}, u32[]{:S(2)}) async-start(bf16[8,6,128,128]{3,2,1,0:T(8,128)(2,1)} %pad_maximum_fusion), calls=%async_computation | async-start | bytes 3145728 | tf_op jit(solution)/shard_map/all_to_all | solution.py:308
  10.0 1.7 %dynamic-slice_bitcast_fusion = (f32[4,64,128]{2,1,0:T(8,128)}, f32[4,64,128]{2,1,0:T(8,128)}) fusion(f32[32,128,64]{1,2,0:T(8,128)} %param.9, s32[]{:T(128)S(6)} %select_n.8, f32[32,128,64]{1,2,0:T(8,128)} %param.8), kind=kLoop, calls=%fused_computation.6 | loop fusion | bytes 524292 | tf_op jit(solution)/shard_map/dynamic_slice | solution.py:312
  11.7 19.3 %all-to-all-done.q_ref.k_ref.v_ref.x_ref = bf16[8,6,128,128]{3,2,1,0:T(8,128)(2,1)S(1)} async-done(((bf16[8,6,128,128]{3,2,1,0:T(8,128)(2,1)}), bf16[8,6,128,128]{3,2,1,0:T(8,128)(2,1)S(1)}, u32[]{:S(2)}, u32[]{:S(2)}) %all-to-all-start) | async-done | bytes 1572896 | tf_op jit(solution)/shard_map/all_to_all | solution.py:308
  31.0 0.0 copy-start
  31.0 1.1 %copy-done = bf16[8,6,128,128]{3,2,1,0:T(8,128)(2,1)} copy-done((bf16[8,6,128,128]{3,2,1,0:T(8,128)(2,1)}, bf16[8,6,128,128]{3,2,1,0:T(8,128)(2,1)S(1)}, u32[]{:S(2)}) %copy-start) | copy-done | bytes 1572888
  32.1 8.9 %shard_map.68 = (f32[8,4,128,128]{3,2,1,0:T(8,128)}, f32[4,8,128]{2,1,0:T(8,128)}) custom-call(bf16[8,6,128,128]{3,2,1,0:T(8,128)(2,1)} %copy-done, bf16[8,6,128,128]{3,2,1,0:T(8,128)(2,1)} %copy-done, bf16[8,6,128,128]{3,2,1,0:T(8,128)(2,1)} %copy-done), custom_call_target="tpu_custom_call" | custom-call | flops 1073741824 | bytes 4194304 | tf_op jit(solution)/shard_map/pallas_call | solution.py:114
  41.0 1.4 %select_reduce_fusion = f32[]{:T(128)} fusion(f32[4,8,128]{2,1,0:T(8,128)} %get-tuple-element.9, pred[4]{0:T(512)(128)(4,1)S(1)} %add_compare_fusion), kind=kLoop, calls=%fused_computation.29 | loop fusion | flops 8191 | bytes 16392 | tf_op jit(solution)/shard_map/reduce_sum | solution.py:316
  42.4 1.6 %collective-permute-start = (f32[1,1]{1,0:T(1,128)}, f32[1,1]{1,0:T(1,128)}, u32[]{:S(2)}, u32[]{:S(2)}) collective-permute-start(f32[1,1]{1,0:T(1,128)} %bitcast.11), channel_id=1, source_target_pairs={{0,1},{1,2},{2,3},{3,0},{4,5},{5,6},{6,7},{7,4},{8,9},{9,10},{10,1... | collective-permute-start | bytes 20 | tf_op jit(solution)/shard_map/ppermute | solution.py:318
  44.0 2.6 %collective-permute-start.1 = (f32[1,1]{1,0:T(1,128)}, f32[1,1]{1,0:T(1,128)}, u32[]{:S(2)}, u32[]{:S(2)}) collective-permute-start(f32[1,1]{1,0:T(1,128)} %bitcast.11), channel_id=1, source_target_pairs={{0,2},{1,3},{2,0},{3,1},{4,6},{5,7},{6,4},{7,5},{8,10},{9,11},{10,... | collective-permute-start | bytes 20 | tf_op jit(solution)/shard_map/ppermute | solution.py:318
  46.6 1.4 %collective-permute-start.2 = (f32[1,1]{1,0:T(1,128)}, f32[1,1]{1,0:T(1,128)}, u32[]{:S(2)}, u32[]{:S(2)}) collective-permute-start(f32[1,1]{1,0:T(1,128)} %bitcast.11), channel_id=1, source_target_pairs={{0,3},{1,0},{2,1},{3,2},{4,7},{5,4},{6,5},{7,6},{8,11},{9,8},{10,9... | collective-permute-start | bytes 20 | tf_op jit(solution)/shard_map/ppermute | solution.py:318
  48.0 37.5 %shard_map.69 = (f32[512,128]{1,0:T(8,128)}, f32[4,128]{1,0:T(4,128)}) custom-call(bf16[8,6,128,128]{3,2,1,0:T(8,128)(2,1)} %copy-done, f32[8,4,128,128]{3,2,1,0:T(8,128)} %get-tuple-element.6.teacher_ref, f32[4,64,128]{2,1,0:T(8,128)} %get-tuple-element.27.mq_ref, f32[4,64,128]{2,1,0:T(8,128)} %get-tuple-element.26.mk_ref), custom_call_target="tpu_custom_call" | custom-call | flops 2684354560 | bytes 6291456 | tf_op jit(solution)/shard_map/pallas_call | solution.py:261
  85.5 0.8 reduce_max.9
  86.3 0.1 broadcast_bitcast_fusion
  86.4 1.1 %multiply_convert_fusion = f16[512,128]{1,0:T(8,128)(2,1)S(1)} fusion(f32[512,128]{1,0:T(8,128)} %get-tuple-element.7, f32[512]{0:T(512)S(1)} %broadcast_bitcast_fusion), kind=kLoop, calls=%fused_computation.4 | loop fusion | flops 131072 | bytes 395264 | tf_op jit(solution)/shard_map/convert_element_type | solution.py:335
  87.5 0.0 collective-permute-done
  88.7 0.0 collective-permute-done.1
  89.3 0.0 collective-permute-done.2
  90.1 0.1 select_maximum_fusion
  90.2 0.1 pad_maximum_fusion.1
  90.3 10.2 %all-gather.2 = f16[4224,128]{1,0:T(8,128)(2,1)S(1)} all-gather(f16[528,128]{1,0:T(8,128)(2,1)S(1)} %pad_maximum_fusion.1), channel_id=2, replica_groups=mesh['ctx'=8,'head'=4] {'ctx'}, dimensions={0}, use_global_device_ids=true | all-gather | bytes 1216512 | tf_op jit(solution)/shard_map/all_gather | solution.py:337
  100.5 0.1 convert
  100.6 0.1 slice_reduce_fusion
  100.7 0.1 slice.60
  100.9 0.7 multiply_reduce_fusion
  102.2 0.1 mul.60
  102.3 0.2 multiply_bitcast_fusion
  102.5 1.5 %slice_bitcast_fusion = (f32[32,128,64]{1,2,0:T(8,128)}, f32[32,128,64]{1,2,0:T(8,128)}) fusion(f32[2,32,128,64]{2,3,0,1:T(8,128)S(1)} %multiply_bitcast_fusion), kind=kLoop, calls=%fused_computation.2 | loop fusion | bytes 4194304 | tf_op jit(solution)/shard_map/squeeze | solution.py:345
  (20 shorter events, 0.2 us)
Async XLA Ops:
  0.6 2.4 %copy-start.1 = (bf16[128,32,128]{2,1,0:T(8,128)(2,1)S(1)}, bf16[128,32,128]{2,1,0:T(8,128)(2,1)}, u32[]{:S(2)}) copy-start(bf16[128,32,128]{2,1,0:T(8,128)(2,1)} %param.5) | copy-start | bytes 3145732
  4.8 26.2 %all-to-all-start = ((bf16[8,6,128,128]{3,2,1,0:T(8,128)(2,1)}), bf16[8,6,128,128]{3,2,1,0:T(8,128)(2,1)S(1)}, u32[]{:S(2)}, u32[]{:S(2)}) async-start(bf16[8,6,128,128]{3,2,1,0:T(8,128)(2,1)} %pad_maximum_fusion), calls=%async_computation | async-start | bytes 3145728 | tf_op jit(solution)/shard_map/all_to_all | solution.py:308
  31.0 1.2 %copy-start = (bf16[8,6,128,128]{3,2,1,0:T(8,128)(2,1)}, bf16[8,6,128,128]{3,2,1,0:T(8,128)(2,1)S(1)}, u32[]{:S(2)}) copy-start(bf16[8,6,128,128]{3,2,1,0:T(8,128)(2,1)S(1)} %all-to-all-done.q_ref.k_ref.v_ref.x_ref) | copy-start | bytes 4718596
  42.4 45.0 %collective-permute-start = (f32[1,1]{1,0:T(1,128)}, f32[1,1]{1,0:T(1,128)}, u32[]{:S(2)}, u32[]{:S(2)}) collective-permute-start(f32[1,1]{1,0:T(1,128)} %bitcast.11), channel_id=1, source_target_pairs={{0,1},{1,2},{2,3},{3,0},{4,5},{5,6},{6,7},{7,4},{8,9},{9,10},{10,1... | collective-permute-start | bytes 20 | tf_op jit(solution)/shard_map/ppermute | solution.py:318
  44.0 44.7 %collective-permute-start.1 = (f32[1,1]{1,0:T(1,128)}, f32[1,1]{1,0:T(1,128)}, u32[]{:S(2)}, u32[]{:S(2)}) collective-permute-start(f32[1,1]{1,0:T(1,128)} %bitcast.11), channel_id=1, source_target_pairs={{0,2},{1,3},{2,0},{3,1},{4,6},{5,7},{6,4},{7,5},{8,10},{9,11},{10,... | collective-permute-start | bytes 20 | tf_op jit(solution)/shard_map/ppermute | solution.py:318
  46.6 42.8 %collective-permute-start.2 = (f32[1,1]{1,0:T(1,128)}, f32[1,1]{1,0:T(1,128)}, u32[]{:S(2)}, u32[]{:S(2)}) collective-permute-start(f32[1,1]{1,0:T(1,128)} %bitcast.11), channel_id=1, source_target_pairs={{0,3},{1,0},{2,1},{3,2},{4,7},{5,4},{6,5},{7,6},{8,11},{9,8},{10,9... | collective-permute-start | bytes 20 | tf_op jit(solution)/shard_map/ppermute | solution.py:318
where the time goes:
time: 104 us
  Pallas kernels  46.4 us (45%)
  waiting for transfers between devices  19.3 us (19%)
  starting transfers between devices  10.7 us (10%)
  blocking collectives  10.2 us (10%)
  local copies, waits for them, and re-layouts  7.39 us (7%)
  other arithmetic  5.92 us (6%)
  between operations  4.11 us (4%)
    pallas_call x1, Pallas kernels, student_call(): pl.pallas_call(functools.partial(student_kernel, heads), in_specs=[whole]...  37.5 us
    all_to_all x1, waiting for transfers between devices, on_device(): x = lax.all_to_all(parts, 'ctx', 0, 0)  19.3 us
    all_gather x1, blocking collectives, on_device(): gathered = lax.all_gather(sent, 'ctx').astype(F32)  10.2 us
    pallas_call x1, Pallas kernels, teacher_call(): pl.pallas_call(functools.partial(teacher_kernel, 1.0 / math.sqrt(dim), ro...  8.88 us
    ppermute x3, starting transfers between devices, on_device(): lax.ppermute(energy, 'head', [(i, (i + k) % planes) for i in range(planes)])  5.52 us
    all_to_all x1, starting transfers between devices, on_device(): x = lax.all_to_all(parts, 'ctx', 0, 0)  5.17 us
  transfers between devices with their start and end apart: 4, of which 1 were waited for; matrix products, arithmetic and copies ran while one was open for 4% of the time, Pallas kernels for 36%

commit v1 on v0

--- a/solution.py
+++ b/solution.py
@@ -37,10 +37,8 @@
     return jnp.concatenate(parts, axis=0)
 
 
-def feature_and_slope(logit):
-    grown = jnp.exp(jnp.minimum(logit, 0.0))
-    positive = logit > 0
-    return jnp.where(positive, logit + 1.0, grown), jnp.where(positive, 1.0, grown)
+def feature(logit):
+    return jnp.where(logit > 0, logit + 1.0, jnp.exp(jnp.minimum(logit, 0.0)))
 
 
 def causal(rows, columns, shift):
@@ -147,9 +145,13 @@
     top_ref,
     wq_ref,
     wk_ref,
+    q_ref,
+    t_ref,
+    k_ref,
+    before_ref,
+    norm_ref,
     state_ref,
     local_ref,
-    slope_ref,
     back_ref,
     sum_q_ref,
     sum_k_ref,
@@ -157,80 +159,108 @@
     blocks, _, chunk, dim = x_ref.shape
     features = mq_ref.shape[1]
     both = 2 * features
+    at = [slice(h * both, (h + 1) * both) for h in range(heads)]
+    per = 2 if blocks % 2 == 0 else 1
 
     for h in range(heads):
-        rows = pl.ds(h * both, both)
         for source, target in ((mq_ref, wq_ref), (mk_ref, wk_ref)):
             high, low = halves(source[h])
-            target[rows, :] = below(beside(high, low), beside(-high, -low))
+            target[at[h], :] = below(beside(high, low), beside(-high, -low))
     state_ref[...] = jnp.zeros_like(state_ref)
     sum_q_ref[...] = jnp.zeros_like(sum_q_ref)
     sum_k_ref[...] = jnp.zeros_like(sum_k_ref)
     mask = causal(chunk, chunk, 0)
     ones = jnp.ones((chunk, dim), BF16)
 
-    def forward(r, carry):
+    def query_features(i, carry):
+        for h in range(heads):
+            for j in range(per):
+                r = i * per + j
+                q = x_ref[r, h]
+                high, low = halves(feature(dot_nt(beside(q, q), wq_ref[at[h], :])))
+                q_ref[r, at[h], :] = beside(high, low)
+                t_ref[r, at[h], :] = beside(high.T, low.T)
+        return carry
+
+    def key_features(r, carry):
         k, v = x_ref[r, heads], x_ref[r, heads + 1]
         wide = beside(v, ones)
-        wide = below(wide, wide)
-        twice = beside(v, v)
-        phi_k, slope_k = feature_and_slope(dot_nt(wk_ref[...], beside(k, k)))
-        slope_ref[r] = slope_k
-        k_high, k_low = halves(phi_k)
-        for h in range(heads):
-            rows = pl.ds(h * both, both)
-            at = slice(h * both, (h + 1) * both)
+        pair = beside(*halves(feature(dot_nt(wk_ref[...], beside(k, k)))))
+        k_ref[r] = pair
+        state = state_ref[...]
+        before_ref[r] = beside(*halves(state))
+        norm_ref[r] = state[:, dim:]
+        state_ref[...] = state + dot(pair, below(wide, wide))
+        return carry
+
+    lax.fori_loop(0, blocks // per, query_features, 0)
+    lax.fori_loop(0, blocks, key_features, 0)
+
+    def forward(i, carry):
+        chunks = [i * per + j for j in range(per)]
+        pairs = [(r, h) for r in chunks for h in range(heads)]
+
+        def stacked(parts):
+            return [below(*parts[j * heads : (j + 1) * heads]) for j in range(per)]
+
+        def split(parts):
+            return [part[s] for part in parts for s in at]
+
+        def weigh(r, h):
+            k = k_ref[r, at[h], :]
+            both_ways = dot(q_ref[r, at[h], :], below(k, k))
+            return jnp.where(mask, both_ways[:, :chunk] + both_ways[:, chunk:], 0.0)
+
+        def from_before(r, h):
+            q = q_ref[r, at[h], :both]
+            s = before_ref[r, at[h], :]
+            return dot(beside(q, q), below(s[:, : 2 * dim], s[:, 2 * dim :]))
+
+        inner = stacked([weigh(r, h) for r, h in pairs])
+        values = [x_ref[r, heads + 1] for r in chunks]
+        wide = [beside(v, ones) for v in values]
+        state_part = stacked([from_before(r, h) for r, h in pairs])
+        out = [
+            dot(beside(*halves(a)), below(w, w)) + b for a, w, b in zip(inner, wide, state_part)
+        ]
+        inverse = [1.0 / o[:, dim:] for o in out]
+        student = [o[:, :dim] * n for o, n in zip(out, inverse)]
+        error = [s - below(*[teacher_ref[r, h] for h in range(heads)]) for s, r in zip(student, chunks)]
+        numer = [e * n for e, n in zip(error, inverse)]
+        denom = [
+            -jnp.sum(e * s, axis=1, keepdims=True) * n for e, s, n in zip(error, student, inverse)
+        ]
+        numer_pair = [beside(*halves(n)) for n in numer]
+        denom_pair = [beside(*halves(d)) for d in denom]
+        spread = [dot_nt(n, beside(v, v)) for n, v in zip(numer_pair, values)]
+        mask_all = below(*[mask] * heads)
+        inner_grad = [
+            jnp.where(mask_all, s + d[:, :chunk], 0.0) for s, d in zip(spread, denom)
+        ]
+        grad_pair = [beside(*halves(g)) for g in inner_grad]
+        numer_pair, denom_pair = split(numer_pair), split(denom_pair)
+        grad_pair, denom = split(grad_pair), split(denom)
+        for (r, h), n, d, g, d_full in zip(pairs, numer_pair, denom_pair, grad_pair, denom):
+            t, k, s = t_ref[r, at[h], :], k_ref[r, at[h], :], before_ref[r, at[h], :]
+            t_high, k_high = t[:, :chunk], k[:, :chunk]
+            g_high, g_low = g[:, :chunk], g[:, chunk:]
+            n_high, n_low = n[:, :dim], n[:, dim:]
+            s_high, s_low = s[:, :dim], s[:, 2 * dim : 3 * dim]
+            back_ref[r, at[h], :] = dot(
+                beside(t_high, t_high), below(beside(n_high, d[:, :dim]), beside(n_low, d[:, dim:]))
+            )
+            local_ref[r, at[h], :] = dot(beside(t, t_high), below(g_high, g_high, g_low))
+            grad_t = dot_nt(
+                beside(k, k_high, s_high, s_high, s_low),
+                beside(g_high, g_high, g_low, n_high, n_low, n_high),
+            )
+            grad_t = grad_t + norm_ref[r, at[h], :] * d_full.T
+            slope = jnp.minimum(t_high.astype(F32) + t[:, chunk:].astype(F32), 1.0)
             q = x_ref[r, h]
-            qq = beside(q, q)
-            weight = wq_ref[rows, :]
-            phi, _ = feature_and_slope(dot_nt(qq, weight))
-            phi_t, slope_t = feature_and_slope(dot_nt(weight, qq))
-            q_high, q_low = halves(phi)
-            t_high, t_low = halves(phi_t)
-            q_pair = beside(q_high, q_low)
-            kh, kl = k_high[at], k_low[at]
-            pair = beside(kh, kl)
-            inner = dot(q_pair, below(pair, pair))
-            inner = jnp.where(mask, inner[:, :chunk] + inner[:, chunk:], 0.0)
-            state = state_ref[rows, :]
-            s_high, s_low = halves(state)
-            out = (
-                dot(beside(*halves(inner)), wide)
-                + dot(q_pair, below(s_high, s_high))
-                + dot(q_high, s_low)
-            )
-            inverse = 1.0 / out[:, dim:]
-            student = out[:, :dim] * inverse
-            error = student - teacher_ref[r, h]
-            numer = error * inverse
-            denom = -jnp.sum(error * student, axis=1, keepdims=True) * inverse
-            n_high, n_low = halves(numer)
-            d_high, d_low = halves(denom)
-            inner_grad = jnp.where(
-                mask, dot_nt(beside(n_high, n_low), twice) + denom[:, :chunk], 0.0
-            )
-            i_high, i_low = halves(inner_grad)
-            back_ref[r, rows, :] = dot(
-                beside(t_high, t_high), below(beside(n_high, d_high), beside(n_low, d_low))
-            )
-            grad_t = (
-                dot_nt(pair, beside(i_high, i_high))
-                + dot_nt(beside(kh, s_high[:, :dim]), beside(i_low, n_high))
-                + dot_nt(
-                    beside(s_high[:, :dim], s_high[:, dim:] * (1.0 / dim)), beside(n_low, d_high)
-                )
-                + dot_nt(
-                    beside(s_low[:, :dim], s_low[:, dim:] * (1.0 / dim)), beside(n_high, d_high)
-                )
-            )
-            sum_q_ref[rows, :] += dot(beside(*halves(grad_t * slope_t)), below(q, q))
-            local_ref[r, rows, :] = dot(beside(t_high, t_low), below(i_high, i_high)) + dot(
-                t_high, i_low
-            )
-        state_ref[...] += dot(beside(k_high, k_low), wide)
+            sum_q_ref[at[h], :] += dot(beside(*halves(grad_t * slope)), below(q, q))
         return carry
 
-    lax.fori_loop(0, blocks, forward, 0)
+    lax.fori_loop(0, blocks // per, forward, 0)
     state_ref[...] = jnp.zeros_like(state_ref)
 
     def backward(i, carry):
@@ -239,7 +269,9 @@
         later = state_ref[...]
         high, low = halves(later[:, :dim])
         grad_t = local_ref[r] + dot_nt(beside(high, low), beside(v, v)) + later[:, dim:]
-        sum_k_ref[...] += dot(beside(*halves(grad_t * slope_ref[r])), below(k, k))
+        pair = k_ref[r]
+        slope = jnp.minimum(pair[:, :chunk].astype(F32) + pair[:, chunk:].astype(F32), 1.0)
+        sum_k_ref[...] += dot(beside(*halves(grad_t * slope)), below(k, k))
         state_ref[...] = later + back_ref[r]
         return carry
 
@@ -269,8 +301,12 @@
         scratch_shapes=[
             pltpu.VMEM((rows, 2 * dim), BF16),
             pltpu.VMEM((rows, 2 * dim), BF16),
+            pltpu.VMEM((blocks, rows, 2 * chunk), BF16),
+            pltpu.VMEM((blocks, rows, 2 * chunk), BF16),
+            pltpu.VMEM((blocks, rows, 2 * chunk), BF16),
+            pltpu.VMEM((blocks, rows, 4 * dim), BF16),
+            pltpu.VMEM((blocks, rows, dim), F32),
             pltpu.VMEM((rows, 2 * dim), F32),
-            pltpu.VMEM((blocks, rows, chunk), F32),
             pltpu.VMEM((blocks, rows, chunk), F32),
             pltpu.VMEM((blocks, rows, 2 * dim), F32),
             pltpu.VMEM((rows, dim), F32),

time: 104 us -> 90.5 us (0.87)
  Pallas kernels: 46.4 us -> 32.4 us
    pallas_call x1, Pallas kernels: 37.5 us -> 23.5 us  [student_call(): pl.pallas_call(functools.partial(student_kernel, heads), in_specs=[whole]...]
  transfers between devices with their start and end apart: 4 -> 4, of which waited for: 1 -> 1; matrix products, arithmetic and copies ran while one was open for 4% -> 4% of each run, Pallas kernels for 36% -> 26%
where the time goes in v1:
time: 90.5 us; the launch traced here: 90 us
  Pallas kernels  32.4 us (36%)
  waiting for transfers between devices  19.3 us (21%)
  starting transfers between devices  10.7 us (12%)
  blocking collectives  10.2 us (11%)
  local copies, waits for them, and re-layouts  7.39 us (8%)
  other arithmetic  5.92 us (7%)
  between operations  4.11 us (5%)
    pallas_call x1, Pallas kernels, student_call(): pl.pallas_call(functools.partial(student_kernel, heads), in_specs=[whole]...  23.5 us
    all_to_all x1, waiting for transfers between devices, on_device(): x = lax.all_to_all(parts, 'ctx', 0, 0)  19.3 us
    all_gather x1, blocking collectives, on_device(): gathered = lax.all_gather(sent, 'ctx').astype(F32)  10.2 us
    pallas_call x1, Pallas kernels, teacher_call(): pl.pallas_call(functools.partial(teacher_kernel, 1.0 / math.sqrt(dim), ro...  8.88 us
    ppermute x3, starting transfers between devices, on_device(): lax.ppermute(energy, 'head', [(i, (i + k) % planes) for i in range(planes)])  5.52 us
    all_to_all x1, starting transfers between devices, on_device(): x = lax.all_to_all(parts, 'ctx', 0, 0)  5.17 us
  transfers between devices with their start and end apart: 4, of which 1 were waited for; matrix products, arithmetic and copies ran while one was open for 4% of the time, Pallas kernels for 26%

profile of v1, /device:TPU:0, one launch (start us, length us, event | category | flops | bytes accessed | tf_op | source)
XLA Modules:
  0.0 90.0 jit_solution(17664728783890405214)
XLA Ops:
  0.6 0.0 copy-start.1
  0.6 1.1 %fusion.1 = (bf16[128,1,128]{2,1,0:T(2,128)(2,1)S(1)}, bf16[128,1,128]{2,1,0:T(2,128)(2,1)S(1)}) fusion(bf16[128,2,128]{2,1,0:T(2,128)(2,1)} %param.6), kind=kLoop, calls=%fused_computation.41 | loop fusion | bytes 131072 | tf_op jit(solution)/shard_map/slice | solution.py:341
  1.9 1.0 %fusion.2 = (bf16[128,1,128]{2,1,0:T(2,128)(2,1)S(1)}, bf16[128,1,128]{2,1,0:T(2,128)(2,1)S(1)}) fusion(bf16[128,2,128]{2,1,0:T(2,128)(2,1)} %param.7), kind=kLoop, calls=%fused_computation.42 | loop fusion | bytes 131072 | tf_op jit(solution)/shard_map/slice | solution.py:342
  3.0 0.0 copy-done.1
  3.0 0.4 copy.18
  3.4 1.3 %pad_maximum_fusion = bf16[8,6,128,128]{3,2,1,0:T(8,128)(2,1)} fusion(bf16[8,1,128,128]{3,2,1,0:T(8,128)(2,1)S(1)} %bitcast.41, bf16[8,1,128,128]{3,2,1,0:T(8,128)(2,1)S(1)} %bitcast.40, bf16[8,4,128,128]{3,2,1,0:T(8,128)(2,1)S(1)} %bitcast.38), kind=kLoop, calls=%fused_computation.1 | loop fusion | flops 1572864 | bytes 3145728 | tf_op jit(solution)/shard_map/concatenate | solution.py:343
  4.8 5.2 %all-to-all-start = ((bf16[8,6,128,128]{3,2,1,0:T(8,128)(2,1)}), bf16[8,6,128,128]{3,2,1,0:T(8,128)(2,1)S(1)}, u32[]{:S(2)}, u32[]{:S(2)}) async-start(bf16[8,6,128,128]{3,2,1,0:T(8,128)(2,1)} %pad_maximum_fusion), calls=%async_computation | async-start | bytes 3145728 | tf_op jit(solution)/shard_map/all_to_all | solution.py:344
  10.0 1.7 %dynamic-slice_bitcast_fusion = (f32[4,64,128]{2,1,0:T(8,128)}, f32[4,64,128]{2,1,0:T(8,128)}) fusion(f32[32,128,64]{1,2,0:T(8,128)} %param.9, s32[]{:T(128)S(6)} %select_n.8, f32[32,128,64]{1,2,0:T(8,128)} %param.8), kind=kLoop, calls=%fused_computation.6 | loop fusion | bytes 524292 | tf_op jit(solution)/shard_map/dynamic_slice | solution.py:348
  11.7 19.3 %all-to-all-done.q_ref.k_ref.v_ref.x_ref = bf16[8,6,128,128]{3,2,1,0:T(8,128)(2,1)S(1)} async-done(((bf16[8,6,128,128]{3,2,1,0:T(8,128)(2,1)}), bf16[8,6,128,128]{3,2,1,0:T(8,128)(2,1)S(1)}, u32[]{:S(2)}, u32[]{:S(2)}) %all-to-all-start) | async-done | bytes 1572896 | tf_op jit(solution)/shard_map/all_to_all | solution.py:344
  31.0 0.0 copy-start
  31.0 1.1 %copy-done = bf16[8,6,128,128]{3,2,1,0:T(8,128)(2,1)} copy-done((bf16[8,6,128,128]{3,2,1,0:T(8,128)(2,1)}, bf16[8,6,128,128]{3,2,1,0:T(8,128)(2,1)S(1)}, u32[]{:S(2)}) %copy-start) | copy-done | bytes 1572888
  32.1 8.9 %shard_map.68 = (f32[8,4,128,128]{3,2,1,0:T(8,128)}, f32[4,8,128]{2,1,0:T(8,128)}) custom-call(bf16[8,6,128,128]{3,2,1,0:T(8,128)(2,1)} %copy-done, bf16[8,6,128,128]{3,2,1,0:T(8,128)(2,1)} %copy-done, bf16[8,6,128,128]{3,2,1,0:T(8,128)(2,1)} %copy-done), custom_call_target="tpu_custom_call" | custom-call | flops 1073741824 | bytes 4194304 | tf_op jit(solution)/shard_map/pallas_call | solution.py:112
  41.0 1.4 %select_reduce_fusion = f32[]{:T(128)} fusion(f32[4,8,128]{2,1,0:T(8,128)} %get-tuple-element.9, pred[4]{0:T(512)(128)(4,1)S(1)} %add_compare_fusion), kind=kLoop, calls=%fused_computation.29 | loop fusion | flops 8191 | bytes 16392 | tf_op jit(solution)/shard_map/reduce_sum | solution.py:352
  42.4 1.6 %collective-permute-start = (f32[1,1]{1,0:T(1,128)}, f32[1,1]{1,0:T(1,128)}, u32[]{:S(2)}, u32[]{:S(2)}) collective-permute-start(f32[1,1]{1,0:T(1,128)} %bitcast.11), channel_id=1, source_target_pairs={{0,1},{1,2},{2,3},{3,0},{4,5},{5,6},{6,7},{7,4},{8,9},{9,10},{10,1... | collective-permute-start | bytes 20 | tf_op jit(solution)/shard_map/ppermute | solution.py:354
  44.0 2.6 %collective-permute-start.1 = (f32[1,1]{1,0:T(1,128)}, f32[1,1]{1,0:T(1,128)}, u32[]{:S(2)}, u32[]{:S(2)}) collective-permute-start(f32[1,1]{1,0:T(1,128)} %bitcast.11), channel_id=1, source_target_pairs={{0,2},{1,3},{2,0},{3,1},{4,6},{5,7},{6,4},{7,5},{8,10},{9,11},{10,... | collective-permute-start | bytes 20 | tf_op jit(solution)/shard_map/ppermute | solution.py:354
  46.6 1.4 %collective-permute-start.2 = (f32[1,1]{1,0:T(1,128)}, f32[1,1]{1,0:T(1,128)}, u32[]{:S(2)}, u32[]{:S(2)}) collective-permute-start(f32[1,1]{1,0:T(1,128)} %bitcast.11), channel_id=1, source_target_pairs={{0,3},{1,0},{2,1},{3,2},{4,7},{5,4},{6,5},{7,6},{8,11},{9,8},{10,9... | collective-permute-start | bytes 20 | tf_op jit(solution)/shard_map/ppermute | solution.py:354
  48.0 23.5 %shard_map.69 = (f32[512,128]{1,0:T(8,128)}, f32[4,128]{1,0:T(4,128)}) custom-call(bf16[8,6,128,128]{3,2,1,0:T(8,128)(2,1)} %copy-done, f32[8,4,128,128]{3,2,1,0:T(8,128)} %get-tuple-element.6.teacher_ref, f32[4,64,128]{2,1,0:T(8,128)} %get-tuple-element.27.mq_ref, f32[4,64,128]{2,1,0:T(8,128)} %get-tuple-element.26.mk_ref), custom_call_target="tpu_custom_call" | custom-call | flops 2684354560 | bytes 6291456 | tf_op jit(solution)/shard_map/pallas_call | solution.py:293
  71.5 0.8 reduce_max.9
  72.3 0.1 broadcast_bitcast_fusion
  72.4 1.1 %multiply_convert_fusion = f16[512,128]{1,0:T(8,128)(2,1)S(1)} fusion(f32[512,128]{1,0:T(8,128)} %get-tuple-element.7, f32[512]{0:T(512)S(1)} %broadcast_bitcast_fusion), kind=kLoop, calls=%fused_computation.4 | loop fusion | flops 131072 | bytes 395264 | tf_op jit(solution)/shard_map/convert_element_type | solution.py:371
  73.5 0.0 collective-permute-done
  74.7 0.0 collective-permute-done.1
  75.3 0.0 collective-permute-done.2
  76.1 0.1 select_maximum_fusion
  76.2 0.1 pad_maximum_fusion.1
  76.3 10.2 %all-gather.2 = f16[4224,128]{1,0:T(8,128)(2,1)S(1)} all-gather(f16[528,128]{1,0:T(8,128)(2,1)S(1)} %pad_maximum_fusion.1), channel_id=2, replica_groups=mesh['ctx'=8,'head'=4] {'ctx'}, dimensions={0}, use_global_device_ids=true | all-gather | bytes 1216512 | tf_op jit(solution)/shard_map/all_gather | solution.py:373
  86.5 0.1 convert
  86.6 0.1 slice_reduce_fusion
  86.7 0.1 slice.60
  86.9 0.7 multiply_reduce_fusion
  88.2 0.1 mul.60
  88.3 0.2 multiply_bitcast_fusion
  88.5 1.5 %slice_bitcast_fusion = (f32[32,128,64]{1,2,0:T(8,128)}, f32[32,128,64]{1,2,0:T(8,128)}) fusion(f32[2,32,128,64]{2,3,0,1:T(8,128)S(1)} %multiply_bitcast_fusion), kind=kLoop, calls=%fused_computation.2 | loop fusion | bytes 4194304 | tf_op jit(solution)/shard_map/squeeze | solution.py:381
  (20 shorter events, 0.2 us)
Async XLA Ops:
  0.6 2.4 %copy-start.1 = (bf16[128,32,128]{2,1,0:T(8,128)(2,1)S(1)}, bf16[128,32,128]{2,1,0:T(8,128)(2,1)}, u32[]{:S(2)}) copy-start(bf16[128,32,128]{2,1,0:T(8,128)(2,1)} %param.5) | copy-start | bytes 3145732
  4.8 26.2 %all-to-all-start = ((bf16[8,6,128,128]{3,2,1,0:T(8,128)(2,1)}), bf16[8,6,128,128]{3,2,1,0:T(8,128)(2,1)S(1)}, u32[]{:S(2)}, u32[]{:S(2)}) async-start(bf16[8,6,128,128]{3,2,1,0:T(8,128)(2,1)} %pad_maximum_fusion), calls=%async_computation | async-start | bytes 3145728 | tf_op jit(solution)/shard_map/all_to_all | solution.py:344
  31.0 1.2 %copy-start = (bf16[8,6,128,128]{3,2,1,0:T(8,128)(2,1)}, bf16[8,6,128,128]{3,2,1,0:T(8,128)(2,1)S(1)}, u32[]{:S(2)}) copy-start(bf16[8,6,128,128]{3,2,1,0:T(8,128)(2,1)S(1)} %all-to-all-done.q_ref.k_ref.v_ref.x_ref) | copy-start | bytes 4718596
  42.4 31.0 %collective-permute-start = (f32[1,1]{1,0:T(1,128)}, f32[1,1]{1,0:T(1,128)}, u32[]{:S(2)}, u32[]{:S(2)}) collective-permute-start(f32[1,1]{1,0:T(1,128)} %bitcast.11), channel_id=1, source_target_pairs={{0,1},{1,2},{2,3},{3,0},{4,5},{5,6},{6,7},{7,4},{8,9},{9,10},{10,1... | collective-permute-start | bytes 20 | tf_op jit(solution)/shard_map/ppermute | solution.py:354
  44.0 30.7 %collective-permute-start.1 = (f32[1,1]{1,0:T(1,128)}, f32[1,1]{1,0:T(1,128)}, u32[]{:S(2)}, u32[]{:S(2)}) collective-permute-start(f32[1,1]{1,0:T(1,128)} %bitcast.11), channel_id=1, source_target_pairs={{0,2},{1,3},{2,0},{3,1},{4,6},{5,7},{6,4},{7,5},{8,10},{9,11},{10,... | collective-permute-start | bytes 20 | tf_op jit(solution)/shard_map/ppermute | solution.py:354
  46.6 28.8 %collective-permute-start.2 = (f32[1,1]{1,0:T(1,128)}, f32[1,1]{1,0:T(1,128)}, u32[]{:S(2)}, u32[]{:S(2)}) collective-permute-start(f32[1,1]{1,0:T(1,128)} %bitcast.11), channel_id=1, source_target_pairs={{0,3},{1,0},{2,1},{3,2},{4,7},{5,4},{6,5},{7,6},{8,11},{9,8},{10,9... | collective-permute-start | bytes 20 | tf_op jit(solution)/shard_map/ppermute | solution.py:354

commit v2 on v1

v2 whole, which is shorter than its diff:
```python
import functools
import math

import jax
import jax.numpy as jnp
import numpy as np
from jax import lax
from jax.experimental import pallas as pl
from jax.experimental.pallas import tpu as pltpu
from jax.sharding import PartitionSpec as P

F32 = jnp.float32
BF16 = jnp.bfloat16
F16 = jnp.float16
VMEM_LIMIT = 44 * 1024 * 1024


def dot(a, b):
    return lax.dot_general(a, b, (((1,), (0,)), ((), ())), preferred_element_type=F32)


def dot_nt(a, b):
    return lax.dot_general(a, b, (((1,), (1,)), ((), ())), preferred_element_type=F32)


def halves(x):
    high = x.astype(BF16)
    return high, (x - high.astype(F32)).astype(BF16)


def beside(*parts):
    return jnp.concatenate(parts, axis=1)


def below(*parts):
    return jnp.concatenate(parts, axis=0)


def feature(logit):
    return jnp.where(logit > 0, logit + 1.0, jnp.exp(jnp.minimum(logit, 0.0)))


def power_of(top):
    return jnp.clip(jnp.round(jnp.log2(jnp.maximum(top, 1e-30))), -100.0, 126.0)


def causal(rows, columns, shift):
    row = lax.broadcasted_iota(jnp.int32, (rows, columns), 0)
    column = lax.broadcasted_iota(jnp.int32, (rows, columns), 1)
    return column <= row + shift


def teacher_kernel(heads, rows, scale, x_ref, out_ref, energy_ref, scores_ref):
    blocks, _, chunk, dim = x_ref.shape
    per_row = rows // chunk
    steps = blocks // per_row
    power = scale * math.log2(math.e)
    mask = causal(rows, rows, 0)

    def finish(h, r, weighted, total):
        teacher = weighted / total
        for i in range(per_row):
            out_ref[r * per_row + i, h] = teacher[i * chunk : (i + 1) * chunk]
        return jnp.sum((teacher * teacher).reshape(rows // 8, 8, dim), axis=0)

    def take(h, r, count=1):
        return x_ref[pl.ds(r * per_row, count * per_row), h].reshape(count * rows, dim)

    def one_head(h, energy):
        parts, tops, done = [], [], []
        for r in range(steps):
            scores = dot_nt(take(h, r), take(heads, 0, r + 1))
            last = jnp.where(mask, scores[:, r * rows :], -1e30)
            scores = beside(scores[:, : r * rows], last) if r else last
            parts.append(scores)
            tops.append(jnp.max(scores, axis=1, keepdims=True))
        for r in range(steps):
            weights = jnp.exp2((parts[r] - tops[r]) * power)
            total = jnp.sum(weights, axis=1, keepdims=True)
            done.append((dot(weights.astype(BF16), take(heads + 1, 0, r + 1)), total))
        for r in range(steps):
            energy = energy + finish(h, r, *done[r])
        return energy

    def one_long_head(h, energy):
        def one_row(r, energy):
            q = take(h, r)

            def look(j, top):
                scores = dot_nt(q, take(heads, j))
                scores = jnp.where((j < r) | mask, scores, -1e30)
                scores_ref[j] = scores
                return jnp.maximum(top, jnp.max(scores, axis=1, keepdims=True))

            top = lax.fori_loop(0, r + 1, look, jnp.full((rows, 1), -1e30, F32))

            def add(j, state):
                weighted, total = state
                weights = jnp.exp2((scores_ref[j] - top) * power)
                total = total + jnp.sum(weights, axis=1, keepdims=True)
                return weighted + dot(weights.astype(BF16), take(heads + 1, j)), total

            weighted, total = lax.fori_loop(
                0, r + 1, add, (jnp.zeros((rows, dim), F32), jnp.zeros((rows, 1), F32))
            )
            return energy + finish(h, r, weighted, total)

        return lax.fori_loop(0, steps, one_row, energy)

    body = one_head if steps <= 8 else one_long_head
    energy = lax.fori_loop(0, heads, body, jnp.zeros((8, dim), F32))
    energy = jnp.sum(jnp.sum(energy, axis=0, keepdims=True), axis=1, keepdims=True)
    energy_ref[...] = jnp.broadcast_to(energy, energy_ref.shape)


def teacher_call(x, heads):
    blocks, _, chunk, dim = x.shape
    rows = 2 * chunk if blocks % 2 == 0 else chunk
    steps = blocks * chunk // rows
    held = (steps, rows, rows) if steps > 8 else (1, 8, 128)
    whole = pl.BlockSpec(memory_space=pltpu.VMEM)
    return pl.pallas_call(
        functools.partial(teacher_kernel, heads, rows, 1.0 / math.sqrt(dim)),
        in_specs=[whole],
        out_specs=[whole, whole],
        out_shape=[
            pltpu.VMEM((blocks, heads, chunk, dim), F32),
            jax.ShapeDtypeStruct((8, dim), F32),
        ],
        scratch_shapes=[pltpu.VMEM(held, F32)],
        compiler_params=pltpu.CompilerParams(vmem_limit_bytes=VMEM_LIMIT),
        cost_estimate=pl.CostEstimate(
            flops=2 * heads * (blocks * chunk) ** 2 * dim,
            bytes_accessed=8 * heads * blocks * chunk * dim,
            transcendentals=heads * (blocks * chunk) ** 2 // 2,
        ),
    )(x)


def student_kernel(
    heads,
    x_ref,
    teacher_ref,
    mq_ref,
    mk_ref,
    grad_ref,
    wq_ref,
    wk_ref,
    q_ref,
    t_ref,
    k_ref,
    before_ref,
    norm_ref,
    state_ref,
    bias_ref,
    later_ref,
    sum_q_ref,
    sum_k_ref,
):
    blocks, _, chunk, dim = x_ref.shape
    features = mq_ref.shape[1]
    both = 2 * features
    spare = grad_ref.shape[0] - heads * both
    at = [slice(h * both, (h + 1) * both) for h in range(heads)]
    per = next(p for p in (4, 2, 1) if blocks % p == 0)

    for h in range(heads):
        for source, target in ((mq_ref, wq_ref), (mk_ref, wk_ref)):
            high, low = halves(source[h])
            target[at[h], :] = below(beside(high, low), beside(-high, -low))
    state_ref[...] = jnp.zeros_like(state_ref)
    sum_q_ref[...] = jnp.zeros_like(sum_q_ref)
    sum_k_ref[...] = jnp.zeros_like(sum_k_ref)
    mask = causal(chunk, chunk, 0)
    mask_all = below(*[mask] * heads)
    ones = jnp.ones((chunk, dim), BF16)

    def features_of(i, carry):
        chunks = [i * per + j for j in range(per)]
        keys = [x_ref[r, heads] for r in chunks]
        pairs = [
            beside(*halves(feature(dot_nt(wk_ref[...], beside(k, k))))) for k in keys
        ]
        wide = [beside(x_ref[r, heads + 1], ones) for r in chunks]
        added = [dot(p, below(w, w)) for p, w in zip(pairs, wide)]
        for r in chunks:
            for h in range(heads):
                q = x_ref[r, h]
                high, low = halves(feature(dot_nt(beside(q, q), wq_ref[at[h], :])))
                q_ref[r, at[h], :] = beside(high, low)
                t_ref[r, at[h], :] = beside(high.T, low.T)
        state = state_ref[...]
        for r, p, a in zip(chunks, pairs, added):
            k_ref[r] = p
            before_ref[r] = beside(*halves(state))
            norm_ref[r] = state[:, dim:]
            state = state + a
        state_ref[...] = state
        return carry

    lax.fori_loop(0, blocks // per, features_of, 0)
    bias_ref[...] = jnp.zeros_like(bias_ref)
    later_ref[...] = jnp.zeros_like(later_ref)

    def gradients(i, carry):
        chunks = [blocks - 1 - i * per - j for j in range(per)]
        pairs = [(r, h) for r in chunks for h in range(heads)]

        def stacked(parts):
            return [below(*parts[j * heads : (j + 1) * heads]) for j in range(per)]

        def split(parts):
            return [part[s] for part in parts for s in at]

        def weigh(r, h):
            k = k_ref[r, at[h], :]
            both_ways = dot(q_ref[r, at[h], :], below(k, k))
            return jnp.where(mask, both_ways[:, :chunk] + both_ways[:, chunk:], 0.0)

        def from_before(r, h):
            q = q_ref[r, at[h], :both]
            s = before_ref[r, at[h], :]
            return dot(beside(q, q), below(s[:, : 2 * dim], s[:, 2 * dim :]))

        inner = stacked([weigh(r, h) for r, h in pairs])
        values = [x_ref[r, heads + 1] for r in chunks]
        wide = [beside(v, ones) for v in values]
        state_part = stacked([from_before(r, h) for r, h in pairs])
        out = [
            dot(beside(*halves(a)), below(w, w)) + b for a, w, b in zip(inner, wide, state_part)
        ]
        inverse = [1.0 / o[:, dim:] for o in out]
        student = [o[:, :dim] * n for o, n in zip(out, inverse)]
        error = [s - below(*[teacher_ref[r, h] for h in range(heads)]) for s, r in zip(student, chunks)]
        numer = [e * n for e, n in zip(error, inverse)]
        denom = [
            -jnp.sum(e * s, axis=1, keepdims=True) * n for e, s, n in zip(error, student, inverse)
        ]
        numer_pair = [beside(*halves(n)) for n in numer]
        spread = [dot_nt(n, beside(v, v)) for n, v in zip(numer_pair, values)]
        inner_grad = [
            jnp.where(mask_all, s + d[:, :chunk], 0.0) for s, d in zip(spread, denom)
        ]
        grad_pair = [beside(*halves(g)) for g in inner_grad]
        numer_pair, grad_pair, denom = split(numer_pair), split(grad_pair), split(denom)
        query_side, from_later, later_bias = [], [], []
        for (r, h), n, g, d_full in zip(pairs, numer_pair, grad_pair, denom):
            t, k, s = t_ref[r, at[h], :], k_ref[r, at[h], :], before_ref[r, at[h], :]
            t_high, k_high = t[:, :chunk], k[:, :chunk]
            g_high, g_low = g[:, :chunk], g[:, chunk:]
            n_high, n_low = n[:, :dim], n[:, dim:]
            s_high, s_low = s[:, :dim], s[:, 2 * dim : 3 * dim]
            first = beside(n_high, g_high)
            from_later.append(dot(beside(t, t_high), below(first, first, beside(n_low, g_low))))
            grad_t = dot_nt(
                beside(k, k_high, s_high, s_high, s_low),
                beside(g_high, g_high, g_low, n_high, n_low, n_high),
            )
            d_row = d_full.T
            phi = t_high.astype(F32) + t[:, chunk:].astype(F32)
            later_bias.append(jnp.sum(phi * d_row, axis=1, keepdims=True))
            grad_t = grad_t + norm_ref[r, at[h], :] * d_row
            query_side.append(beside(*halves(grad_t * jnp.minimum(phi, 1.0))))
        for h in range(heads):
            left = beside(*[query_side[j * heads + h] for j in range(per)])
            right = below(*[x_ref[r, h] for r in chunks for _ in range(2)])
            sum_q_ref[at[h], :] += dot(left, right)
        later = later_ref[...]
        bias = bias_ref[...]
        key_side = []
        for j, (r, v) in enumerate(zip(chunks, values)):
            own = below(*from_later[j * heads : (j + 1) * heads])
            grad_t = own[:, dim:] + dot_nt(beside(*halves(later)), beside(v, v)) + bias
            pair = k_ref[r]
            slope = jnp.minimum(pair[:, :chunk].astype(F32) + pair[:, chunk:].astype(F32), 1.0)
            key_side.append(beside(*halves(grad_t * slope)))
            later = later + own[:, :dim]
            bias = bias + below(*later_bias[j * heads : (j + 1) * heads])
        sum_k_ref[...] += dot(
            beside(*key_side), below(*[x_ref[r, heads] for r in chunks for _ in range(2)])
        )
        later_ref[...] = later
        bias_ref[...] = jnp.broadcast_to(bias, bias_ref.shape)
        return carry

    lax.fori_loop(0, blocks // per, gradients, 0)
    grad_ref[pl.ds(heads * both, spare), :] = jnp.zeros((spare, dim), F32)
    for h in range(heads):
        base = h * both
        parts = [
            total[pl.ds(base, features), :] - total[pl.ds(base + features, features), :]
            for total in (sum_q_ref, sum_k_ref)
        ]
        grads = below(*parts)
        top = jnp.max(jnp.abs(grads), axis=0, keepdims=True)
        top = jnp.max(top, axis=1, keepdims=True)
        power = power_of(top)
        grad_ref[at[h], :] = grads * jnp.exp2(-power)
        grad_ref[pl.ds(heads * both + h, 1), :] = jnp.broadcast_to(power, (1, dim))


def student_call(x, teacher, map_query, map_key):
    blocks, _, chunk, dim = x.shape
    heads, features, _ = map_query.shape
    rows = heads * 2 * features
    whole = pl.BlockSpec(memory_space=pltpu.VMEM)
    return pl.pallas_call(
        functools.partial(student_kernel, heads),
        in_specs=[whole] * 4,
        out_specs=whole,
        out_shape=jax.ShapeDtypeStruct((rows + (heads + 7) // 8 * 8, dim), F32),
        scratch_shapes=[
            pltpu.VMEM((rows, 2 * dim), BF16),
            pltpu.VMEM((rows, 2 * dim), BF16),
            pltpu.VMEM((blocks, rows, 2 * chunk), BF16),
            pltpu.VMEM((blocks, rows, 2 * chunk), BF16),
            pltpu.VMEM((blocks, rows, 2 * chunk), BF16),
            pltpu.VMEM((blocks, rows, 4 * dim), BF16),
            pltpu.VMEM((blocks, rows, dim), F32),
            pltpu.VMEM((rows, 2 * dim), F32),
            pltpu.VMEM((rows, chunk), F32),
            pltpu.VMEM((rows, dim), F32),
            pltpu.VMEM((rows, dim), F32),
            pltpu.VMEM((rows, dim), F32),
        ],
        compiler_params=pltpu.CompilerParams(vmem_limit_bytes=VMEM_LIMIT),
        cost_estimate=pl.CostEstimate(
            flops=40 * rows * blocks * chunk * dim,
            bytes_accessed=12 * heads * blocks * chunk * dim,
            transcendentals=3 * rows * blocks * chunk,
        ),
    )(x, teacher, map_query, map_key)


def on_device(queries, key_states, value_vector_states, map_query, map_key):
    places = lax.axis_size("ctx")
    planes = lax.axis_size("head")
    place = lax.axis_index("ctx")
    tokens, query_heads, dim = queries.shape
    key_heads = key_states.shape[1]
    features = map_query.shape[2]
    group = query_heads // key_heads
    heads = min(d for d in range(1, group + 1) if group % d == 0 and d * places >= query_heads)
    padding = heads * places - query_heads
    key_of = np.minimum(np.arange(places) * heads, query_heads - 1) // group

    def padded(a, axis):
        width = [(0, padding if i == axis else 0) for i in range(a.ndim)]
        return jnp.pad(a, width) if padding else a

    by_head = padded(queries, 1).transpose(1, 0, 2).reshape(places, heads, tokens, dim)
    flat = [a.reshape(tokens, key_heads * dim) for a in (key_states, value_vector_states)]
    keyed = [jnp.stack([a[:, g * dim : (g + 1) * dim] for a in flat]) for g in key_of]
    parts = jnp.concatenate([by_head, jnp.stack(keyed)], axis=1)
    x = lax.all_to_all(parts, "ctx", 0, 0)
    x = pltpu.with_memory_space_constraint(x, pltpu.VMEM)

    def own(weights):
        weights = padded(weights, 0).transpose(0, 2, 1)
        return lax.dynamic_slice_in_dim(weights, place * heads, heads, 0)

    teacher, energy = teacher_call(x, heads)
    energy = jnp.where(place * heads < query_heads, energy, 0.0)
    shifted = [
        lax.ppermute(energy, "head", [(i, (i + k) % planes) for i in range(planes)])
        for k in range(1, planes)
    ]
    teacher = pltpu.with_memory_space_constraint(teacher, pltpu.VMEM)
    grads = student_call(x, teacher, own(map_query), own(map_key))
    energy = sum(shifted, energy)
    power = power_of(energy)
    near_one = energy * jnp.exp2(-power)
    first = lax.reduce_precision(near_one, 5, 10)
    row = lax.broadcasted_iota(jnp.int32, energy.shape, 0)
    tail = jnp.where(row == 0, power, jnp.where(row == 1, first, (near_one - first) * 1024.0))
    gathered = lax.all_gather(jnp.concatenate([grads, tail]).astype(F16), "ctx")
    rows = heads * 2 * features
    power = gathered[:, rows : rows + heads].astype(F32)
    tail = gathered[:, -8:-5].astype(F32)
    energy = jnp.sum((tail[:, 1] + tail[:, 2] * (1.0 / 1024.0)) * jnp.exp2(tail[:, 0]), axis=0)
    factor = (jnp.exp2(power) * (2.0 * query_heads * planes / energy))[:, :, None]

    def unpacked(i):
        part = gathered[:, :rows].reshape(places, heads, 2, features, dim)[:, :, i]
        part = (part.astype(F32) * factor).reshape(places * heads, features, dim)
        return part[:query_heads].transpose(0, 2, 1)

    return (unpacked(0), unpacked(1))


def solution(mesh):
    placed = (
        P("ctx", "head", None),
        P("ctx", "head", None),
        P("ctx", "head", None),
        P("head", None, None),
        P("head", None, None),
    )
    return jax.shard_map(
        on_device,
        mesh=mesh,
        in_specs=placed,
        out_specs=(P("head", None, None), P("head", None, None)),
        check_vma=False,
    )
```

time: 90.5 us -> 63.2 us (0.70)
  Pallas kernels: 32.4 us -> 15.1 us
  local copies, waits for them, and re-layouts: 7.39 us -> 3.75 us
  between operations: 4.11 us -> 0.8 us
  other arithmetic: 5.92 us -> 3.27 us
  starting transfers between devices: 10.7 us -> 9.78 us
    pallas_call x1, Pallas kernels: 23.5 us -> 10.5 us  [student_call(): pl.pallas_call(functools.partial(student_kernel, heads), in_specs=[whole]...]
    pallas_call x1, Pallas kernels: 8.88 us -> 4.59 us  [teacher_call(): pl.pallas_call(functools.partial(teacher_kernel, heads, rows, 1.0 / math....]
    reduce_sum x2 -> x1, other arithmetic: 2.1 us -> 0.03 us  [on_device(): jnp.sum((tail[:, 1] + tail[:, 2] * (1.0 / 1024.0)) * jnp.exp2(tail[:, 0])...]
    slice x4 -> x2, local copies, waits for them, and re-layouts: 2.33 us -> 0.53 us  [unpacked(): part = gathered[:, :rows].reshape(places, heads, 2, features, dim)[:, :, i]]
    transpose x1, other arithmetic: 0.21 us -> 1.66 us  [unpacked(): return part[:query_heads].transpose(0, 2, 1)]
    squeeze x1 -> x0, local copies, waits for them, and re-layouts: 1.45 us -> none  [on_device(): return (result[0], result[1])]
    convert_element_type x3 -> x1, other arithmetic: 1.24 us -> 0.01 us  [on_device(): tail = gathered[:, -8:-5].astype(F32)]
    ppermute x3, starting transfers between devices: 5.52 us -> 4.6 us  [on_device(): lax.ppermute(energy, 'head', [(i, (i + k) % planes) for i in range(planes)])]
  transfers between devices with their start and end apart: 4 -> 4, of which waited for: 1 -> 1; matrix products, arithmetic and copies ran while one was open for 4% -> 2% of each run, Pallas kernels for 26% -> 17%
where the time goes in v2:
time: 63.2 us; the launch traced here: 62.9 us
  waiting for transfers between devices  20 us (32%)
  Pallas kernels  15.1 us (24%)
  blocking collectives  10.1 us (16%)
  starting transfers between devices  9.78 us (15%)
  local copies, waits for them, and re-layouts  3.75 us (6%)
  other arithmetic  3.27 us (5%)
  between operations  0.8 us (1%)
    all_to_all x1, waiting for transfers between devices, on_device(): x = lax.all_to_all(parts, 'ctx', 0, 0)  20 us
    pallas_call x1, Pallas kernels, student_call(): pl.pallas_call(functools.partial(student_kernel, heads), in_specs=[whole]...  10.5 us
    all_gather x1, blocking collectives, on_device(): gathered = lax.all_gather(jnp.concatenate([grads, tail]).astype(F16), 'ctx')  10.1 us
    all_to_all x1, starting transfers between devices, on_device(): x = lax.all_to_all(parts, 'ctx', 0, 0)  5.17 us
    ppermute x3, starting transfers between devices, on_device(): lax.ppermute(energy, 'head', [(i, (i + k) % planes) for i in range(planes)])  4.6 us
    pallas_call x1, Pallas kernels, teacher_call(): pl.pallas_call(functools.partial(teacher_kernel, heads, rows, 1.0 / math....  4.59 us
    unnamed x4, local copies, waits for them, and re-layouts  1.79 us
    transpose x1, other arithmetic, unpacked(): return part[:query_heads].transpose(0, 2, 1)  1.66 us
  transfers between devices with their start and end apart: 4, of which 1 were waited for; matrix products, arithmetic and copies ran while one was open for 2% of the time, Pallas kernels for 17%

profile of v2, /device:TPU:0, one launch (start us, length us, event | category | flops | bytes accessed | tf_op | source)
XLA Modules:
  0.0 62.9 jit_solution(17459526141327510254)
XLA Ops:
  0.6 0.0 copy-start
  0.6 0.9 %copy.13 = bf16[16,8,2,128]{3,1,2,0:T(8,128)(2,1)S(1)} copy(bf16[16,8,2,128]{3,2,1,0:T(2,128)(2,1)} %bitcast.64) | data formatting | bytes 131072
  1.6 0.9 %copy.14 = bf16[16,8,2,128]{3,1,2,0:T(8,128)(2,1)S(1)} copy(bf16[16,8,2,128]{3,2,1,0:T(2,128)(2,1)} %bitcast.65) | data formatting | bytes 131072
  2.6 0.0 copy-done
  2.6 0.4 copy.8
  3.0 1.3 %pad_maximum_fusion = bf16[8,6,128,128]{3,2,1,0:T(8,128)(2,1)} fusion(bf16[8,2,128,128]{3,2,1,0:T(8,128)(2,1)S(1)} %constant_dynamic-update-slice_fusion, bf16[8,4,128,128]{3,2,1,0:T(8,128)(2,1)S(1)} %bitcast.58), kind=kLoop, calls=%fused_computation | loop fusion | flops 786432 | bytes 3145728 | tf_op jit(solution)/shard_map/concatenate | solution.py:354
  4.3 5.2 %all-to-all-start = ((bf16[8,6,128,128]{3,2,1,0:T(8,128)(2,1)}), bf16[8,6,128,128]{3,2,1,0:T(8,128)(2,1)S(1)}, u32[]{:S(2)}, u32[]{:S(2)}) async-start(bf16[8,6,128,128]{3,2,1,0:T(8,128)(2,1)} %pad_maximum_fusion), calls=%async_computation | async-start | bytes 3145728 | tf_op jit(solution)/shard_map/all_to_all | solution.py:355
  9.5 1.0 %dynamic-slice_bitcast_fusion = (f32[4,64,128]{2,1,0:T(8,128)S(1)}, f32[4,64,128]{2,1,0:T(8,128)S(1)}) fusion(f32[32,128,64]{1,2,0:T(8,128)} %param.9, s32[]{:T(128)S(6)} %select_n.19, f32[32,128,64]{1,2,0:T(8,128)} %param.8), kind=kLoop, calls=%fused_computation.7 | loop fusion | bytes 524292 | tf_op jit(solution)/shard_map/dynamic_slice | solution.py:360
  10.5 20.0 %all-to-all-done.x_ref = bf16[8,6,128,128]{3,2,1,0:T(8,128)(2,1)S(1)} async-done(((bf16[8,6,128,128]{3,2,1,0:T(8,128)(2,1)}), bf16[8,6,128,128]{3,2,1,0:T(8,128)(2,1)S(1)}, u32[]{:S(2)}, u32[]{:S(2)}) %all-to-all-start) | async-done | bytes 1572896 | tf_op jit(solution)/shard_map/all_to_all | solution.py:355
  30.5 4.6 %shard_map.68 = (f32[8,4,128,128]{3,2,1,0:T(8,128)S(1)}, f32[8,128]{1,0:T(8,128)S(1)}) custom-call(bf16[8,6,128,128]{3,2,1,0:T(8,128)(2,1)S(1)} %all-to-all-done.x_ref), custom_call_target="tpu_custom_call" | custom-call | flops 1073741824 | bytes 4194304 | tf_op jit(solution)/shard_map/pallas_call | solution.py:122
  35.1 3.6 %collective-permute-start.2 = (f32[8,128]{1,0:T(8,128)S(1)}, f32[8,128]{1,0:T(8,128)S(1)}, u32[]{:S(2)}, u32[]{:S(2)}) collective-permute-start(f32[8,128]{1,0:T(8,128)S(1)} %broadcast_select_fusion), channel_id=1, source_target_pairs={{0,3},{1,0},{2,1},{3,2},{4,7},{5,4},{6,5},{7,6},{8,11},{9,8},{10,9... | collective-permute-start | bytes 12296 | tf_op jit(solution)/shard_map/ppermute | solution.py:365
  38.7 0.0 collective-permute-start.1
  38.7 1.0 %collective-permute-start = (f32[8,128]{1,0:T(8,128)S(1)}, f32[8,128]{1,0:T(8,128)S(1)}, u32[]{:S(2)}, u32[]{:S(2)}) collective-permute-start(f32[8,128]{1,0:T(8,128)S(1)} %broadcast_select_fusion), channel_id=1, source_target_pairs={{0,1},{1,2},{2,3},{3,0},{4,5},{5,6},{6,7},{7,4},{8,9},{9,10},{10,1... | collective-permute-start | bytes 12296 | tf_op jit(solution)/shard_map/ppermute | solution.py:365
  39.7 10.5 %shard_map.69 = f32[520,128]{1,0:T(8,128)S(1)} custom-call(bf16[8,6,128,128]{3,2,1,0:T(8,128)(2,1)S(1)} %all-to-all-done.x_ref, f32[8,4,128,128]{3,2,1,0:T(8,128)S(1)} %get-tuple-element.4.teacher_ref, f32[4,64,128]{2,1,0:T(8,128)S(1)} %get-tuple-element.19.mq_ref, f32[4,64,128]{2,1,0:T(8,128)S(1)} %get-tuple-element.18.mk_ref), custom_call_target="tpu_custom_call" | custom-call | flops 2684354560 | bytes 6291456 | tf_op jit(solution)/shard_map/pallas_call | solution.py:307
  50.3 0.0 collective-permute-done.2
  50.3 0.0 collective-permute-done.1
  50.3 0.0 collective-permute-done
  50.3 0.1 fusion.9
  50.5 10.1 %all-gather.1 = f16[8,528,128]{2,1,0:T(8,128)(2,1)S(1)} all-gather(f16[1,528,128]{2,1,0:T(8,128)(2,1)S(1)} %pad_maximum_fusion.1), channel_id=1, replica_groups=mesh['ctx'=8,'head'=4] {'ctx'}, dimensions={0}, use_global_device_ids=true | all-gather | bytes 1216512 | tf_op jit(solution)/shard_map/all_gather | solution.py:376
  60.6 0.2 slice.65
  60.8 0.3 fusion.10
  61.2 1.7 %fusion = (f32[32,128,64]{1,2,0:T(8,128)}, f32[32,128,64]{1,2,0:T(8,128)}) fusion(f16[8,4,1,64,128]{4,3,2,1,0:T(8,128)(2,1)S(1)} %get-tuple-element.6, f32[32,128]{1,0:T(8,128)S(1)} %bitcast.63, f16[8,4,1,64,128]{4,3,2,1,0:T(8,128)(2,1)S(1)} %get-tuple-element.7), kind=kLoop, calls=%fused_computation.2 | loop fusion | flops 1048576 | bytes 3162112 | tf_op jit(solution)/shard_map/transpose | solution.py:386
  (17 shorter events, 0.3 us)
Async XLA Ops:
  0.6 2.0 %copy-start = (bf16[128,32,128]{2,1,0:T(8,128)(2,1)S(1)}, bf16[128,32,128]{2,1,0:T(8,128)(2,1)}, u32[]{:S(2)}) copy-start(bf16[128,32,128]{2,1,0:T(8,128)(2,1)} %param.5) | copy-start | bytes 3145732
  4.3 26.2 %all-to-all-start = ((bf16[8,6,128,128]{3,2,1,0:T(8,128)(2,1)}), bf16[8,6,128,128]{3,2,1,0:T(8,128)(2,1)S(1)}, u32[]{:S(2)}, u32[]{:S(2)}) async-start(bf16[8,6,128,128]{3,2,1,0:T(8,128)(2,1)} %pad_maximum_fusion), calls=%async_computation | async-start | bytes 3145728 | tf_op jit(solution)/shard_map/all_to_all | solution.py:355
  35.1 15.2 %collective-permute-start.2 = (f32[8,128]{1,0:T(8,128)S(1)}, f32[8,128]{1,0:T(8,128)S(1)}, u32[]{:S(2)}, u32[]{:S(2)}) collective-permute-start(f32[8,128]{1,0:T(8,128)S(1)} %broadcast_select_fusion), channel_id=1, source_target_pairs={{0,3},{1,0},{2,1},{3,2},{4,7},{5,4},{6,5},{7,6},{8,11},{9,8},{10,9... | collective-permute-start | bytes 12296 | tf_op jit(solution)/shard_map/ppermute | solution.py:365
  38.7 11.6 %collective-permute-start.1 = (f32[8,128]{1,0:T(8,128)S(1)}, f32[8,128]{1,0:T(8,128)S(1)}, u32[]{:S(2)}, u32[]{:S(2)}) collective-permute-start(f32[8,128]{1,0:T(8,128)S(1)} %broadcast_select_fusion), channel_id=1, source_target_pairs={{0,2},{1,3},{2,0},{3,1},{4,6},{5,7},{6,4},{7,5},{8,10},{9,11},{10,... | collective-permute-start | bytes 12296 | tf_op jit(solution)/shard_map/ppermute | solution.py:365
  38.7 11.6 %collective-permute-start = (f32[8,128]{1,0:T(8,128)S(1)}, f32[8,128]{1,0:T(8,128)S(1)}, u32[]{:S(2)}, u32[]{:S(2)}) collective-permute-start(f32[8,128]{1,0:T(8,128)S(1)} %broadcast_select_fusion), channel_id=1, source_target_pairs={{0,1},{1,2},{2,3},{3,0},{4,5},{5,6},{6,7},{7,4},{8,9},{9,10},{10,1... | collective-permute-start | bytes 12296 | tf_op jit(solution)/shard_map/ppermute | solution.py:365

commit v3 on v2

--- a/solution.py
+++ b/solution.py
@@ -3,7 +3,6 @@
 
 import jax
 import jax.numpy as jnp
-import numpy as np
 from jax import lax
 from jax.experimental import pallas as pl
 from jax.experimental.pallas import tpu as pltpu
@@ -50,12 +49,29 @@
     return column <= row + shift
 
 
-def teacher_kernel(heads, rows, scale, x_ref, out_ref, energy_ref, scores_ref):
+def teacher_kernel(shape, rows, scale, source_of, place_ref, *refs):
+    places, cores, heads, with_keys = shape
+    chips = places // cores
+    pieces, refs = refs[:chips], refs[chips:]
+    if with_keys:
+        keys, refs = refs[:cores], refs[cores:]
+        x_ref, kv_ref, out_ref, energy_ref, scores_ref = refs
+    else:
+        kv_ref, before_ref, x_ref, out_ref, energy_ref, scores_ref = refs
     blocks, _, chunk, dim = x_ref.shape
     per_row = rows // chunk
     steps = blocks // per_row
     power = scale * math.log2(math.e)
     mask = causal(rows, rows, 0)
+    place = place_ref[0]
+    core = place % cores
+    for j, piece in enumerate(pieces):
+        base = source_of(place // cores, j) * cores
+        for i in range(cores):
+            block = base + (core if i == 0 else 1 - core)
+            x_ref[block] = piece[i]
+            if with_keys:
+                kv_ref[block] = keys[i][j]
 
     def finish(h, r, weighted, total):
         teacher = weighted / total
@@ -63,13 +79,16 @@
             out_ref[r * per_row + i, h] = teacher[i * chunk : (i + 1) * chunk]
         return jnp.sum((teacher * teacher).reshape(rows // 8, 8, dim), axis=0)
 
-    def take(h, r, count=1):
-        return x_ref[pl.ds(r * per_row, count * per_row), h].reshape(count * rows, dim)
+    def take(h, r):
+        return x_ref[pl.ds(r * per_row, per_row), h].reshape(rows, dim)
+
+    def keyed(i, r, count=1):
+        return kv_ref[pl.ds(r * per_row, count * per_row), i].reshape(count * rows, dim)
 
     def one_head(h, energy):
         parts, tops, done = [], [], []
         for r in range(steps):
-            scores = dot_nt(take(h, r), take(heads, 0, r + 1))
+            scores = dot_nt(take(h, r), keyed(0, 0, r + 1))
             last = jnp.where(mask, scores[:, r * rows :], -1e30)
             scores = beside(scores[:, : r * rows], last) if r else last
             parts.append(scores)
@@ -77,7 +96,7 @@
         for r in range(steps):
             weights = jnp.exp2((parts[r] - tops[r]) * power)
             total = jnp.sum(weights, axis=1, keepdims=True)
-            done.append((dot(weights.astype(BF16), take(heads + 1, 0, r + 1)), total))
+            done.append((dot(weights.astype(BF16), keyed(1, 0, r + 1)), total))
         for r in range(steps):
             energy = energy + finish(h, r, *done[r])
         return energy
@@ -87,7 +106,7 @@
             q = take(h, r)
 
             def look(j, top):
-                scores = dot_nt(q, take(heads, j))
+                scores = dot_nt(q, keyed(0, j))
                 scores = jnp.where((j < r) | mask, scores, -1e30)
                 scores_ref[j] = scores
                 return jnp.maximum(top, jnp.max(scores, axis=1, keepdims=True))
@@ -98,7 +117,7 @@
                 weighted, total = state
                 weights = jnp.exp2((scores_ref[j] - top) * power)
                 total = total + jnp.sum(weights, axis=1, keepdims=True)
-                return weighted + dot(weights.astype(BF16), take(heads + 1, j)), total
+                return weighted + dot(weights.astype(BF16), keyed(1, j)), total
 
             weighted, total = lax.fori_loop(
                 0, r + 1, add, (jnp.zeros((rows, dim), F32), jnp.zeros((rows, 1), F32))
@@ -110,36 +129,54 @@
     body = one_head if steps <= 8 else one_long_head
     energy = lax.fori_loop(0, heads, body, jnp.zeros((8, dim), F32))
     energy = jnp.sum(jnp.sum(energy, axis=0, keepdims=True), axis=1, keepdims=True)
-    energy_ref[...] = jnp.broadcast_to(energy, energy_ref.shape)
-
-
-def teacher_call(x, heads):
-    blocks, _, chunk, dim = x.shape
-    rows = 2 * chunk if blocks % 2 == 0 else chunk
-    steps = blocks * chunk // rows
+    energy = jnp.broadcast_to(energy, energy_ref.shape)
+    energy_ref[...] = energy if with_keys else energy + before_ref[...]
+
+
+def in_vmem(a):
+    return pltpu.with_memory_space_constraint(a, pltpu.VMEM)
+
+
+def teacher_call(place, pieces, kv, keys, before, places, source_of):
+    cores, heads, chunk, dim = pieces[0].shape
+    with_keys = kv is None
+    rows = 2 * chunk if places % 2 == 0 else chunk
+    steps = places * chunk // rows
     held = (steps, rows, rows) if steps > 8 else (1, 8, 128)
     whole = pl.BlockSpec(memory_space=pltpu.VMEM)
+    operands = [in_vmem(p) for p in pieces + (keys if with_keys else [kv])]
+    operands += [] if with_keys else [before]
     return pl.pallas_call(
-        functools.partial(teacher_kernel, heads, rows, 1.0 / math.sqrt(dim)),
-        in_specs=[whole],
-        out_specs=[whole, whole],
-        out_shape=[
-            pltpu.VMEM((blocks, heads, chunk, dim), F32),
+        functools.partial(
+            teacher_kernel,
+            (places, cores, heads, with_keys),
+            rows,
+            1.0 / math.sqrt(dim),
+            source_of,
+        ),
+        in_specs=[pl.BlockSpec(memory_space=pltpu.SMEM)] + [whole] * len(operands),
+        out_specs=[whole] * (3 + with_keys),
+        out_shape=[pltpu.VMEM((places, heads, chunk, dim), BF16)]
+        + [pltpu.VMEM((places, 2, chunk, dim), BF16)] * with_keys
+        + [
+            pltpu.VMEM((places, heads, chunk, dim), F32),
             jax.ShapeDtypeStruct((8, dim), F32),
         ],
         scratch_shapes=[pltpu.VMEM(held, F32)],
         compiler_params=pltpu.CompilerParams(vmem_limit_bytes=VMEM_LIMIT),
         cost_estimate=pl.CostEstimate(
-            flops=2 * heads * (blocks * chunk) ** 2 * dim,
-            bytes_accessed=8 * heads * blocks * chunk * dim,
-            transcendentals=heads * (blocks * chunk) ** 2 // 2,
+            flops=10 * heads * (places * chunk) ** 2 * dim,
+            bytes_accessed=8 * heads * places * chunk * dim,
+            transcendentals=heads * (places * chunk) ** 2 // 2,
         ),
-    )(x)
+    )(place, *operands)
 
 
 def student_kernel(
+    start,
     heads,
     x_ref,
+    kv_ref,
     teacher_ref,
     mq_ref,
     mk_ref,
@@ -162,11 +199,11 @@
     both = 2 * features
     spare = grad_ref.shape[0] - heads * both
     at = [slice(h * both, (h + 1) * both) for h in range(heads)]
-    per = next(p for p in (4, 2, 1) if blocks % p == 0)
+    per = next(p for p in (8, 4, 2, 1) if blocks % p == 0 and (p * heads <= 16 or p == 1))
 
     for h in range(heads):
         for source, target in ((mq_ref, wq_ref), (mk_ref, wk_ref)):
-            high, low = halves(source[h])
+            high, low = halves(source[start + h])
             target[at[h], :] = below(beside(high, low), beside(-high, -low))
     state_ref[...] = jnp.zeros_like(state_ref)
     sum_q_ref[...] = jnp.zeros_like(sum_q_ref)
@@ -177,11 +214,11 @@
 
     def features_of(i, carry):
         chunks = [i * per + j for j in range(per)]
-        keys = [x_ref[r, heads] for r in chunks]
+        keys = [kv_ref[r, 0] for r in chunks]
         pairs = [
             beside(*halves(feature(dot_nt(wk_ref[...], beside(k, k))))) for k in keys
         ]
-        wide = [beside(x_ref[r, heads + 1], ones) for r in chunks]
+        wide = [beside(kv_ref[r, 1], ones) for r in chunks]
         added = [dot(p, below(w, w)) for p, w in zip(pairs, wide)]
         for r in chunks:
             for h in range(heads):
@@ -223,7 +260,7 @@
             return dot(beside(q, q), below(s[:, : 2 * dim], s[:, 2 * dim :]))
 
         inner = stacked([weigh(r, h) for r, h in pairs])
-        values = [x_ref[r, heads + 1] for r in chunks]
+        values = [kv_ref[r, 1] for r in chunks]
         wide = [beside(v, ones) for v in values]
         state_part = stacked([from_before(r, h) for r, h in pairs])
         out = [
@@ -277,7 +314,7 @@
             later = later + own[:, :dim]
             bias = bias + below(*later_bias[j * heads : (j + 1) * heads])
         sum_k_ref[...] += dot(
-            beside(*key_side), below(*[x_ref[r, heads] for r in chunks for _ in range(2)])
+            beside(*key_side), below(*[kv_ref[r, 0] for r in chunks for _ in range(2)])
         )
         later_ref[...] = later
         bias_ref[...] = jnp.broadcast_to(bias, bias_ref.shape)
@@ -299,14 +336,14 @@
         grad_ref[pl.ds(heads * both + h, 1), :] = jnp.broadcast_to(power, (1, dim))
 
 
-def student_call(x, teacher, map_query, map_key):
-    blocks, _, chunk, dim = x.shape
-    heads, features, _ = map_query.shape
+def student_call(start, x, kv, teacher, map_query, map_key):
+    blocks, heads, chunk, dim = x.shape
+    features = map_query.shape[1]
     rows = heads * 2 * features
     whole = pl.BlockSpec(memory_space=pltpu.VMEM)
     return pl.pallas_call(
-        functools.partial(student_kernel, heads),
-        in_specs=[whole] * 4,
+        functools.partial(student_kernel, start, heads),
+        in_specs=[whole] * 5,
         out_specs=whole,
         out_shape=jax.ShapeDtypeStruct((rows + (heads + 7) // 8 * 8, dim), F32),
         scratch_shapes=[
@@ -325,11 +362,70 @@
         ],
         compiler_params=pltpu.CompilerParams(vmem_limit_bytes=VMEM_LIMIT),
         cost_estimate=pl.CostEstimate(
-            flops=40 * rows * blocks * chunk * dim,
+            flops=200 * rows * blocks * chunk * dim,
             bytes_accessed=12 * heads * blocks * chunk * dim,
             transcendentals=3 * rows * blocks * chunk,
         ),
-    )(x, teacher, map_query, map_key)
+    )(in_vmem(x), in_vmem(kv), in_vmem(teacher), map_query, map_key)
+
+
+def exchange(queries, key_states, value_vector_states, heads, parts):
+    places = lax.axis_size("ctx")
+    cores = 2 if places % 2 == 0 else 1
+    chips = places // cores
+    place = lax.axis_index("ctx")
+    core, chip = place % cores, place // cores
+    tokens, query_heads, dim = queries.shape
+    key_heads = key_states.shape[1]
+    padding = heads * places - query_heads
+    mirrored = chips & (chips - 1) == 0
+
+    def target_of(at, j):
+        return at ^ j if mirrored else (at + j) % chips
+
+    def source_of(at, j):
+        return at ^ j if mirrored else (at + chips - j) % chips
+
+    def send(a, j):
+        return lax.ppermute(
+            a, "ctx", [(i, target_of(i // cores, j) * cores + i % cores) for i in range(places)]
+        )
+
+    def swap(a):
+        return lax.ppermute(a, "ctx", [(i, i ^ 1) for i in range(places)])
+
+    def pick(a, i, axis=0):
+        return lax.dynamic_index_in_dim(a, i, axis, False)
+
+    by_head = jnp.pad(queries, ((0, 0), (0, padding), (0, 0))) if padding else queries
+    by_head = by_head.transpose(1, 0, 2).reshape(chips, cores, heads, tokens, dim)
+    flat = [a.reshape(tokens, key_heads * dim) for a in (key_states, value_vector_states)]
+    kv = jnp.stack(
+        [jnp.stack([a[:, g * dim : (g + 1) * dim] for a in flat]) for g in range(key_heads)]
+    )
+    def group_of(at):
+        first = jnp.minimum((at * cores + core) * heads, query_heads - 1)
+        return first // (query_heads // key_heads)
+
+    mine = [pick(by_head, core, 1)]
+    if cores == 2:
+        mine.append(swap(pick(by_head, 1 - core, 1)))
+    own_keys = [pick(kv, group_of(target_of(chip, j))) for j in range(chips)]
+    own_keys = [own_keys[0]] + [send(a, j) for j, a in enumerate(own_keys) if j]
+    keys = [jnp.stack(own_keys)]
+    arrived = []
+    for start, stop in parts:
+        pieces = []
+        for j in range(chips):
+            target = target_of(chip, j)
+            pieces.append(jnp.stack([pick(q, target)[start:stop] for q in mine]))
+        if arrived and chips > 1:
+            pieces = lax.optimization_barrier((*pieces, arrived[-1][1]))[:chips]
+        arrived.append([pieces[0]] + [send(a, j) for j, a in enumerate(pieces) if j])
+        if cores == 2 and len(keys) == 1:
+            ready = lax.optimization_barrier((keys[0], arrived[0][chips > 1]))[0]
+            keys.append(swap(ready))
+    return arrived, keys, source_of
 
 
 def on_device(queries, key_states, value_vector_states, map_query, map_key):
@@ -342,41 +438,50 @@
     group = query_heads // key_heads
     heads = min(d for d in range(1, group + 1) if group % d == 0 and d * places >= query_heads)
     padding = heads * places - query_heads
-    key_of = np.minimum(np.arange(places) * heads, query_heads - 1) // group
-
-    def padded(a, axis):
-        width = [(0, padding if i == axis else 0) for i in range(a.ndim)]
-        return jnp.pad(a, width) if padding else a
-
-    by_head = padded(queries, 1).transpose(1, 0, 2).reshape(places, heads, tokens, dim)
-    flat = [a.reshape(tokens, key_heads * dim) for a in (key_states, value_vector_states)]
-    keyed = [jnp.stack([a[:, g * dim : (g + 1) * dim] for a in flat]) for g in key_of]
-    parts = jnp.concatenate([by_head, jnp.stack(keyed)], axis=1)
-    x = lax.all_to_all(parts, "ctx", 0, 0)
-    x = pltpu.with_memory_space_constraint(x, pltpu.VMEM)
+    half = heads // 2
+    parts = [(0, half), (half, heads)] if half else [(0, heads)]
+    arrived, keys, source_of = exchange(queries, key_states, value_vector_states, heads, parts)
 
     def own(weights):
-        weights = padded(weights, 0).transpose(0, 2, 1)
+        weights = weights.transpose(0, 2, 1)
+        weights = jnp.pad(weights, ((0, padding), (0, 0), (0, 0))) if padding else weights
         return lax.dynamic_slice_in_dim(weights, place * heads, heads, 0)
 
-    teacher, energy = teacher_call(x, heads)
+    own_query, own_key = own(map_query), own(map_key)
+    position = place.astype(jnp.int32).reshape(1)
+    kv, energy, grads, powers = None, None, [], []
+    for (start, stop), pieces in zip(parts, arrived):
+        x, *found = teacher_call(position, pieces, kv, keys, energy, places, source_of)
+        if kv is None:
+            kv = found.pop(0)
+        teacher, energy = found
+        rows = (stop - start) * 2 * features
+        result = student_call(start, x, kv, teacher, own_query, own_key)
+        if stop < heads:
+            energy, result = lax.optimization_barrier((energy, result))
+        grads.append(result[:rows])
+        powers.append(result[rows:])
     energy = jnp.where(place * heads < query_heads, energy, 0.0)
     shifted = [
         lax.ppermute(energy, "head", [(i, (i + k) % planes) for i in range(planes)])
         for k in range(1, planes)
     ]
-    teacher = pltpu.with_memory_space_constraint(teacher, pltpu.VMEM)
-    grads = student_call(x, teacher, own(map_query), own(map_key))
     energy = sum(shifted, energy)
     power = power_of(energy)
     near_one = energy * jnp.exp2(-power)
     first = lax.reduce_precision(near_one, 5, 10)
     row = lax.broadcasted_iota(jnp.int32, energy.shape, 0)
     tail = jnp.where(row == 0, power, jnp.where(row == 1, first, (near_one - first) * 1024.0))
-    gathered = lax.all_gather(jnp.concatenate([grads, tail]).astype(F16), "ctx")
+    sent = jnp.concatenate(grads + powers + [tail]).astype(F16)
+    used = sent.shape[0]
+    gathered = lax.all_gather(jnp.pad(sent, ((0, -used % 16), (0, 0))), "ctx")
     rows = heads * 2 * features
-    power = gathered[:, rows : rows + heads].astype(F32)
-    tail = gathered[:, -8:-5].astype(F32)
+    power, at = [], rows
+    for (start, stop), p in zip(parts, powers):
+        power.append(gathered[:, at : at + stop - start])
+        at += p.shape[0]
+    power = jnp.concatenate(power, axis=1).astype(F32)
+    tail = gathered[:, at : at + 3].astype(F32)
     energy = jnp.sum((tail[:, 1] + tail[:, 2] * (1.0 / 1024.0)) * jnp.exp2(tail[:, 0]), axis=0)
     factor = (jnp.exp2(power) * (2.0 * query_heads * planes / energy))[:, :, None]
 

time: 63.2 us -> 55.8 us (0.88)
  waiting for transfers between devices: 20 us -> 5.41 us
  starting transfers between devices: 9.78 us -> 17.8 us
  other arithmetic: 3.27 us -> 2.14 us
    all_to_all x1 -> x0, waiting for transfers between devices: 20 us -> none  [on_device(): x = lax.all_to_all(parts, 'ctx', 0, 0)]
    ppermute x0 -> x11, starting transfers between devices: none -> 12.3 us  [the longest x9 11.8 us: send(): lax.ppermute(a, 'ctx', [(i, target_of(i // cores, j) * cores + i % cores)...]
    ppermute x0 -> x11, waiting for transfers between devices: none -> 5.4 us  [the longest x9 5.4 us: send(): lax.ppermute(a, 'ctx', [(i, target_of(i // cores, j) * cores + i % cores)...]
    all_to_all x1 -> x0, starting transfers between devices: 5.17 us -> none  [on_device(): x = lax.all_to_all(parts, 'ctx', 0, 0)]
    unnamed x4 -> x10, local copies, waits for them, and re-layouts: 1.79 us -> 0.34 us
    concatenate x4 -> x1, other arithmetic: 1.42 us -> 0.08 us  [on_device(): sent = jnp.concatenate(grads + powers + [tail]).astype(F16)]
    transpose x1, local copies, waits for them, and re-layouts: 0.41 us -> 1.63 us  [exchange(): by_head.transpose(1, 0, 2).reshape(chips, cores, heads, tokens, dim)]
    ppermute x3, starting transfers between devices: 4.6 us -> 5.52 us  [on_device(): lax.ppermute(energy, 'head', [(i, (i + k) % planes) for i in range(planes)])]
  transfers between devices with their start and end apart: 4 -> 14, of which waited for: 1 -> 3; matrix products, arithmetic and copies ran while one was open for 2% -> 3% of each run, Pallas kernels for 17% -> 23%
where the time goes in v3:
time: 55.8 us; the launch traced here: 55.6 us
  starting transfers between devices  17.8 us (32%)
  Pallas kernels  15 us (27%)
  blocking collectives  10.5 us (19%)
  waiting for transfers between devices  5.41 us (10%)
  local copies, waits for them, and re-layouts  3.71 us (7%)
  other arithmetic  2.14 us (4%)
  between operations  0.99 us (2%)
    ppermute x9, starting transfers between devices, send(): lax.ppermute(a, 'ctx', [(i, target_of(i // cores, j) * cores + i % cores)...  11.8 us
    all_gather x1, blocking collectives, on_device(): gathered = lax.all_gather(jnp.pad(sent, ((0, -used % 16), (0, 0))), 'ctx')  10.5 us
    pallas_call x2, Pallas kernels, student_call(): pl.pallas_call(functools.partial(student_kernel, start, heads), in_specs=...  10.2 us
    ppermute x3, starting transfers between devices, on_device(): lax.ppermute(energy, 'head', [(i, (i + k) % planes) for i in range(planes)])  5.52 us
    ppermute x9, waiting for transfers between devices, send(): lax.ppermute(a, 'ctx', [(i, target_of(i // cores, j) * cores + i % cores)...  5.4 us
    pallas_call x2, Pallas kernels, teacher_call(): pl.pallas_call(functools.partial(teacher_kernel, (places, cores, heads, w...  4.8 us
    transpose x1, other arithmetic, unpacked(): return part[:query_heads].transpose(0, 2, 1)  1.66 us
    transpose x1, local copies, waits for them, and re-layouts, exchange(): by_head.transpose(1, 0, 2).reshape(chips, cores, heads, tokens, dim)  1.63 us
  transfers between devices with their start and end apart: 14, of which 3 were waited for; matrix products, arithmetic and copies ran while one was open for 3% of the time, Pallas kernels for 23%

profile of v3, /device:TPU:0, one launch (start us, length us, event | category | flops | bytes accessed | tf_op | source)
XLA Modules:
  0.0 55.6 jit_solution(8380818236321969514)
XLA Ops:
  0.6 1.6 %copy.7 = bf16[32,128,128]{2,1,0:T(8,128)(2,1)S(1)} copy(bf16[32,128,128]{2,0,1:T(8,128)(2,1)} %bitcast.81) | data formatting | bytes 2097152 | tf_op jit(solution)/shard_map/transpose | solution.py:401
  2.3 0.0 copy-start
  2.3 0.0 copy-start.1
  2.4 0.5 collective-permute-start
  2.9 0.2 copy-done
  3.2 0.0 copy-done.1
  3.2 0.1 fusion.4
  3.4 3.0 %collective-permute-start.4 = (bf16[2,128,128]{2,1,0:T(8,128)(2,1)S(1)}, bf16[2,128,128]{2,1,0:T(8,128)(2,1)S(1)}, u32[]{:S(2)}, u32[]{:S(2)}) collective-permute-start(bf16[2,128,128]{2,1,0:T(8,128)(2,1)S(1)} %get-tuple-element.51), channel_id=1, source_target_pairs={{0,8},{4,12},{8,0},{12,4},{16,24},{20,28},{24,16},{28,20},{1,9},{5... | collective-permute-start | bytes 196616 | tf_op jit(solution)/shard_map/ppermute | solution.py:390
  6.4 1.5 %collective-permute-start.5 = (bf16[2,128,128]{2,1,0:T(8,128)(2,1)S(1)}, bf16[2,128,128]{2,1,0:T(8,128)(2,1)S(1)}, u32[]{:S(2)}, u32[]{:S(2)}) collective-permute-start(bf16[2,128,128]{2,1,0:T(8,128)(2,1)S(1)} %get-tuple-element.52), channel_id=1, source_target_pairs={{0,16},{4,20},{8,24},{12,28},{16,0},{20,4},{24,8},{28,12},{1,17},{... | collective-permute-start | bytes 196616 | tf_op jit(solution)/shard_map/ppermute | solution.py:390
  7.9 0.0 collective-permute-start.6
  7.9 1.0 %dynamic-slice_bitcast_fusion.1 = (f32[4,64,128]{2,1,0:T(8,128)S(1)}, f32[4,64,128]{2,1,0:T(8,128)S(1)}) fusion(f32[32,128,64]{1,2,0:T(8,128)} %param.9, s32[]{:T(128)S(6)} %select_n.118, f32[32,128,64]{1,2,0:T(8,128)} %param.8), kind=kLoop, calls=%fused_computation.22 | loop fusion | bytes 524292 | tf_op jit(solution)/shard_map/dynamic_slice | solution.py:448
  8.9 0.1 dynamic-slice_bitcast_fusion.3
  9.0 0.0 collective-permute-done.4
  9.0 1.7 %collective-permute-done.5 = bf16[2,128,128]{2,1,0:T(8,128)(2,1)S(1)} collective-permute-done((bf16[2,128,128]{2,1,0:T(8,128)(2,1)S(1)}, bf16[2,128,128]{2,1,0:T(8,128)(2,1)S(1)}, u32[]{:S(2)}, u32[]{:S(2)}) %collective-permute-start.5) | collective-permute-done | bytes 65568 | tf_op jit(solution)/shard_map/ppermute | solution.py:390
  10.6 2.4 %collective-permute-done.6 = bf16[2,128,128]{2,1,0:T(8,128)(2,1)S(1)} collective-permute-done((bf16[2,128,128]{2,1,0:T(8,128)(2,1)S(1)}, bf16[2,128,128]{2,1,0:T(8,128)(2,1)S(1)}, u32[]{:S(2)}, u32[]{:S(2)}) %collective-permute-start.6) | collective-permute-done | bytes 65568 | tf_op jit(solution)/shard_map/ppermute | solution.py:390
  13.1 0.0 collective-permute-done
  13.1 0.1 constant_dynamic-slice_fusion.4
  13.2 0.6 %collective-permute-start.1 = (bf16[2,2,128,128]{3,2,1,0:T(8,128)(2,1)S(1)}, bf16[2,2,128,128]{3,2,1,0:T(8,128)(2,1)S(1)}, u32[]{:S(2)}, u32[]{:S(2)}) collective-permute-start(bf16[2,2,128,128]{3,2,1,0:T(8,128)(2,1)S(1)} %pad_maximum_fusion.2), channel_id=1, source_target_pairs={{0,8},{4,12},{8,0},{12,4},{16,24},{20,28},{24,16},{28,20},{1,9},{5... | collective-permute-start | bytes 393224 | tf_op jit(solution)/shard_map/ppermute | solution.py:390
  13.8 1.5 %collective-permute-start.3 = (bf16[2,2,128,128]{3,2,1,0:T(8,128)(2,1)S(1)}, bf16[2,2,128,128]{3,2,1,0:T(8,128)(2,1)S(1)}, u32[]{:S(2)}, u32[]{:S(2)}) collective-permute-start(bf16[2,2,128,128]{3,2,1,0:T(8,128)(2,1)S(1)} %pad_maximum_fusion.4), channel_id=1, source_target_pairs={{0,24},{4,28},{8,16},{12,20},{16,8},{20,12},{24,0},{28,4},{1,25},{... | collective-permute-start | bytes 393224 | tf_op jit(solution)/shard_map/ppermute | solution.py:390
  15.3 1.6 %collective-permute-start.2 = (bf16[2,2,128,128]{3,2,1,0:T(8,128)(2,1)S(1)}, bf16[2,2,128,128]{3,2,1,0:T(8,128)(2,1)S(1)}, u32[]{:S(2)}, u32[]{:S(2)}) collective-permute-start(bf16[2,2,128,128]{3,2,1,0:T(8,128)(2,1)S(1)} %pad_maximum_fusion.3), channel_id=1, source_target_pairs={{0,16},{4,20},{8,24},{12,28},{16,0},{20,4},{24,8},{28,12},{1,17},{... | collective-permute-start | bytes 393224 | tf_op jit(solution)/shard_map/ppermute | solution.py:390
  16.9 1.3 %collective-permute-done.1.refs_1_ = bf16[2,2,128,128]{3,2,1,0:T(8,128)(2,1)S(1)} collective-permute-done((bf16[2,2,128,128]{3,2,1,0:T(8,128)(2,1)S(1)}, bf16[2,2,128,128]{3,2,1,0:T(8,128)(2,1)S(1)}, u32[]{:S(2)}, u32[]{:S(2)}) %collective-permute-start.1) | collective-permute-done | bytes 131104 | tf_op jit(solution)/shard_map/ppermute | solution.py:390
  18.2 0.0 collective-permute-start.7
  18.3 1.4 %collective-permute-start.10 = (bf16[2,2,128,128]{3,2,1,0:T(8,128)(2,1)S(1)}, bf16[2,2,128,128]{3,2,1,0:T(8,128)(2,1)S(1)}, u32[]{:S(2)}, u32[]{:S(2)}) collective-permute-start(bf16[2,2,128,128]{3,2,1,0:T(8,128)(2,1)S(1)} %get-tuple-element.25), channel_id=1, source_target_pairs={{0,24},{4,28},{8,16},{12,20},{16,8},{20,12},{24,0},{28,4},{1,25},{... | collective-permute-start | bytes 393224 | tf_op jit(solution)/shard_map/ppermute | solution.py:390
  19.7 1.0 %collective-permute-start.8 = (bf16[2,2,128,128]{3,2,1,0:T(8,128)(2,1)S(1)}, bf16[2,2,128,128]{3,2,1,0:T(8,128)(2,1)S(1)}, u32[]{:S(2)}, u32[]{:S(2)}) collective-permute-start(bf16[2,2,128,128]{3,2,1,0:T(8,128)(2,1)S(1)} %get-tuple-element.23), channel_id=1, source_target_pairs={{0,8},{4,12},{8,0},{12,4},{16,24},{20,28},{24,16},{28,20},{1,9},{5... | collective-permute-start | bytes 393224 | tf_op jit(solution)/shard_map/ppermute | solution.py:390
  20.7 0.0 collective-permute-done.3.refs_3_
  20.7 1.2 %collective-permute-start.9 = (bf16[2,2,128,128]{3,2,1,0:T(8,128)(2,1)S(1)}, bf16[2,2,128,128]{3,2,1,0:T(8,128)(2,1)S(1)}, u32[]{:S(2)}, u32[]{:S(2)}) collective-permute-start(bf16[2,2,128,128]{3,2,1,0:T(8,128)(2,1)S(1)} %get-tuple-element.24), channel_id=1, source_target_pairs={{0,16},{4,20},{8,24},{12,28},{16,0},{20,4},{24,8},{28,12},{1,17},{... | collective-permute-start | bytes 393224 | tf_op jit(solution)/shard_map/ppermute | solution.py:390
  21.9 0.0 collective-permute-done.2.refs_2_
  21.9 0.0 collective-permute-done.7.refs_5_
  21.9 2.4 %shard_map.68 = (bf16[8,2,128,128]{3,2,1,0:T(8,128)(2,1)S(1)}, bf16[8,2,128,128]{3,2,1,0:T(8,128)(2,1)S(1)}, f32[8,2,128,128]{3,2,1,0:T(8,128)S(1)}, f32[8,128]{1,0:T(8,128)S(1)}) custom-call(s32[1]{0:T(128)} %bitcast.place_ref, bf16[2,2,128,128]{3,2,1,0:T(8,128)(2,1)S(1)} %pad_maximum_fusion.1.refs_0_, ...), custom_call_target="tpu_custom_call" | custom-call | flops 2684354560 | bytes 2097152 | tf_op jit(solution)/shard_map/pallas_call | solution.py:149
  24.3 5.1 %shard_map.69 = f32[264,128]{1,0:T(8,128)S(1)} custom-call(bf16[8,2,128,128]{3,2,1,0:T(8,128)(2,1)S(1)} %get-tuple-element.18.x_ref, bf16[8,2,128,128]{3,2,1,0:T(8,128)(2,1)S(1)} %get-tuple-element.19.kv_ref.refs_4_, f32[8,2,128,128]{3,2,1,0:T(8,128)S(1)} %get-tuple-element.20.teacher_ref, f32[4,64,128]{2,1,0:T(8,128)S(1)} %get-tuple-element.67.mq_ref, ...), custom_call_target="tpu_custom_call" | custom-call | flops 6710886400 | bytes 3145728 | tf_op jit(solution)/shard_map/pallas_call | solution.py:344
  29.4 0.0 collective-permute-done.10.refs_3_
  29.4 0.0 collective-permute-done.8.refs_1_
  29.4 0.0 collective-permute-done.9.refs_2_
  29.5 2.4 %shard_map.70 = (bf16[8,2,128,128]{3,2,1,0:T(8,128)(2,1)S(1)}, f32[8,2,128,128]{3,2,1,0:T(8,128)S(1)}, f32[8,128]{1,0:T(8,128)S(1)}) custom-call(s32[1]{0:T(128)} %bitcast.place_ref, bf16[2,2,128,128]{3,2,1,0:T(8,128)(2,1)S(1)} %get-tuple-element.22.refs_0_, bf16[2,2,128,128]{3,2,1,0:T(8,128)(2,1)S(1)} %collective-permute-done.8.refs_1_, ...), custom_call_target="tpu_custom_call" | custom-call | flops 2684354560 | bytes 2097152 | tf_op jit(solution)/shard_map/pallas_call | solution.py:149
  31.9 1.6 %collective-permute-start.11 = (f32[8,128]{1,0:T(8,128)S(1)}, f32[8,128]{1,0:T(8,128)S(1)}, u32[]{:S(2)}, u32[]{:S(2)}) collective-permute-start(f32[8,128]{1,0:T(8,128)S(1)} %broadcast_select_fusion), channel_id=1, source_target_pairs={{0,1},{1,2},{2,3},{3,0},{4,5},{5,6},{6,7},{7,4},{8,9},{9,10},{10,1... | collective-permute-start | bytes 12296 | tf_op jit(solution)/shard_map/ppermute | solution.py:466
  33.4 2.6 %collective-permute-start.12 = (f32[8,128]{1,0:T(8,128)S(1)}, f32[8,128]{1,0:T(8,128)S(1)}, u32[]{:S(2)}, u32[]{:S(2)}) collective-permute-start(f32[8,128]{1,0:T(8,128)S(1)} %broadcast_select_fusion), channel_id=1, source_target_pairs={{0,2},{1,3},{2,0},{3,1},{4,6},{5,7},{6,4},{7,5},{8,10},{9,11},{10,... | collective-permute-start | bytes 12296 | tf_op jit(solution)/shard_map/ppermute | solution.py:466
  36.0 1.3 %collective-permute-start.13 = (f32[8,128]{1,0:T(8,128)S(1)}, f32[8,128]{1,0:T(8,128)S(1)}, u32[]{:S(2)}, u32[]{:S(2)}) collective-permute-start(f32[8,128]{1,0:T(8,128)S(1)} %broadcast_select_fusion), channel_id=1, source_target_pairs={{0,3},{1,0},{2,1},{3,2},{4,7},{5,4},{6,5},{7,6},{8,11},{9,8},{10,9... | collective-permute-start | bytes 12296 | tf_op jit(solution)/shard_map/ppermute | solution.py:466
  37.4 5.1 %shard_map.71 = f32[264,128]{1,0:T(8,128)S(1)} custom-call(bf16[8,2,128,128]{3,2,1,0:T(8,128)(2,1)S(1)} %get-tuple-element.27.x_ref, bf16[8,2,128,128]{3,2,1,0:T(8,128)(2,1)S(1)} %get-tuple-element.19.kv_ref.refs_4_, f32[8,2,128,128]{3,2,1,0:T(8,128)S(1)} %get-tuple-element.28.teacher_ref, f32[4,64,128]{2,1,0:T(8,128)S(1)} %get-tuple-element.67.mq_ref, ...), custom_call_target="tpu_custom_call" | custom-call | flops 6710886400 | bytes 3145728 | tf_op jit(solution)/shard_map/pallas_call | solution.py:344
  42.6 0.0 collective-permute-done.11
  42.6 0.0 collective-permute-done.12
  42.6 0.0 collective-permute-done.13
  42.6 0.1 constant_dynamic-update-slice_fusion
  42.8 10.5 %all-gather.2 = f16[4352,128]{1,0:T(8,128)(2,1)S(1)} all-gather(f16[544,128]{1,0:T(8,128)(2,1)S(1)} %pad.4), channel_id=2, replica_groups=mesh['ctx'=8,'head'=4] {'ctx'}, dimensions={0}, use_global_device_ids=true | all-gather | bytes 1253376 | tf_op jit(solution)/shard_map/all_gather | solution.py:477
  53.3 0.2 slice.161
  53.5 0.3 fusion.16
  53.9 1.7 %fusion = (f32[32,128,64]{1,2,0:T(8,128)}, f32[32,128,64]{1,2,0:T(8,128)}) fusion(f16[8,4,1,64,128]{4,3,2,1,0:T(8,128)(2,1)S(1)} %get-tuple-element.32, f32[32,128]{1,0:T(8,128)S(1)} %broadcast_multiply_fusion, f16[8,4,1,64,128]{4,3,2,1,0:T(8,128)(2,1)S(1)} %get-tuple-element.33), kind=kLoop, calls=%fused_computation.1 | loop fusion | flops 1048576 | bytes 3162112 | tf_op jit(solution)/shard_map/transpose | solution.py:491
  (28 shorter events, 0.5 us)
Async XLA Ops:
  2.3 0.8 %copy-start = (bf16[128,2,128]{2,1,0:T(2,128)(2,1)S(1)}, bf16[128,2,128]{2,1,0:T(2,128)(2,1)}, u32[]{:S(2)}) copy-start(bf16[128,2,128]{2,1,0:T(2,128)(2,1)} %param.6) | copy-start | bytes 196612
  2.3 0.9 %copy-start.1 = (bf16[128,2,128]{2,1,0:T(2,128)(2,1)S(1)}, bf16[128,2,128]{2,1,0:T(2,128)(2,1)}, u32[]{:S(2)}) copy-start(bf16[128,2,128]{2,1,0:T(2,128)(2,1)} %param.7) | copy-start | bytes 196612
  2.4 10.7 %collective-permute-start = (bf16[4,4,128,128]{3,2,1,0:T(8,128)(2,1)S(1)}, bf16[4,4,128,128]{3,2,1,0:T(8,128)(2,1)S(1)}, u32[]{:S(2)}, u32[]{:S(2)}) collective-permute-start(bf16[4,4,128,128]{3,2,1,0:T(8,128)(2,1)S(1)} %dynamic-slice_bitcast_fusion), channel_id=1, source_target_pairs={{0,4},{4,0},{8,12},{12,8},{16,20},{20,16},{24,28},{28,24},{1,5},{5... | collective-permute-start | bytes 1572872 | tf_op jit(solution)/shard_map/ppermute | solution.py:395
  3.4 5.6 %collective-permute-start.4 = (bf16[2,128,128]{2,1,0:T(8,128)(2,1)S(1)}, bf16[2,128,128]{2,1,0:T(8,128)(2,1)S(1)}, u32[]{:S(2)}, u32[]{:S(2)}) collective-permute-start(bf16[2,128,128]{2,1,0:T(8,128)(2,1)S(1)} %get-tuple-element.51), channel_id=1, source_target_pairs={{0,8},{4,12},{8,0},{12,4},{16,24},{20,28},{24,16},{28,20},{1,9},{5... | collective-permute-start | bytes 196616 | tf_op jit(solution)/shard_map/ppermute | solution.py:390
  6.4 4.3 %collective-permute-start.5 = (bf16[2,128,128]{2,1,0:T(8,128)(2,1)S(1)}, bf16[2,128,128]{2,1,0:T(8,128)(2,1)S(1)}, u32[]{:S(2)}, u32[]{:S(2)}) collective-permute-start(bf16[2,128,128]{2,1,0:T(8,128)(2,1)S(1)} %get-tuple-element.52), channel_id=1, source_target_pairs={{0,16},{4,20},{8,24},{12,28},{16,0},{20,4},{24,8},{28,12},{1,17},{... | collective-permute-start | bytes 196616 | tf_op jit(solution)/shard_map/ppermute | solution.py:390
  7.9 5.2 %collective-permute-start.6 = (bf16[2,128,128]{2,1,0:T(8,128)(2,1)S(1)}, bf16[2,128,128]{2,1,0:T(8,128)(2,1)S(1)}, u32[]{:S(2)}, u32[]{:S(2)}) collective-permute-start(bf16[2,128,128]{2,1,0:T(8,128)(2,1)S(1)} %get-tuple-element.53), channel_id=1, source_target_pairs={{0,24},{4,28},{8,16},{12,20},{16,8},{20,12},{24,0},{28,4},{1,25},{... | collective-permute-start | bytes 196616 | tf_op jit(solution)/shard_map/ppermute | solution.py:390
  13.2 5.0 %collective-permute-start.1 = (bf16[2,2,128,128]{3,2,1,0:T(8,128)(2,1)S(1)}, bf16[2,2,128,128]{3,2,1,0:T(8,128)(2,1)S(1)}, u32[]{:S(2)}, u32[]{:S(2)}) collective-permute-start(bf16[2,2,128,128]{3,2,1,0:T(8,128)(2,1)S(1)} %pad_maximum_fusion.2), channel_id=1, source_target_pairs={{0,8},{4,12},{8,0},{12,4},{16,24},{20,28},{24,16},{28,20},{1,9},{5... | collective-permute-start | bytes 393224 | tf_op jit(solution)/shard_map/ppermute | solution.py:390
  13.8 6.8 %collective-permute-start.3 = (bf16[2,2,128,128]{3,2,1,0:T(8,128)(2,1)S(1)}, bf16[2,2,128,128]{3,2,1,0:T(8,128)(2,1)S(1)}, u32[]{:S(2)}, u32[]{:S(2)}) collective-permute-start(bf16[2,2,128,128]{3,2,1,0:T(8,128)(2,1)S(1)} %pad_maximum_fusion.4), channel_id=1, source_target_pairs={{0,24},{4,28},{8,16},{12,20},{16,8},{20,12},{24,0},{28,4},{1,25},{... | collective-permute-start | bytes 393224 | tf_op jit(solution)/shard_map/ppermute | solution.py:390
  15.3 6.6 %collective-permute-start.2 = (bf16[2,2,128,128]{3,2,1,0:T(8,128)(2,1)S(1)}, bf16[2,2,128,128]{3,2,1,0:T(8,128)(2,1)S(1)}, u32[]{:S(2)}, u32[]{:S(2)}) collective-permute-start(bf16[2,2,128,128]{3,2,1,0:T(8,128)(2,1)S(1)} %pad_maximum_fusion.3), channel_id=1, source_target_pairs={{0,16},{4,20},{8,24},{12,28},{16,0},{20,4},{24,8},{28,12},{1,17},{... | collective-permute-start | bytes 393224 | tf_op jit(solution)/shard_map/ppermute | solution.py:390
  18.2 3.7 %collective-permute-start.7 = (bf16[4,2,128,128]{3,2,1,0:T(8,128)(2,1)S(1)}, bf16[4,2,128,128]{3,2,1,0:T(8,128)(2,1)S(1)}, u32[]{:S(2)}, u32[]{:S(2)}) collective-permute-start(bf16[4,2,128,128]{3,2,1,0:T(8,128)(2,1)S(1)} %pad_maximum_fusion.refs_4_), channel_id=1, source_target_pairs={{0,4},{4,0},{8,12},{12,8},{16,20},{20,16},{24,28},{28,24},{1,5},{5... | collective-permute-start | bytes 786440 | tf_op jit(solution)/shard_map/ppermute | solution.py:395
  18.3 11.1 %collective-permute-start.10 = (bf16[2,2,128,128]{3,2,1,0:T(8,128)(2,1)S(1)}, bf16[2,2,128,128]{3,2,1,0:T(8,128)(2,1)S(1)}, u32[]{:S(2)}, u32[]{:S(2)}) collective-permute-start(bf16[2,2,128,128]{3,2,1,0:T(8,128)(2,1)S(1)} %get-tuple-element.25), channel_id=1, source_target_pairs={{0,24},{4,28},{8,16},{12,20},{16,8},{20,12},{24,0},{28,4},{1,25},{... | collective-permute-start | bytes 393224 | tf_op jit(solution)/shard_map/ppermute | solution.py:390
  19.7 9.8 %collective-permute-start.8 = (bf16[2,2,128,128]{3,2,1,0:T(8,128)(2,1)S(1)}, bf16[2,2,128,128]{3,2,1,0:T(8,128)(2,1)S(1)}, u32[]{:S(2)}, u32[]{:S(2)}) collective-permute-start(bf16[2,2,128,128]{3,2,1,0:T(8,128)(2,1)S(1)} %get-tuple-element.23), channel_id=1, source_target_pairs={{0,8},{4,12},{8,0},{12,4},{16,24},{20,28},{24,16},{28,20},{1,9},{5... | collective-permute-start | bytes 393224 | tf_op jit(solution)/shard_map/ppermute | solution.py:390
  20.7 8.8 %collective-permute-start.9 = (bf16[2,2,128,128]{3,2,1,0:T(8,128)(2,1)S(1)}, bf16[2,2,128,128]{3,2,1,0:T(8,128)(2,1)S(1)}, u32[]{:S(2)}, u32[]{:S(2)}) collective-permute-start(bf16[2,2,128,128]{3,2,1,0:T(8,128)(2,1)S(1)} %get-tuple-element.24), channel_id=1, source_target_pairs={{0,16},{4,20},{8,24},{12,28},{16,0},{20,4},{24,8},{28,12},{1,17},{... | collective-permute-start | bytes 393224 | tf_op jit(solution)/shard_map/ppermute | solution.py:390
  31.9 10.8 %collective-permute-start.11 = (f32[8,128]{1,0:T(8,128)S(1)}, f32[8,128]{1,0:T(8,128)S(1)}, u32[]{:S(2)}, u32[]{:S(2)}) collective-permute-start(f32[8,128]{1,0:T(8,128)S(1)} %broadcast_select_fusion), channel_id=1, source_target_pairs={{0,1},{1,2},{2,3},{3,0},{4,5},{5,6},{6,7},{7,4},{8,9},{9,10},{10,1... | collective-permute-start | bytes 12296 | tf_op jit(solution)/shard_map/ppermute | solution.py:466
  33.4 9.2 %collective-permute-start.12 = (f32[8,128]{1,0:T(8,128)S(1)}, f32[8,128]{1,0:T(8,128)S(1)}, u32[]{:S(2)}, u32[]{:S(2)}) collective-permute-start(f32[8,128]{1,0:T(8,128)S(1)} %broadcast_select_fusion), channel_id=1, source_target_pairs={{0,2},{1,3},{2,0},{3,1},{4,6},{5,7},{6,4},{7,5},{8,10},{9,11},{10,... | collective-permute-start | bytes 12296 | tf_op jit(solution)/shard_map/ppermute | solution.py:466
  36.0 6.6 %collective-permute-start.13 = (f32[8,128]{1,0:T(8,128)S(1)}, f32[8,128]{1,0:T(8,128)S(1)}, u32[]{:S(2)}, u32[]{:S(2)}) collective-permute-start(f32[8,128]{1,0:T(8,128)S(1)} %broadcast_select_fusion), channel_id=1, source_target_pairs={{0,3},{1,0},{2,1},{3,2},{4,7},{5,4},{6,5},{7,6},{8,11},{9,8},{10,9... | collective-permute-start | bytes 12296 | tf_op jit(solution)/shard_map/ppermute | solution.py:466

commit v4 on v3

--- a/solution.py
+++ b/solution.py
@@ -69,7 +69,7 @@
         base = source_of(place // cores, j) * cores
         for i in range(cores):
             block = base + (core if i == 0 else 1 - core)
-            x_ref[block] = piece[i]
+            x_ref[block] = piece[i * heads : (i + 1) * heads]
             if with_keys:
                 kv_ref[block] = keys[i][j]
 
@@ -126,8 +126,12 @@
 
         return lax.fori_loop(0, steps, one_row, energy)
 
-    body = one_head if steps <= 8 else one_long_head
-    energy = lax.fori_loop(0, heads, body, jnp.zeros((8, dim), F32))
+    energy = jnp.zeros((8, dim), F32)
+    if steps <= 8:
+        for h in range(heads):
+            energy = one_head(h, energy)
+    else:
+        energy = lax.fori_loop(0, heads, one_long_head, energy)
     energy = jnp.sum(jnp.sum(energy, axis=0, keepdims=True), axis=1, keepdims=True)
     energy = jnp.broadcast_to(energy, energy_ref.shape)
     energy_ref[...] = energy if with_keys else energy + before_ref[...]
@@ -138,8 +142,10 @@
 
 
 def teacher_call(place, pieces, kv, keys, before, places, source_of):
-    cores, heads, chunk, dim = pieces[0].shape
+    _, chunk, dim = pieces[0].shape
+    cores = len(keys)
     with_keys = kv is None
+    heads = pieces[0].shape[0] // cores
     rows = 2 * chunk if places % 2 == 0 else chunk
     steps = places * chunk // rows
     held = (steps, rows, rows) if steps > 8 else (1, 8, 128)
@@ -399,7 +405,8 @@
 
     by_head = jnp.pad(queries, ((0, 0), (0, padding), (0, 0))) if padding else queries
     by_head = by_head.transpose(1, 0, 2).reshape(chips, cores, heads, tokens, dim)
-    flat = [a.reshape(tokens, key_heads * dim) for a in (key_states, value_vector_states)]
+    *flat, by_head = lax.optimization_barrier((key_states, value_vector_states, by_head))
+    flat = [a.reshape(tokens, key_heads * dim) for a in flat]
     kv = jnp.stack(
         [jnp.stack([a[:, g * dim : (g + 1) * dim] for a in flat]) for g in range(key_heads)]
     )
@@ -410,21 +417,25 @@
     mine = [pick(by_head, core, 1)]
     if cores == 2:
         mine.append(swap(pick(by_head, 1 - core, 1)))
-    own_keys = [pick(kv, group_of(target_of(chip, j))) for j in range(chips)]
-    own_keys = [own_keys[0]] + [send(a, j) for j, a in enumerate(own_keys) if j]
-    keys = [jnp.stack(own_keys)]
+        kv = lax.optimization_barrier((kv, mine[1]))[0]
+    to_send = [pick(kv, group_of(target_of(chip, j))) for j in range(chips)]
     arrived = []
     for start, stop in parts:
         pieces = []
         for j in range(chips):
-            target = target_of(chip, j)
-            pieces.append(jnp.stack([pick(q, target)[start:stop] for q in mine]))
+            piece = [pick(q, target_of(chip, j))[start:stop] for q in mine]
+            if j == 1 and not arrived:
+                piece.append(to_send[j])
+            pieces.append(jnp.concatenate(piece))
         if arrived and chips > 1:
             pieces = lax.optimization_barrier((*pieces, arrived[-1][1]))[:chips]
         arrived.append([pieces[0]] + [send(a, j) for j, a in enumerate(pieces) if j])
-        if cores == 2 and len(keys) == 1:
-            ready = lax.optimization_barrier((keys[0], arrived[0][chips > 1]))[0]
-            keys.append(swap(ready))
+    own_keys = [send(a, j) if j > 1 else a for j, a in enumerate(to_send)]
+    if chips > 1:
+        own_keys[1] = arrived[0][1][-2:]
+    keys = [jnp.stack(own_keys)]
+    if cores == 2:
+        keys.append(swap(keys[0]))
     return arrived, keys, source_of
 
 

time: 55.8 us -> 54.5 us (0.977)
  waiting for transfers between devices: 5.41 us -> 3.85 us
    ppermute x9 -> x8, waiting for transfers between devices: 5.4 us -> 3.84 us  [send(): lax.ppermute(a, 'ctx', [(i, target_of(i // cores, j) * cores + i % cores)...]
    ppermute x9 -> x8, starting transfers between devices: 11.8 us -> 11.6 us  [send(): lax.ppermute(a, 'ctx', [(i, target_of(i // cores, j) * cores + i % cores)...]
  transfers between devices with their start and end apart: 14 -> 13, of which waited for: 3 -> 3; matrix products, arithmetic and copies ran while one was open for 3% -> 3% of each run, Pallas kernels for 23% -> 23%
where the time goes in v4:
time: 54.5 us; the launch traced here: 54.2 us
  starting transfers between devices  17.7 us (32%)
  Pallas kernels  14.9 us (27%)
  blocking collectives  10.9 us (20%)
  waiting for transfers between devices  3.85 us (7%)
  local copies, waits for them, and re-layouts  3.76 us (7%)
  other arithmetic  2.05 us (4%)
  between operations  1.13 us (2%)
    ppermute x8, starting transfers between devices, send(): lax.ppermute(a, 'ctx', [(i, target_of(i // cores, j) * cores + i % cores)...  11.6 us
    all_gather x1, blocking collectives, on_device(): gathered = lax.all_gather(jnp.pad(sent, ((0, -used % 16), (0, 0))), 'ctx')  10.9 us
    pallas_call x2, Pallas kernels, student_call(): pl.pallas_call(functools.partial(student_kernel, start, heads), in_specs=...  10.4 us
    ppermute x3, starting transfers between devices, on_device(): lax.ppermute(energy, 'head', [(i, (i + k) % planes) for i in range(planes)])  5.52 us
    pallas_call x2, Pallas kernels, teacher_call(): pl.pallas_call(functools.partial(teacher_kernel, (places, cores, heads, w...  4.44 us
    ppermute x8, waiting for transfers between devices, send(): lax.ppermute(a, 'ctx', [(i, target_of(i // cores, j) * cores + i % cores)...  3.84 us
    transpose x1, local copies, waits for them, and re-layouts, exchange(): by_head.transpose(1, 0, 2).reshape(chips, cores, heads, tokens, dim)  1.66 us
    transpose x1, other arithmetic, unpacked(): return part[:query_heads].transpose(0, 2, 1)  1.66 us
  transfers between devices with their start and end apart: 13, of which 3 were waited for; matrix products, arithmetic and copies ran while one was open for 3% of the time, Pallas kernels for 23%

profile of v4, /device:TPU:0, one launch (start us, length us, event | category | flops | bytes accessed | tf_op | source)
XLA Modules:
  0.0 54.2 jit_solution(813556760663030884)
XLA Ops:
  0.6 0.0 copy-start
  0.7 1.7 %copy.7 = bf16[32,128,128]{2,1,0:T(8,128)(2,1)S(1)} copy(bf16[32,128,128]{2,0,1:T(8,128)(2,1)} %bitcast.98) | data formatting | bytes 2097152 | tf_op jit(solution)/shard_map/transpose | solution.py:407
  2.3 0.0 copy-start.1
  2.4 0.5 collective-permute-start
  2.9 0.0 copy-done
  2.9 0.2 copy-done.1
  3.4 1.0 %dynamic-slice_bitcast_fusion.1 = (f32[4,64,128]{2,1,0:T(8,128)S(1)}, f32[4,64,128]{2,1,0:T(8,128)S(1)}) fusion(f32[32,128,64]{1,2,0:T(8,128)} %param.9, s32[]{:T(128)S(6)} %select_n.118, f32[32,128,64]{1,2,0:T(8,128)} %param.8), kind=kLoop, calls=%fused_computation.15 | loop fusion | bytes 524292 | tf_op jit(solution)/shard_map/dynamic_slice | solution.py:459
  4.4 0.1 dynamic-slice_bitcast_fusion.4
  4.5 0.0 collective-permute-done
  4.5 0.1 dynamic-slice_bitcast_fusion.3
  4.6 3.0 %collective-permute-start.1 = (bf16[6,128,128]{2,1,0:T(8,128)(2,1)S(1)}, bf16[6,128,128]{2,1,0:T(8,128)(2,1)S(1)}, u32[]{:S(2)}, u32[]{:S(2)}) collective-permute-start(bf16[6,128,128]{2,1,0:T(8,128)(2,1)S(1)} %pad_maximum_fusion.1), channel_id=1, source_target_pairs={{0,8},{4,12},{8,0},{12,4},{16,24},{20,28},{24,16},{28,20},{1,9},{5... | collective-permute-start | bytes 589832 | tf_op jit(solution)/shard_map/ppermute | solution.py:396
  7.6 1.5 %collective-permute-start.4 = (bf16[2,128,128]{2,1,0:T(8,128)(2,1)S(1)}, bf16[2,128,128]{2,1,0:T(8,128)(2,1)S(1)}, u32[]{:S(2)}, u32[]{:S(2)}) collective-permute-start(bf16[2,128,128]{2,1,0:T(8,128)(2,1)S(1)} %get-tuple-element.58), channel_id=1, source_target_pairs={{0,16},{4,20},{8,24},{12,28},{16,0},{20,4},{24,8},{28,12},{1,17},{... | collective-permute-start | bytes 196616 | tf_op jit(solution)/shard_map/ppermute | solution.py:396
  9.1 0.0 collective-permute-start.5
  9.2 3.0 %collective-permute-start.3 = (bf16[4,128,128]{2,1,0:T(8,128)(2,1)S(1)}, bf16[4,128,128]{2,1,0:T(8,128)(2,1)S(1)}, u32[]{:S(2)}, u32[]{:S(2)}) collective-permute-start(bf16[4,128,128]{2,1,0:T(8,128)(2,1)S(1)} %pad_maximum_fusion.5), channel_id=1, source_target_pairs={{0,24},{4,28},{8,16},{12,20},{16,8},{20,12},{24,0},{28,4},{1,25},{... | collective-permute-start | bytes 393224 | tf_op jit(solution)/shard_map/ppermute | solution.py:396
  12.2 0.6 %collective-permute-start.2 = (bf16[4,128,128]{2,1,0:T(8,128)(2,1)S(1)}, bf16[4,128,128]{2,1,0:T(8,128)(2,1)S(1)}, u32[]{:S(2)}, u32[]{:S(2)}) collective-permute-start(bf16[4,128,128]{2,1,0:T(8,128)(2,1)S(1)} %pad_maximum_fusion.4), channel_id=1, source_target_pairs={{0,16},{4,20},{8,24},{12,28},{16,0},{20,4},{24,8},{28,12},{1,17},{... | collective-permute-start | bytes 393224 | tf_op jit(solution)/shard_map/ppermute | solution.py:396
  12.7 0.6 %collective-permute-done.1.refs_1_ = bf16[6,128,128]{2,1,0:T(8,128)(2,1)S(1)} collective-permute-done((bf16[6,128,128]{2,1,0:T(8,128)(2,1)S(1)}, bf16[6,128,128]{2,1,0:T(8,128)(2,1)S(1)}, u32[]{:S(2)}, u32[]{:S(2)}) %collective-permute-start.1) | collective-permute-done | bytes 196640 | tf_op jit(solution)/shard_map/ppermute | solution.py:396
  13.3 0.0 collective-permute-done.4
  13.3 3.0 %collective-permute-done.5 = bf16[2,128,128]{2,1,0:T(8,128)(2,1)S(1)} collective-permute-done((bf16[2,128,128]{2,1,0:T(8,128)(2,1)S(1)}, bf16[2,128,128]{2,1,0:T(8,128)(2,1)S(1)}, u32[]{:S(2)}, u32[]{:S(2)}) %collective-permute-start.5) | collective-permute-done | bytes 65568 | tf_op jit(solution)/shard_map/ppermute | solution.py:396
  16.4 0.1 collective-permute-start.6
  16.6 1.6 %collective-permute-start.7 = (bf16[4,128,128]{2,1,0:T(8,128)(2,1)S(1)}, bf16[4,128,128]{2,1,0:T(8,128)(2,1)S(1)}, u32[]{:S(2)}, u32[]{:S(2)}) collective-permute-start(bf16[4,128,128]{2,1,0:T(8,128)(2,1)S(1)} %get-tuple-element.29), channel_id=1, source_target_pairs={{0,8},{4,12},{8,0},{12,4},{16,24},{20,28},{24,16},{28,20},{1,9},{5... | collective-permute-start | bytes 393224 | tf_op jit(solution)/shard_map/ppermute | solution.py:396
  18.1 0.5 collective-permute-start.8
  18.6 0.0 collective-permute-done.3.refs_3_
  18.6 1.5 %collective-permute-start.9 = (bf16[4,128,128]{2,1,0:T(8,128)(2,1)S(1)}, bf16[4,128,128]{2,1,0:T(8,128)(2,1)S(1)}, u32[]{:S(2)}, u32[]{:S(2)}) collective-permute-start(bf16[4,128,128]{2,1,0:T(8,128)(2,1)S(1)} %get-tuple-element.31), channel_id=1, source_target_pairs={{0,24},{4,28},{8,16},{12,20},{16,8},{20,12},{24,0},{28,4},{1,25},{... | collective-permute-start | bytes 393224 | tf_op jit(solution)/shard_map/ppermute | solution.py:396
  20.1 0.2 collective-permute-done.2.refs_2_
  20.3 0.0 collective-permute-done.6.refs_5_
  20.3 2.2 %shard_map.68 = (bf16[8,2,128,128]{3,2,1,0:T(8,128)(2,1)S(1)}, bf16[8,2,128,128]{3,2,1,0:T(8,128)(2,1)S(1)}, f32[8,2,128,128]{3,2,1,0:T(8,128)S(1)}, f32[8,128]{1,0:T(8,128)S(1)}) custom-call(s32[1]{0:T(128)} %bitcast.place_ref, bf16[4,128,128]{2,1,0:T(8,128)(2,1)S(1)} %pad_maximum_fusion.2.refs_0_, bf16[6,128,128]{2,1,0:T(8,128)(2,1)S(1)} %collective-permute-done.1.refs_1_, ...), custom_call_target="tpu_custom_call" | custom-call | flops 2684354560 | bytes 2097152 | tf_op jit(solution)/shard_map/pallas_call | solution.py:155
  22.6 5.2 %shard_map.69 = f32[264,128]{1,0:T(8,128)S(1)} custom-call(bf16[8,2,128,128]{3,2,1,0:T(8,128)(2,1)S(1)} %get-tuple-element.24.x_ref, bf16[8,2,128,128]{3,2,1,0:T(8,128)(2,1)S(1)} %get-tuple-element.25.kv_ref.refs_4_, f32[8,2,128,128]{3,2,1,0:T(8,128)S(1)} %get-tuple-element.26.teacher_ref, f32[4,64,128]{2,1,0:T(8,128)S(1)} %get-tuple-element.73.mq_ref, ...), custom_call_target="tpu_custom_call" | custom-call | flops 6710886400 | bytes 3145728 | tf_op jit(solution)/shard_map/pallas_call | solution.py:350
  27.8 0.0 collective-permute-done.7.refs_1_
  27.8 0.0 collective-permute-done.8.refs_2_
  27.8 0.0 collective-permute-done.9.refs_3_
  27.8 2.2 %shard_map.70 = (bf16[8,2,128,128]{3,2,1,0:T(8,128)(2,1)S(1)}, f32[8,2,128,128]{3,2,1,0:T(8,128)S(1)}, f32[8,128]{1,0:T(8,128)S(1)}) custom-call(s32[1]{0:T(128)} %bitcast.place_ref, bf16[4,128,128]{2,1,0:T(8,128)(2,1)S(1)} %get-tuple-element.28.refs_0_, bf16[4,128,128]{2,1,0:T(8,128)(2,1)S(1)} %collective-permute-done.7.refs_1_, ...), custom_call_target="tpu_custom_call" | custom-call | flops 2684354560 | bytes 2097152 | tf_op jit(solution)/shard_map/pallas_call | solution.py:155
  30.1 1.6 %collective-permute-start.10 = (f32[8,128]{1,0:T(8,128)S(1)}, f32[8,128]{1,0:T(8,128)S(1)}, u32[]{:S(2)}, u32[]{:S(2)}) collective-permute-start(f32[8,128]{1,0:T(8,128)S(1)} %broadcast_select_fusion), channel_id=1, source_target_pairs={{0,1},{1,2},{2,3},{3,0},{4,5},{5,6},{6,7},{7,4},{8,9},{9,10},{10,1... | collective-permute-start | bytes 12296 | tf_op jit(solution)/shard_map/ppermute | solution.py:477
  31.6 2.6 %collective-permute-start.11 = (f32[8,128]{1,0:T(8,128)S(1)}, f32[8,128]{1,0:T(8,128)S(1)}, u32[]{:S(2)}, u32[]{:S(2)}) collective-permute-start(f32[8,128]{1,0:T(8,128)S(1)} %broadcast_select_fusion), channel_id=1, source_target_pairs={{0,2},{1,3},{2,0},{3,1},{4,6},{5,7},{6,4},{7,5},{8,10},{9,11},{10,... | collective-permute-start | bytes 12296 | tf_op jit(solution)/shard_map/ppermute | solution.py:477
  34.2 1.4 %collective-permute-start.12 = (f32[8,128]{1,0:T(8,128)S(1)}, f32[8,128]{1,0:T(8,128)S(1)}, u32[]{:S(2)}, u32[]{:S(2)}) collective-permute-start(f32[8,128]{1,0:T(8,128)S(1)} %broadcast_select_fusion), channel_id=1, source_target_pairs={{0,3},{1,0},{2,1},{3,2},{4,7},{5,4},{6,5},{7,6},{8,11},{9,8},{10,9... | collective-permute-start | bytes 12296 | tf_op jit(solution)/shard_map/ppermute | solution.py:477
  35.6 5.2 %shard_map.71 = f32[264,128]{1,0:T(8,128)S(1)} custom-call(bf16[8,2,128,128]{3,2,1,0:T(8,128)(2,1)S(1)} %get-tuple-element.33.x_ref, bf16[8,2,128,128]{3,2,1,0:T(8,128)(2,1)S(1)} %get-tuple-element.25.kv_ref.refs_4_, f32[8,2,128,128]{3,2,1,0:T(8,128)S(1)} %get-tuple-element.34.teacher_ref, f32[4,64,128]{2,1,0:T(8,128)S(1)} %get-tuple-element.73.mq_ref, ...), custom_call_target="tpu_custom_call" | custom-call | flops 6710886400 | bytes 3145728 | tf_op jit(solution)/shard_map/pallas_call | solution.py:350
  40.9 0.0 collective-permute-done.10
  40.9 0.0 collective-permute-done.11
  40.9 0.0 collective-permute-done.12
  40.9 0.1 constant_dynamic-update-slice_fusion
  41.1 10.9 %all-gather.2 = f16[4352,128]{1,0:T(8,128)(2,1)S(1)} all-gather(f16[544,128]{1,0:T(8,128)(2,1)S(1)} %pad.4), channel_id=2, replica_groups=mesh['ctx'=8,'head'=4] {'ctx'}, dimensions={0}, use_global_device_ids=true | all-gather | bytes 1253376 | tf_op jit(solution)/shard_map/all_gather | solution.py:488
  51.9 0.2 slice.214
  52.2 0.3 fusion.9
  52.6 1.7 %fusion = (f32[32,128,64]{1,2,0:T(8,128)}, f32[32,128,64]{1,2,0:T(8,128)}) fusion(f16[8,4,1,64,128]{4,3,2,1,0:T(8,128)(2,1)S(1)} %get-tuple-element.38, f32[32,128]{1,0:T(8,128)S(1)} %broadcast_multiply_fusion, f16[8,4,1,64,128]{4,3,2,1,0:T(8,128)(2,1)S(1)} %get-tuple-element.39), kind=kLoop, calls=%fused_computation.1 | loop fusion | flops 1048576 | bytes 3162112 | tf_op jit(solution)/shard_map/transpose | solution.py:502
  (31 shorter events, 0.5 us)
Async XLA Ops:
  0.6 2.3 %copy-start = (bf16[128,2,128]{2,1,0:T(2,128)(2,1)S(1)}, bf16[128,2,128]{2,1,0:T(2,128)(2,1)}, u32[]{:S(2)}) copy-start(bf16[128,2,128]{2,1,0:T(2,128)(2,1)} %param.6) | copy-start | bytes 196612
  2.3 0.8 %copy-start.1 = (bf16[128,2,128]{2,1,0:T(2,128)(2,1)S(1)}, bf16[128,2,128]{2,1,0:T(2,128)(2,1)}, u32[]{:S(2)}) copy-start(bf16[128,2,128]{2,1,0:T(2,128)(2,1)} %param.7) | copy-start | bytes 196612
  2.4 2.1 %collective-permute-start = (bf16[4,4,128,128]{3,2,1,0:T(8,128)(2,1)S(1)}, bf16[4,4,128,128]{3,2,1,0:T(8,128)(2,1)S(1)}, u32[]{:S(2)}, u32[]{:S(2)}) collective-permute-start(bf16[4,4,128,128]{3,2,1,0:T(8,128)(2,1)S(1)} %dynamic-slice_bitcast_fusion), channel_id=1, source_target_pairs={{0,4},{4,0},{8,12},{12,8},{16,20},{20,16},{24,28},{28,24},{1,5},{5... | collective-permute-start | bytes 1572872 | tf_op jit(solution)/shard_map/ppermute | solution.py:401
  4.6 8.7 %collective-permute-start.1 = (bf16[6,128,128]{2,1,0:T(8,128)(2,1)S(1)}, bf16[6,128,128]{2,1,0:T(8,128)(2,1)S(1)}, u32[]{:S(2)}, u32[]{:S(2)}) collective-permute-start(bf16[6,128,128]{2,1,0:T(8,128)(2,1)S(1)} %pad_maximum_fusion.1), channel_id=1, source_target_pairs={{0,8},{4,12},{8,0},{12,4},{16,24},{20,28},{24,16},{28,20},{1,9},{5... | collective-permute-start | bytes 589832 | tf_op jit(solution)/shard_map/ppermute | solution.py:396
  7.6 5.7 %collective-permute-start.4 = (bf16[2,128,128]{2,1,0:T(8,128)(2,1)S(1)}, bf16[2,128,128]{2,1,0:T(8,128)(2,1)S(1)}, u32[]{:S(2)}, u32[]{:S(2)}) collective-permute-start(bf16[2,128,128]{2,1,0:T(8,128)(2,1)S(1)} %get-tuple-element.58), channel_id=1, source_target_pairs={{0,16},{4,20},{8,24},{12,28},{16,0},{20,4},{24,8},{28,12},{1,17},{... | collective-permute-start | bytes 196616 | tf_op jit(solution)/shard_map/ppermute | solution.py:396
  9.1 7.2 %collective-permute-start.5 = (bf16[2,128,128]{2,1,0:T(8,128)(2,1)S(1)}, bf16[2,128,128]{2,1,0:T(8,128)(2,1)S(1)}, u32[]{:S(2)}, u32[]{:S(2)}) collective-permute-start(bf16[2,128,128]{2,1,0:T(8,128)(2,1)S(1)} %get-tuple-element.57), channel_id=1, source_target_pairs={{0,24},{4,28},{8,16},{12,20},{16,8},{20,12},{24,0},{28,4},{1,25},{... | collective-permute-start | bytes 196616 | tf_op jit(solution)/shard_map/ppermute | solution.py:396
  9.2 9.5 %collective-permute-start.3 = (bf16[4,128,128]{2,1,0:T(8,128)(2,1)S(1)}, bf16[4,128,128]{2,1,0:T(8,128)(2,1)S(1)}, u32[]{:S(2)}, u32[]{:S(2)}) collective-permute-start(bf16[4,128,128]{2,1,0:T(8,128)(2,1)S(1)} %pad_maximum_fusion.5), channel_id=1, source_target_pairs={{0,24},{4,28},{8,16},{12,20},{16,8},{20,12},{24,0},{28,4},{1,25},{... | collective-permute-start | bytes 393224 | tf_op jit(solution)/shard_map/ppermute | solution.py:396
  12.2 8.2 %collective-permute-start.2 = (bf16[4,128,128]{2,1,0:T(8,128)(2,1)S(1)}, bf16[4,128,128]{2,1,0:T(8,128)(2,1)S(1)}, u32[]{:S(2)}, u32[]{:S(2)}) collective-permute-start(bf16[4,128,128]{2,1,0:T(8,128)(2,1)S(1)} %pad_maximum_fusion.4), channel_id=1, source_target_pairs={{0,16},{4,20},{8,24},{12,28},{16,0},{20,4},{24,8},{28,12},{1,17},{... | collective-permute-start | bytes 393224 | tf_op jit(solution)/shard_map/ppermute | solution.py:396
  16.4 3.9 %collective-permute-start.6 = (bf16[4,2,128,128]{3,2,1,0:T(8,128)(2,1)S(1)}, bf16[4,2,128,128]{3,2,1,0:T(8,128)(2,1)S(1)}, u32[]{:S(2)}, u32[]{:S(2)}) collective-permute-start(bf16[4,2,128,128]{3,2,1,0:T(8,128)(2,1)S(1)} %pad_maximum_fusion.refs_4_), channel_id=1, source_target_pairs={{0,4},{4,0},{8,12},{12,8},{16,20},{20,16},{24,28},{28,24},{1,5},{5... | collective-permute-start | bytes 786440 | tf_op jit(solution)/shard_map/ppermute | solution.py:401
  16.6 11.2 %collective-permute-start.7 = (bf16[4,128,128]{2,1,0:T(8,128)(2,1)S(1)}, bf16[4,128,128]{2,1,0:T(8,128)(2,1)S(1)}, u32[]{:S(2)}, u32[]{:S(2)}) collective-permute-start(bf16[4,128,128]{2,1,0:T(8,128)(2,1)S(1)} %get-tuple-element.29), channel_id=1, source_target_pairs={{0,8},{4,12},{8,0},{12,4},{16,24},{20,28},{24,16},{28,20},{1,9},{5... | collective-permute-start | bytes 393224 | tf_op jit(solution)/shard_map/ppermute | solution.py:396
  18.1 9.7 %collective-permute-start.8 = (bf16[4,128,128]{2,1,0:T(8,128)(2,1)S(1)}, bf16[4,128,128]{2,1,0:T(8,128)(2,1)S(1)}, u32[]{:S(2)}, u32[]{:S(2)}) collective-permute-start(bf16[4,128,128]{2,1,0:T(8,128)(2,1)S(1)} %get-tuple-element.30), channel_id=1, source_target_pairs={{0,16},{4,20},{8,24},{12,28},{16,0},{20,4},{24,8},{28,12},{1,17},{... | collective-permute-start | bytes 393224 | tf_op jit(solution)/shard_map/ppermute | solution.py:396
  18.6 9.2 %collective-permute-start.9 = (bf16[4,128,128]{2,1,0:T(8,128)(2,1)S(1)}, bf16[4,128,128]{2,1,0:T(8,128)(2,1)S(1)}, u32[]{:S(2)}, u32[]{:S(2)}) collective-permute-start(bf16[4,128,128]{2,1,0:T(8,128)(2,1)S(1)} %get-tuple-element.31), channel_id=1, source_target_pairs={{0,24},{4,28},{8,16},{12,20},{16,8},{20,12},{24,0},{28,4},{1,25},{... | collective-permute-start | bytes 393224 | tf_op jit(solution)/shard_map/ppermute | solution.py:396
  30.1 10.9 %collective-permute-start.10 = (f32[8,128]{1,0:T(8,128)S(1)}, f32[8,128]{1,0:T(8,128)S(1)}, u32[]{:S(2)}, u32[]{:S(2)}) collective-permute-start(f32[8,128]{1,0:T(8,128)S(1)} %broadcast_select_fusion), channel_id=1, source_target_pairs={{0,1},{1,2},{2,3},{3,0},{4,5},{5,6},{6,7},{7,4},{8,9},{9,10},{10,1... | collective-permute-start | bytes 12296 | tf_op jit(solution)/shard_map/ppermute | solution.py:477
  31.6 9.3 %collective-permute-start.11 = (f32[8,128]{1,0:T(8,128)S(1)}, f32[8,128]{1,0:T(8,128)S(1)}, u32[]{:S(2)}, u32[]{:S(2)}) collective-permute-start(f32[8,128]{1,0:T(8,128)S(1)} %broadcast_select_fusion), channel_id=1, source_target_pairs={{0,2},{1,3},{2,0},{3,1},{4,6},{5,7},{6,4},{7,5},{8,10},{9,11},{10,... | collective-permute-start | bytes 12296 | tf_op jit(solution)/shard_map/ppermute | solution.py:477
  34.2 6.7 %collective-permute-start.12 = (f32[8,128]{1,0:T(8,128)S(1)}, f32[8,128]{1,0:T(8,128)S(1)}, u32[]{:S(2)}, u32[]{:S(2)}) collective-permute-start(f32[8,128]{1,0:T(8,128)S(1)} %broadcast_select_fusion), channel_id=1, source_target_pairs={{0,3},{1,0},{2,1},{3,2},{4,7},{5,4},{6,5},{7,6},{8,11},{9,8},{10,9... | collective-permute-start | bytes 12296 | tf_op jit(solution)/shard_map/ppermute | solution.py:477

commit v5 on v4

--- a/solution.py
+++ b/solution.py
@@ -329,17 +329,37 @@
     lax.fori_loop(0, blocks // per, gradients, 0)
     grad_ref[pl.ds(heads * both, spare), :] = jnp.zeros((spare, dim), F32)
     for h in range(heads):
-        base = h * both
-        parts = [
-            total[pl.ds(base, features), :] - total[pl.ds(base + features, features), :]
-            for total in (sum_q_ref, sum_k_ref)
-        ]
-        grads = below(*parts)
-        top = jnp.max(jnp.abs(grads), axis=0, keepdims=True)
-        top = jnp.max(top, axis=1, keepdims=True)
-        power = power_of(top)
-        grad_ref[at[h], :] = grads * jnp.exp2(-power)
+        parts = []
+        for total in (sum_q_ref, sum_k_ref):
+            both_signs = total[at[h], :]
+            parts.append(both_signs[:features] - both_signs[features:])
+        top = jnp.max(jnp.abs(below(*parts)), axis=0, keepdims=True)
+        power = power_of(jnp.max(top, axis=1, keepdims=True))
+        for i, part in enumerate(parts):
+            rows = pl.ds((i * heads + h) * features, features)
+            grad_ref[rows, :] = part * jnp.exp2(-power)
         grad_ref[pl.ds(heads * both + h, 1), :] = jnp.broadcast_to(power, (1, dim))
+
+
+def student_scratch(blocks, rows, chunk, dim):
+    return [
+        pltpu.VMEM((rows, 2 * dim), BF16),
+        pltpu.VMEM((rows, 2 * dim), BF16),
+        pltpu.VMEM((blocks, rows, 2 * chunk), BF16),
+        pltpu.VMEM((blocks, rows, 2 * chunk), BF16),
+        pltpu.VMEM((blocks, rows, 2 * chunk), BF16),
+        pltpu.VMEM((blocks, rows, 4 * dim), BF16),
+        pltpu.VMEM((blocks, rows, dim), F32),
+        pltpu.VMEM((rows, 2 * dim), F32),
+        pltpu.VMEM((rows, chunk), F32),
+        pltpu.VMEM((rows, dim), F32),
+        pltpu.VMEM((rows, dim), F32),
+        pltpu.VMEM((rows, dim), F32),
+    ]
+
+
+def student_shape(heads, rows, dim):
+    return jax.ShapeDtypeStruct((rows + (heads + 7) // 8 * 8, dim), F32)
 
 
 def student_call(start, x, kv, teacher, map_query, map_key):
@@ -351,28 +371,71 @@
         functools.partial(student_kernel, start, heads),
         in_specs=[whole] * 5,
         out_specs=whole,
-        out_shape=jax.ShapeDtypeStruct((rows + (heads + 7) // 8 * 8, dim), F32),
-        scratch_shapes=[
-            pltpu.VMEM((rows, 2 * dim), BF16),
-            pltpu.VMEM((rows, 2 * dim), BF16),
-            pltpu.VMEM((blocks, rows, 2 * chunk), BF16),
-            pltpu.VMEM((blocks, rows, 2 * chunk), BF16),
-            pltpu.VMEM((blocks, rows, 2 * chunk), BF16),
-            pltpu.VMEM((blocks, rows, 4 * dim), BF16),
-            pltpu.VMEM((blocks, rows, dim), F32),
-            pltpu.VMEM((rows, 2 * dim), F32),
-            pltpu.VMEM((rows, chunk), F32),
-            pltpu.VMEM((rows, dim), F32),
-            pltpu.VMEM((rows, dim), F32),
-            pltpu.VMEM((rows, dim), F32),
-        ],
+        out_shape=student_shape(heads, rows, dim),
+        scratch_shapes=student_scratch(blocks, rows, chunk, dim),
         compiler_params=pltpu.CompilerParams(vmem_limit_bytes=VMEM_LIMIT),
         cost_estimate=pl.CostEstimate(
             flops=200 * rows * blocks * chunk * dim,
             bytes_accessed=12 * heads * blocks * chunk * dim,
             transcendentals=3 * rows * blocks * chunk,
         ),
-    )(in_vmem(x), in_vmem(kv), in_vmem(teacher), map_query, map_key)
+    )(*[in_vmem(a) for a in (x, kv, teacher, map_query, map_key)])
+
+
+def partner(at, step, count):
+    return at ^ step if count & (count - 1) == 0 else (at + step) % count
+
+
+def both_kernel(shape, rows, scale, source_of, start, place_ref, *refs):
+    places, cores, heads, _ = shape
+    count = places // cores + cores
+    arrived, (mq_ref, mk_ref), refs = refs[:count], refs[count : count + 2], refs[count + 2 :]
+    kv_ref, energy_ref, grad_ref, x_ref, out_ref, scores_ref, *scratch = refs
+    teacher_kernel(
+        shape, rows, scale, source_of, place_ref, *arrived, x_ref, kv_ref, out_ref, energy_ref, scores_ref
+    )
+    student_kernel(start, heads, x_ref, kv_ref, out_ref, mq_ref, mk_ref, grad_ref, *scratch)
+
+
+def both_call(start, place, pieces, keys, map_query, map_key, places, source_of):
+    _, chunk, dim = pieces[0].shape
+    cores = len(keys)
+    heads = pieces[0].shape[0] // cores
+    rows = 2 * chunk if places % 2 == 0 else chunk
+    steps = places * chunk // rows
+    held = (steps, rows, rows) if steps > 8 else (1, 8, 128)
+    both = heads * 2 * map_query.shape[1]
+    whole = pl.BlockSpec(memory_space=pltpu.VMEM)
+    operands = [in_vmem(a) for a in pieces + keys + [map_query, map_key]]
+    return pl.pallas_call(
+        functools.partial(
+            both_kernel,
+            (places, cores, heads, True),
+            rows,
+            1.0 / math.sqrt(dim),
+            source_of,
+            start,
+        ),
+        in_specs=[pl.BlockSpec(memory_space=pltpu.SMEM)] + [whole] * len(operands),
+        out_specs=[whole] * 3,
+        out_shape=[
+            pltpu.VMEM((places, 2, chunk, dim), BF16),
+            jax.ShapeDtypeStruct((8, dim), F32),
+            student_shape(heads, both, dim),
+        ],
+        scratch_shapes=[
+            pltpu.VMEM((places, heads, chunk, dim), BF16),
+            pltpu.VMEM((places, heads, chunk, dim), F32),
+            pltpu.VMEM(held, F32),
+        ]
+        + student_scratch(places, both, chunk, dim),
+        compiler_params=pltpu.CompilerParams(vmem_limit_bytes=VMEM_LIMIT),
+        cost_estimate=pl.CostEstimate(
+            flops=200 * both * places * chunk * dim + 10 * heads * (places * chunk) ** 2 * dim,
+            bytes_accessed=20 * heads * places * chunk * dim,
+            transcendentals=heads * (places * chunk) ** 2 // 2,
+        ),
+    )(place, *operands)
 
 
 def exchange(queries, key_states, value_vector_states, heads, parts):
@@ -387,7 +450,7 @@
     mirrored = chips & (chips - 1) == 0
 
     def target_of(at, j):
-        return at ^ j if mirrored else (at + j) % chips
+        return partner(at, j, chips)
 
     def source_of(at, j):
         return at ^ j if mirrored else (at + chips - j) % chips
@@ -462,19 +525,22 @@
     position = place.astype(jnp.int32).reshape(1)
     kv, energy, grads, powers = None, None, [], []
     for (start, stop), pieces in zip(parts, arrived):
-        x, *found = teacher_call(position, pieces, kv, keys, energy, places, source_of)
-        if kv is None:
-            kv = found.pop(0)
-        teacher, energy = found
-        rows = (stop - start) * 2 * features
-        result = student_call(start, x, kv, teacher, own_query, own_key)
         if stop < heads:
-            energy, result = lax.optimization_barrier((energy, result))
-        grads.append(result[:rows])
-        powers.append(result[rows:])
+            kv, energy, result = both_call(
+                start, position, pieces, keys, own_query, own_key, places, source_of
+            )
+        else:
+            x, *found = teacher_call(position, pieces, kv, keys, energy, places, source_of)
+            if kv is None:
+                kv = found.pop(0)
+            teacher, energy = found
+            result = student_call(start, x, kv, teacher, own_query, own_key)
+        rows = (stop - start) * features
+        grads.append((result[:rows], result[rows : 2 * rows]))
+        powers.append(result[2 * rows :])
     energy = jnp.where(place * heads < query_heads, energy, 0.0)
     shifted = [
-        lax.ppermute(energy, "head", [(i, (i + k) % planes) for i in range(planes)])
+        lax.ppermute(energy, "head", [(i, partner(i, k, planes)) for i in range(planes)])
         for k in range(1, planes)
     ]
     energy = sum(shifted, energy)
@@ -483,6 +549,7 @@
     first = lax.reduce_precision(near_one, 5, 10)
     row = lax.broadcasted_iota(jnp.int32, energy.shape, 0)
     tail = jnp.where(row == 0, power, jnp.where(row == 1, first, (near_one - first) * 1024.0))
+    grads = [part for side in zip(*grads) for part in side]
     sent = jnp.concatenate(grads + powers + [tail]).astype(F16)
     used = sent.shape[0]
     gathered = lax.all_gather(jnp.pad(sent, ((0, -used % 16), (0, 0))), "ctx")
@@ -497,8 +564,9 @@
     factor = (jnp.exp2(power) * (2.0 * query_heads * planes / energy))[:, :, None]
 
     def unpacked(i):
-        part = gathered[:, :rows].reshape(places, heads, 2, features, dim)[:, :, i]
-        part = (part.astype(F32) * factor).reshape(places * heads, features, dim)
+        part = gathered[:, i * rows // 2 : (i + 1) * rows // 2].astype(F32)
+        part = part.reshape(places, heads, features, dim) * factor
+        part = part.reshape(places * heads, features, dim)
         return part[:query_heads].transpose(0, 2, 1)
 
     return (unpacked(0), unpacked(1))

time: 54.5 us -> 52.7 us (0.967)
  starting transfers between devices: 17.7 us -> 16.5 us
  Pallas kernels: 14.9 us -> 14.3 us
    pallas_call x0 -> x1, Pallas kernels: none -> 6.85 us  [both_call(): pl.pallas_call(functools.partial(both_kernel, (places, cores, heads, True...]
    pallas_call x2 -> x1, Pallas kernels: 10.4 us -> 5.31 us  [student_call(): pl.pallas_call(functools.partial(student_kernel, start, heads), in_specs=...]
    pallas_call x2 -> x1, Pallas kernels: 4.44 us -> 2.15 us  [teacher_call(): pl.pallas_call(functools.partial(teacher_kernel, (places, cores, heads, w...]
    ppermute x3, starting transfers between devices: 5.52 us -> 4.17 us  [on_device(): lax.ppermute(energy, 'head', [(i, partner(i, k, planes)) for i in range(p...]
  transfers between devices with their start and end apart: 13 -> 13, of which waited for: 3 -> 1; matrix products, arithmetic and copies ran while one was open for 3% -> 3% of each run, Pallas kernels for 23% -> 23%
where the time goes in v5:
time: 52.7 us; the launch traced here: 52.5 us
  starting transfers between devices  16.5 us (31%)
  Pallas kernels  14.3 us (27%)
  blocking collectives  11 us (21%)
  waiting for transfers between devices  4.12 us (8%)
  local copies, waits for them, and re-layouts  3.48 us (7%)
  other arithmetic  1.97 us (4%)
  between operations  1.14 us (2%)
    ppermute x8, starting transfers between devices, send(): lax.ppermute(a, 'ctx', [(i, target_of(i // cores, j) * cores + i % cores)...  11.7 us
    all_gather x1, blocking collectives, on_device(): gathered = lax.all_gather(jnp.pad(sent, ((0, -used % 16), (0, 0))), 'ctx')  11 us
    pallas_call x1, Pallas kernels, both_call(): pl.pallas_call(functools.partial(both_kernel, (places, cores, heads, True...  6.85 us
    pallas_call x1, Pallas kernels, student_call(): pl.pallas_call(functools.partial(student_kernel, start, heads), in_specs=...  5.31 us
    ppermute x3, starting transfers between devices, on_device(): lax.ppermute(energy, 'head', [(i, partner(i, k, planes)) for i in range(p...  4.17 us
    ppermute x8, waiting for transfers between devices, send(): lax.ppermute(a, 'ctx', [(i, target_of(i // cores, j) * cores + i % cores)...  4.11 us
    pallas_call x1, Pallas kernels, teacher_call(): pl.pallas_call(functools.partial(teacher_kernel, (places, cores, heads, w...  2.15 us
    transpose x1, local copies, waits for them, and re-layouts, exchange(): by_head.transpose(1, 0, 2).reshape(chips, cores, heads, tokens, dim)  1.66 us
  transfers between devices with their start and end apart: 13, of which 1 were waited for; matrix products, arithmetic and copies ran while one was open for 3% of the time, Pallas kernels for 23%

profile of v5, /device:TPU:0, one launch (start us, length us, event | category | flops | bytes accessed | tf_op | source)
XLA Modules:
  0.0 52.5 jit_solution(12526595070278720292)
XLA Ops:
  0.6 0.0 copy-start
  0.7 1.7 %copy.7 = bf16[32,128,128]{2,1,0:T(8,128)(2,1)S(1)} copy(bf16[32,128,128]{2,0,1:T(8,128)(2,1)} %bitcast.92) | data formatting | bytes 2097152 | tf_op jit(solution)/shard_map/transpose | solution.py:470
  2.3 0.0 copy-start.1
  2.4 0.5 collective-permute-start
  2.9 0.0 copy-done
  2.9 0.2 copy-done.1
  3.4 1.0 %dynamic-slice_bitcast_fusion.1 = (f32[4,64,128]{2,1,0:T(8,128)S(1)}, f32[4,64,128]{2,1,0:T(8,128)S(1)}) fusion(f32[32,128,64]{1,2,0:T(8,128)} %param.9, s32[]{:T(128)S(6)} %select_n.118, f32[32,128,64]{1,2,0:T(8,128)} %param.8), kind=kLoop, calls=%fused_computation.15 | loop fusion | bytes 524292 | tf_op jit(solution)/shard_map/dynamic_slice | solution.py:522
  4.4 0.1 dynamic-slice_bitcast_fusion.4
  4.5 0.0 collective-permute-done
  4.5 4.0 %collective-permute-start.5 = (bf16[2,128,128]{2,1,0:T(8,128)(2,1)S(1)}, bf16[2,128,128]{2,1,0:T(8,128)(2,1)S(1)}, u32[]{:S(2)}, u32[]{:S(2)}) collective-permute-start(bf16[2,128,128]{2,1,0:T(8,128)(2,1)S(1)} %get-tuple-element.51), channel_id=1, source_target_pairs={{0,24},{4,28},{8,16},{12,20},{16,8},{20,12},{24,0},{28,4},{1,25},{... | collective-permute-start | bytes 196616 | tf_op jit(solution)/shard_map/ppermute | solution.py:459
  8.5 0.5 collective-permute-start.4
  9.1 0.2 collective-permute-start.1
  9.3 2.0 %collective-permute-start.2 = (bf16[4,128,128]{2,1,0:T(8,128)(2,1)S(1)}, bf16[4,128,128]{2,1,0:T(8,128)(2,1)S(1)}, u32[]{:S(2)}, u32[]{:S(2)}) collective-permute-start(bf16[4,128,128]{2,1,0:T(8,128)(2,1)S(1)} %pad_maximum_fusion.4), channel_id=1, source_target_pairs={{0,16},{4,20},{8,24},{12,28},{16,0},{20,4},{24,8},{28,12},{1,17},{... | collective-permute-start | bytes 393224 | tf_op jit(solution)/shard_map/ppermute | solution.py:459
  11.3 1.5 %collective-permute-start.3 = (bf16[4,128,128]{2,1,0:T(8,128)(2,1)S(1)}, bf16[4,128,128]{2,1,0:T(8,128)(2,1)S(1)}, u32[]{:S(2)}, u32[]{:S(2)}) collective-permute-start(bf16[4,128,128]{2,1,0:T(8,128)(2,1)S(1)} %pad_maximum_fusion.5), channel_id=1, source_target_pairs={{0,24},{4,28},{8,16},{12,20},{16,8},{20,12},{24,0},{28,4},{1,25},{... | collective-permute-start | bytes 393224 | tf_op jit(solution)/shard_map/ppermute | solution.py:459
  12.8 4.1 %collective-permute-done.1.refs_1_ = bf16[6,128,128]{2,1,0:T(8,128)(2,1)S(1)} collective-permute-done((bf16[6,128,128]{2,1,0:T(8,128)(2,1)S(1)}, bf16[6,128,128]{2,1,0:T(8,128)(2,1)S(1)}, u32[]{:S(2)}, u32[]{:S(2)}) %collective-permute-start.1) | collective-permute-done | bytes 196640 | tf_op jit(solution)/shard_map/ppermute | solution.py:459
  16.9 0.0 collective-permute-done.5
  16.9 0.0 collective-permute-done.4
  17.0 0.1 collective-permute-start.6
  17.1 0.8 %collective-permute-start.7 = (bf16[4,128,128]{2,1,0:T(8,128)(2,1)S(1)}, bf16[4,128,128]{2,1,0:T(8,128)(2,1)S(1)}, u32[]{:S(2)}, u32[]{:S(2)}) collective-permute-start(bf16[4,128,128]{2,1,0:T(8,128)(2,1)S(1)} %get-tuple-element.22), channel_id=1, source_target_pairs={{0,8},{4,12},{8,0},{12,4},{16,24},{20,28},{24,16},{28,20},{1,9},{5... | collective-permute-start | bytes 393224 | tf_op jit(solution)/shard_map/ppermute | solution.py:459
  18.0 1.2 %collective-permute-start.8 = (bf16[4,128,128]{2,1,0:T(8,128)(2,1)S(1)}, bf16[4,128,128]{2,1,0:T(8,128)(2,1)S(1)}, u32[]{:S(2)}, u32[]{:S(2)}) collective-permute-start(bf16[4,128,128]{2,1,0:T(8,128)(2,1)S(1)} %get-tuple-element.23), channel_id=1, source_target_pairs={{0,16},{4,20},{8,24},{12,28},{16,0},{20,4},{24,8},{28,12},{1,17},{... | collective-permute-start | bytes 393224 | tf_op jit(solution)/shard_map/ppermute | solution.py:459
  19.2 0.0 collective-permute-done.2.refs_2_
  19.2 1.5 %collective-permute-start.9 = (bf16[4,128,128]{2,1,0:T(8,128)(2,1)S(1)}, bf16[4,128,128]{2,1,0:T(8,128)(2,1)S(1)}, u32[]{:S(2)}, u32[]{:S(2)}) collective-permute-start(bf16[4,128,128]{2,1,0:T(8,128)(2,1)S(1)} %get-tuple-element.24), channel_id=1, source_target_pairs={{0,24},{4,28},{8,16},{12,20},{16,8},{20,12},{24,0},{28,4},{1,25},{... | collective-permute-start | bytes 393224 | tf_op jit(solution)/shard_map/ppermute | solution.py:459
  20.7 0.0 collective-permute-done.3.refs_3_
  20.7 0.0 collective-permute-done.6.refs_5_
  20.7 6.8 %shard_map.68 = (bf16[8,2,128,128]{3,2,1,0:T(8,128)(2,1)S(1)}, f32[8,128]{1,0:T(8,128)S(1)}, f32[264,128]{1,0:T(8,128)S(1)}) custom-call(s32[1]{0:T(128)} %bitcast.place_ref, bf16[4,128,128]{2,1,0:T(8,128)(2,1)S(1)} %pad_maximum_fusion.2.refs_0_, bf16[6,128,128]{2,1,0:T(8,128)(2,1)S(1)} %collective-permute-done.1.refs_1_, ...), custom_call_target="tpu_custom_call" | custom-call | flops 9395240960 | bytes 5242880 | tf_op jit(solution)/shard_map/pallas_call | solution.py:410
  27.5 0.0 collective-permute-done.7.refs_1_
  27.6 0.0 collective-permute-done.8.refs_2_
  27.6 0.0 collective-permute-done.9.refs_3_
  27.6 2.2 %shard_map.69 = (bf16[8,2,128,128]{3,2,1,0:T(8,128)(2,1)S(1)}, f32[8,2,128,128]{3,2,1,0:T(8,128)S(1)}, f32[8,128]{1,0:T(8,128)S(1)}) custom-call(s32[1]{0:T(128)} %bitcast.place_ref, bf16[4,128,128]{2,1,0:T(8,128)(2,1)S(1)} %get-tuple-element.21.refs_0_, bf16[4,128,128]{2,1,0:T(8,128)(2,1)S(1)} %collective-permute-done.7.refs_1_, ...), custom_call_target="tpu_custom_call" | custom-call | flops 2684354560 | bytes 2097152 | tf_op jit(solution)/shard_map/pallas_call | solution.py:155
  29.7 2.6 %collective-permute-start.11 = (f32[8,128]{1,0:T(8,128)S(1)}, f32[8,128]{1,0:T(8,128)S(1)}, u32[]{:S(2)}, u32[]{:S(2)}) collective-permute-start(f32[8,128]{1,0:T(8,128)S(1)} %broadcast_select_fusion), channel_id=1, source_target_pairs={{0,2},{1,3},{2,0},{3,1},{4,6},{5,7},{6,4},{7,5},{8,10},{9,11},{10,... | collective-permute-start | bytes 12296 | tf_op jit(solution)/shard_map/ppermute | solution.py:543
  32.3 1.3 %collective-permute-start.12 = (f32[8,128]{1,0:T(8,128)S(1)}, f32[8,128]{1,0:T(8,128)S(1)}, u32[]{:S(2)}, u32[]{:S(2)}) collective-permute-start(f32[8,128]{1,0:T(8,128)S(1)} %broadcast_select_fusion), channel_id=1, source_target_pairs={{0,3},{1,2},{2,1},{3,0},{4,7},{5,6},{6,5},{7,4},{8,11},{9,10},{10,... | collective-permute-start | bytes 12296 | tf_op jit(solution)/shard_map/ppermute | solution.py:543
  33.7 0.2 collective-permute-start.10
  33.9 5.3 %shard_map.70 = f32[264,128]{1,0:T(8,128)S(1)} custom-call(bf16[8,2,128,128]{3,2,1,0:T(8,128)(2,1)S(1)} %get-tuple-element.27.x_ref, bf16[8,2,128,128]{3,2,1,0:T(8,128)(2,1)S(1)} %get-tuple-element.25.refs_4_.kv_ref, f32[8,2,128,128]{3,2,1,0:T(8,128)S(1)} %get-tuple-element.28.teacher_ref, f32[4,64,128]{2,1,0:T(8,128)S(1)} %get-tuple-element.67.refs_6_.mq_ref, ...), custom_call_target="tpu_custom_call" | custom-call | flops 6710886400 | bytes 3145728 | tf_op jit(solution)/shard_map/pallas_call | solution.py:370
  39.4 0.0 collective-permute-done.11
  39.4 0.0 collective-permute-done.12
  39.4 0.0 collective-permute-done.10
  39.4 0.1 constant_dynamic-update-slice_fusion
  39.5 11.0 %all-gather.2 = f16[4352,128]{1,0:T(8,128)(2,1)S(1)} all-gather(f16[544,128]{1,0:T(8,128)(2,1)S(1)} %pad.4), channel_id=2, replica_groups=mesh['ctx'=8,'head'=4] {'ctx'}, dimensions={0}, use_global_device_ids=true | all-gather | bytes 1253376 | tf_op jit(solution)/shard_map/all_gather | solution.py:555
  50.6 0.2 fusion.9
  50.9 1.6 %fusion = (f32[32,128,64]{1,2,0:T(8,128)}, f32[32,128,64]{1,2,0:T(8,128)}) fusion(f16[32,64,128]{2,1,0:T(8,128)(2,1)S(1)} %bitcast.90, f32[32,128]{1,0:T(8,128)S(1)} %broadcast_multiply_fusion, f16[32,64,128]{2,1,0:T(8,128)(2,1)S(1)} %bitcast.91), kind=kLoop, calls=%fused_computation.1 | loop fusion | flops 1048576 | bytes 3162112 | tf_op jit(solution)/shard_map/transpose | solution.py:570
  (34 shorter events, 0.6 us)
Async XLA Ops:
  0.6 2.3 %copy-start = (bf16[128,2,128]{2,1,0:T(2,128)(2,1)S(1)}, bf16[128,2,128]{2,1,0:T(2,128)(2,1)}, u32[]{:S(2)}) copy-start(bf16[128,2,128]{2,1,0:T(2,128)(2,1)} %param.7) | copy-start | bytes 196612
  2.3 0.8 %copy-start.1 = (bf16[128,2,128]{2,1,0:T(2,128)(2,1)S(1)}, bf16[128,2,128]{2,1,0:T(2,128)(2,1)}, u32[]{:S(2)}) copy-start(bf16[128,2,128]{2,1,0:T(2,128)(2,1)} %param.6) | copy-start | bytes 196612
  2.4 2.1 %collective-permute-start = (bf16[4,4,128,128]{3,2,1,0:T(8,128)(2,1)S(1)}, bf16[4,4,128,128]{3,2,1,0:T(8,128)(2,1)S(1)}, u32[]{:S(2)}, u32[]{:S(2)}) collective-permute-start(bf16[4,4,128,128]{3,2,1,0:T(8,128)(2,1)S(1)} %dynamic-slice_bitcast_fusion), channel_id=1, source_target_pairs={{0,4},{4,0},{8,12},{12,8},{16,20},{20,16},{24,28},{28,24},{1,5},{5... | collective-permute-start | bytes 1572872 | tf_op jit(solution)/shard_map/ppermute | solution.py:464
  4.5 12.4 %collective-permute-start.5 = (bf16[2,128,128]{2,1,0:T(8,128)(2,1)S(1)}, bf16[2,128,128]{2,1,0:T(8,128)(2,1)S(1)}, u32[]{:S(2)}, u32[]{:S(2)}) collective-permute-start(bf16[2,128,128]{2,1,0:T(8,128)(2,1)S(1)} %get-tuple-element.51), channel_id=1, source_target_pairs={{0,24},{4,28},{8,16},{12,20},{16,8},{20,12},{24,0},{28,4},{1,25},{... | collective-permute-start | bytes 196616 | tf_op jit(solution)/shard_map/ppermute | solution.py:459
  8.5 8.4 %collective-permute-start.4 = (bf16[2,128,128]{2,1,0:T(8,128)(2,1)S(1)}, bf16[2,128,128]{2,1,0:T(8,128)(2,1)S(1)}, u32[]{:S(2)}, u32[]{:S(2)}) collective-permute-start(bf16[2,128,128]{2,1,0:T(8,128)(2,1)S(1)} %get-tuple-element.52), channel_id=1, source_target_pairs={{0,16},{4,20},{8,24},{12,28},{16,0},{20,4},{24,8},{28,12},{1,17},{... | collective-permute-start | bytes 196616 | tf_op jit(solution)/shard_map/ppermute | solution.py:459
  9.1 7.8 %collective-permute-start.1 = (bf16[6,128,128]{2,1,0:T(8,128)(2,1)S(1)}, bf16[6,128,128]{2,1,0:T(8,128)(2,1)S(1)}, u32[]{:S(2)}, u32[]{:S(2)}) collective-permute-start(bf16[6,128,128]{2,1,0:T(8,128)(2,1)S(1)} %pad_maximum_fusion.1), channel_id=1, source_target_pairs={{0,8},{4,12},{8,0},{12,4},{16,24},{20,28},{24,16},{28,20},{1,9},{5... | collective-permute-start | bytes 589832 | tf_op jit(solution)/shard_map/ppermute | solution.py:459
  9.3 9.9 %collective-permute-start.2 = (bf16[4,128,128]{2,1,0:T(8,128)(2,1)S(1)}, bf16[4,128,128]{2,1,0:T(8,128)(2,1)S(1)}, u32[]{:S(2)}, u32[]{:S(2)}) collective-permute-start(bf16[4,128,128]{2,1,0:T(8,128)(2,1)S(1)} %pad_maximum_fusion.4), channel_id=1, source_target_pairs={{0,16},{4,20},{8,24},{12,28},{16,0},{20,4},{24,8},{28,12},{1,17},{... | collective-permute-start | bytes 393224 | tf_op jit(solution)/shard_map/ppermute | solution.py:459
  11.3 9.4 %collective-permute-start.3 = (bf16[4,128,128]{2,1,0:T(8,128)(2,1)S(1)}, bf16[4,128,128]{2,1,0:T(8,128)(2,1)S(1)}, u32[]{:S(2)}, u32[]{:S(2)}) collective-permute-start(bf16[4,128,128]{2,1,0:T(8,128)(2,1)S(1)} %pad_maximum_fusion.5), channel_id=1, source_target_pairs={{0,24},{4,28},{8,16},{12,20},{16,8},{20,12},{24,0},{28,4},{1,25},{... | collective-permute-start | bytes 393224 | tf_op jit(solution)/shard_map/ppermute | solution.py:459
  17.0 3.7 %collective-permute-start.6 = (bf16[4,2,128,128]{3,2,1,0:T(8,128)(2,1)S(1)}, bf16[4,2,128,128]{3,2,1,0:T(8,128)(2,1)S(1)}, u32[]{:S(2)}, u32[]{:S(2)}) collective-permute-start(bf16[4,2,128,128]{3,2,1,0:T(8,128)(2,1)S(1)} %pad_maximum_fusion.refs_4_), channel_id=1, source_target_pairs={{0,4},{4,0},{8,12},{12,8},{16,20},{20,16},{24,28},{28,24},{1,5},{5... | collective-permute-start | bytes 786440 | tf_op jit(solution)/shard_map/ppermute | solution.py:464
  17.1 10.4 %collective-permute-start.7 = (bf16[4,128,128]{2,1,0:T(8,128)(2,1)S(1)}, bf16[4,128,128]{2,1,0:T(8,128)(2,1)S(1)}, u32[]{:S(2)}, u32[]{:S(2)}) collective-permute-start(bf16[4,128,128]{2,1,0:T(8,128)(2,1)S(1)} %get-tuple-element.22), channel_id=1, source_target_pairs={{0,8},{4,12},{8,0},{12,4},{16,24},{20,28},{24,16},{28,20},{1,9},{5... | collective-permute-start | bytes 393224 | tf_op jit(solution)/shard_map/ppermute | solution.py:459
  18.0 9.6 %collective-permute-start.8 = (bf16[4,128,128]{2,1,0:T(8,128)(2,1)S(1)}, bf16[4,128,128]{2,1,0:T(8,128)(2,1)S(1)}, u32[]{:S(2)}, u32[]{:S(2)}) collective-permute-start(bf16[4,128,128]{2,1,0:T(8,128)(2,1)S(1)} %get-tuple-element.23), channel_id=1, source_target_pairs={{0,16},{4,20},{8,24},{12,28},{16,0},{20,4},{24,8},{28,12},{1,17},{... | collective-permute-start | bytes 393224 | tf_op jit(solution)/shard_map/ppermute | solution.py:459
  19.2 8.4 %collective-permute-start.9 = (bf16[4,128,128]{2,1,0:T(8,128)(2,1)S(1)}, bf16[4,128,128]{2,1,0:T(8,128)(2,1)S(1)}, u32[]{:S(2)}, u32[]{:S(2)}) collective-permute-start(bf16[4,128,128]{2,1,0:T(8,128)(2,1)S(1)} %get-tuple-element.24), channel_id=1, source_target_pairs={{0,24},{4,28},{8,16},{12,20},{16,8},{20,12},{24,0},{28,4},{1,25},{... | collective-permute-start | bytes 393224 | tf_op jit(solution)/shard_map/ppermute | solution.py:459
  29.7 9.6 %collective-permute-start.11 = (f32[8,128]{1,0:T(8,128)S(1)}, f32[8,128]{1,0:T(8,128)S(1)}, u32[]{:S(2)}, u32[]{:S(2)}) collective-permute-start(f32[8,128]{1,0:T(8,128)S(1)} %broadcast_select_fusion), channel_id=1, source_target_pairs={{0,2},{1,3},{2,0},{3,1},{4,6},{5,7},{6,4},{7,5},{8,10},{9,11},{10,... | collective-permute-start | bytes 12296 | tf_op jit(solution)/shard_map/ppermute | solution.py:543
  32.3 7.1 %collective-permute-start.12 = (f32[8,128]{1,0:T(8,128)S(1)}, f32[8,128]{1,0:T(8,128)S(1)}, u32[]{:S(2)}, u32[]{:S(2)}) collective-permute-start(f32[8,128]{1,0:T(8,128)S(1)} %broadcast_select_fusion), channel_id=1, source_target_pairs={{0,3},{1,2},{2,1},{3,0},{4,7},{5,6},{6,5},{7,4},{8,11},{9,10},{10,... | collective-permute-start | bytes 12296 | tf_op jit(solution)/shard_map/ppermute | solution.py:543
  33.7 5.7 %collective-permute-start.10 = (f32[8,128]{1,0:T(8,128)S(1)}, f32[8,128]{1,0:T(8,128)S(1)}, u32[]{:S(2)}, u32[]{:S(2)}) collective-permute-start(f32[8,128]{1,0:T(8,128)S(1)} %broadcast_select_fusion), channel_id=1, source_target_pairs={{0,1},{1,0},{2,3},{3,2},{4,5},{5,4},{6,7},{7,6},{8,9},{9,8},{10,11... | collective-permute-start | bytes 12296 | tf_op jit(solution)/shard_map/ppermute | solution.py:543

commit v6 on v5

--- a/solution.py
+++ b/solution.py
@@ -502,6 +502,38 @@
     return arrived, keys, source_of
 
 
+def unpack_kernel(heads, power_rows, tail_row, scale, gathered_ref, *out_refs):
+    places, _, dim = gathered_ref.shape
+    features = out_refs[0].shape[1]
+
+    def row(p, i):
+        return gathered_ref[p, i : i + 1, :]
+
+    energy = jnp.zeros((1, dim), F32)
+    for p in range(places):
+        near_one = row(p, tail_row + 1) + row(p, tail_row + 2) * (1.0 / 1024.0)
+        energy = energy + near_one * jnp.exp2(row(p, tail_row))
+    scale = scale / energy
+    for p in range(places):
+        for h in range(heads):
+            factor = jnp.exp2(row(p, power_rows[h])) * scale
+            for i, out_ref in enumerate(out_refs):
+                rows = pl.ds((i * heads + h) * features, features)
+                out_ref[p * heads + h] = gathered_ref[p, rows, :] * factor
+
+
+def unpack_call(gathered, heads, features, power_rows, tail_row, scale):
+    places, _, dim = gathered.shape
+    whole = pl.BlockSpec(memory_space=pltpu.VMEM)
+    return pl.pallas_call(
+        functools.partial(unpack_kernel, heads, power_rows, tail_row, scale),
+        in_specs=[whole],
+        out_specs=[whole, whole],
+        out_shape=[jax.ShapeDtypeStruct((places * heads, features, dim), F32)] * 2,
+        compiler_params=pltpu.CompilerParams(vmem_limit_bytes=VMEM_LIMIT),
+    )(gathered)
+
+
 def on_device(queries, key_states, value_vector_states, map_query, map_key):
     places = lax.axis_size("ctx")
     planes = lax.axis_size("head")
@@ -552,24 +584,14 @@
     grads = [part for side in zip(*grads) for part in side]
     sent = jnp.concatenate(grads + powers + [tail]).astype(F16)
     used = sent.shape[0]
-    gathered = lax.all_gather(jnp.pad(sent, ((0, -used % 16), (0, 0))), "ctx")
-    rows = heads * 2 * features
-    power, at = [], rows
+    gathered = lax.all_gather(jnp.pad(sent, ((0, -used % 16), (0, 0))), "ctx").astype(F32)
+    power_rows, at = [], heads * 2 * features
     for (start, stop), p in zip(parts, powers):
-        power.append(gathered[:, at : at + stop - start])
+        power_rows += [at + h for h in range(stop - start)]
         at += p.shape[0]
-    power = jnp.concatenate(power, axis=1).astype(F32)
-    tail = gathered[:, at : at + 3].astype(F32)
-    energy = jnp.sum((tail[:, 1] + tail[:, 2] * (1.0 / 1024.0)) * jnp.exp2(tail[:, 0]), axis=0)
-    factor = (jnp.exp2(power) * (2.0 * query_heads * planes / energy))[:, :, None]
-
-    def unpacked(i):
-        part = gathered[:, i * rows // 2 : (i + 1) * rows // 2].astype(F32)
-        part = part.reshape(places, heads, features, dim) * factor
-        part = part.reshape(places * heads, features, dim)
-        return part[:query_heads].transpose(0, 2, 1)
-
-    return (unpacked(0), unpacked(1))
+    scale = 2.0 * query_heads * planes
+    unpacked = unpack_call(in_vmem(gathered), heads, features, power_rows, at, scale)
+    return tuple(a[:query_heads].transpose(0, 2, 1) for a in unpacked)
 
 
 def solution(mesh):

time: 52.7 us -> 52.3 us (level)
  other arithmetic: 1.97 us -> 0.45 us
  Pallas kernels: 14.3 us -> 15.8 us
    transpose x1 -> x0, other arithmetic: 1.59 us -> none  [unpacked(): return part[:query_heads].transpose(0, 2, 1)]
    pallas_call x0 -> x1, Pallas kernels: none -> 1.48 us  [unpack_call(): pl.pallas_call(functools.partial(unpack_kernel, heads, power_rows, tail_r...]
  transfers between devices with their start and end apart: 13 -> 13, of which waited for: 1 -> 2; matrix products, arithmetic and copies ran while one was open for 3% -> 3% of each run, Pallas kernels for 23% -> 23%
where the time goes in v6:
time: 52.3 us; the launch traced here: 52.2 us
  starting transfers between devices  16.4 us (31%)
  Pallas kernels  15.8 us (30%)
  blocking collectives  11.1 us (21%)
  waiting for transfers between devices  4.33 us (8%)
  local copies, waits for them, and re-layouts  2.99 us (6%)
  between operations  1.11 us (2%)
    ppermute x8, starting transfers between devices, send(): lax.ppermute(a, 'ctx', [(i, target_of(i // cores, j) * cores + i % cores)...  11.6 us
    all_gather x1, blocking collectives, on_device(): lax.all_gather(jnp.pad(sent, ((0, -used % 16), (0, 0))), 'ctx').astype(F32)  11.1 us
    pallas_call x1, Pallas kernels, both_call(): pl.pallas_call(functools.partial(both_kernel, (places, cores, heads, True...  6.85 us
    pallas_call x1, Pallas kernels, student_call(): pl.pallas_call(functools.partial(student_kernel, start, heads), in_specs=...  5.31 us
    ppermute x3, starting transfers between devices, on_device(): lax.ppermute(energy, 'head', [(i, partner(i, k, planes)) for i in range(p...  4.18 us
    ppermute x8, waiting for transfers between devices, send(): lax.ppermute(a, 'ctx', [(i, target_of(i // cores, j) * cores + i % cores)...  4.15 us
    pallas_call x1, Pallas kernels, teacher_call(): pl.pallas_call(functools.partial(teacher_kernel, (places, cores, heads, w...  2.15 us
    transpose x1, local copies, waits for them, and re-layouts, exchange(): by_head.transpose(1, 0, 2).reshape(chips, cores, heads, tokens, dim)  1.66 us
  transfers between devices with their start and end apart: 13, of which 2 were waited for; matrix products, arithmetic and copies ran while one was open for 3% of the time, Pallas kernels for 23%

profile of v6, /device:TPU:0, one launch (start us, length us, event | category | flops | bytes accessed | tf_op | source)
XLA Modules:
  0.0 52.2 jit_solution(10663605044670993788)
XLA Ops:
  0.6 0.0 copy-start
  0.6 0.0 copy-start.1
  0.7 1.7 %copy.7 = bf16[32,128,128]{2,1,0:T(8,128)(2,1)S(1)} copy(bf16[32,128,128]{2,0,1:T(8,128)(2,1)} %bitcast.78) | data formatting | bytes 2097152 | tf_op jit(solution)/shard_map/transpose | solution.py:470
  2.4 0.5 collective-permute-start
  2.9 0.0 copy-done
  2.9 0.0 copy-done.1
  3.2 1.0 %dynamic-slice_bitcast_fusion.1 = (f32[4,64,128]{2,1,0:T(8,128)S(1)}, f32[4,64,128]{2,1,0:T(8,128)S(1)}) fusion(f32[32,128,64]{1,2,0:T(8,128)} %param.9, s32[]{:T(128)S(6)} %select_n.118, f32[32,128,64]{1,2,0:T(8,128)} %param.8), kind=kLoop, calls=%fused_computation.11 | loop fusion | bytes 524292 | tf_op jit(solution)/shard_map/dynamic_slice | solution.py:554
  4.2 0.1 dynamic-slice_bitcast_fusion.4
  4.3 0.2 collective-permute-done
  4.5 3.9 %collective-permute-start.5 = (bf16[2,128,128]{2,1,0:T(8,128)(2,1)S(1)}, bf16[2,128,128]{2,1,0:T(8,128)(2,1)S(1)}, u32[]{:S(2)}, u32[]{:S(2)}) collective-permute-start(bf16[2,128,128]{2,1,0:T(8,128)(2,1)S(1)} %get-tuple-element.51), channel_id=1, source_target_pairs={{0,24},{4,28},{8,16},{12,20},{16,8},{20,12},{24,0},{28,4},{1,25},{... | collective-permute-start | bytes 196616 | tf_op jit(solution)/shard_map/ppermute | solution.py:459
  8.4 0.5 collective-permute-start.4
  8.9 0.2 collective-permute-start.1
  9.2 2.0 %collective-permute-start.2 = (bf16[4,128,128]{2,1,0:T(8,128)(2,1)S(1)}, bf16[4,128,128]{2,1,0:T(8,128)(2,1)S(1)}, u32[]{:S(2)}, u32[]{:S(2)}) collective-permute-start(bf16[4,128,128]{2,1,0:T(8,128)(2,1)S(1)} %pad_maximum_fusion.4), channel_id=1, source_target_pairs={{0,16},{4,20},{8,24},{12,28},{16,0},{20,4},{24,8},{28,12},{1,17},{... | collective-permute-start | bytes 393224 | tf_op jit(solution)/shard_map/ppermute | solution.py:459
  11.2 1.5 %collective-permute-start.3 = (bf16[4,128,128]{2,1,0:T(8,128)(2,1)S(1)}, bf16[4,128,128]{2,1,0:T(8,128)(2,1)S(1)}, u32[]{:S(2)}, u32[]{:S(2)}) collective-permute-start(bf16[4,128,128]{2,1,0:T(8,128)(2,1)S(1)} %pad_maximum_fusion.5), channel_id=1, source_target_pairs={{0,24},{4,28},{8,16},{12,20},{16,8},{20,12},{24,0},{28,4},{1,25},{... | collective-permute-start | bytes 393224 | tf_op jit(solution)/shard_map/ppermute | solution.py:459
  12.7 4.1 %collective-permute-done.1.refs_1_ = bf16[6,128,128]{2,1,0:T(8,128)(2,1)S(1)} collective-permute-done((bf16[6,128,128]{2,1,0:T(8,128)(2,1)S(1)}, bf16[6,128,128]{2,1,0:T(8,128)(2,1)S(1)}, u32[]{:S(2)}, u32[]{:S(2)}) %collective-permute-start.1) | collective-permute-done | bytes 196640 | tf_op jit(solution)/shard_map/ppermute | solution.py:459
  16.8 0.0 collective-permute-done.5
  16.8 0.0 collective-permute-done.4
  16.9 0.1 collective-permute-start.6
  17.0 0.8 %collective-permute-start.7 = (bf16[4,128,128]{2,1,0:T(8,128)(2,1)S(1)}, bf16[4,128,128]{2,1,0:T(8,128)(2,1)S(1)}, u32[]{:S(2)}, u32[]{:S(2)}) collective-permute-start(bf16[4,128,128]{2,1,0:T(8,128)(2,1)S(1)} %get-tuple-element.24), channel_id=1, source_target_pairs={{0,8},{4,12},{8,0},{12,4},{16,24},{20,28},{24,16},{28,20},{1,9},{5... | collective-permute-start | bytes 393224 | tf_op jit(solution)/shard_map/ppermute | solution.py:459
  17.8 1.3 %collective-permute-start.8 = (bf16[4,128,128]{2,1,0:T(8,128)(2,1)S(1)}, bf16[4,128,128]{2,1,0:T(8,128)(2,1)S(1)}, u32[]{:S(2)}, u32[]{:S(2)}) collective-permute-start(bf16[4,128,128]{2,1,0:T(8,128)(2,1)S(1)} %get-tuple-element.25), channel_id=1, source_target_pairs={{0,16},{4,20},{8,24},{12,28},{16,0},{20,4},{24,8},{28,12},{1,17},{... | collective-permute-start | bytes 393224 | tf_op jit(solution)/shard_map/ppermute | solution.py:459
  19.1 0.0 collective-permute-done.2.refs_2_
  19.1 1.4 %collective-permute-start.9 = (bf16[4,128,128]{2,1,0:T(8,128)(2,1)S(1)}, bf16[4,128,128]{2,1,0:T(8,128)(2,1)S(1)}, u32[]{:S(2)}, u32[]{:S(2)}) collective-permute-start(bf16[4,128,128]{2,1,0:T(8,128)(2,1)S(1)} %get-tuple-element.26), channel_id=1, source_target_pairs={{0,24},{4,28},{8,16},{12,20},{16,8},{20,12},{24,0},{28,4},{1,25},{... | collective-permute-start | bytes 393224 | tf_op jit(solution)/shard_map/ppermute | solution.py:459
  20.6 0.0 collective-permute-done.3.refs_3_
  20.6 0.0 collective-permute-done.6.refs_5_
  20.6 6.8 %shard_map.68 = (bf16[8,2,128,128]{3,2,1,0:T(8,128)(2,1)S(1)}, f32[8,128]{1,0:T(8,128)S(1)}, f32[264,128]{1,0:T(8,128)S(1)}) custom-call(s32[1]{0:T(128)} %bitcast.place_ref, bf16[4,128,128]{2,1,0:T(8,128)(2,1)S(1)} %pad_maximum_fusion.2.refs_0_, bf16[6,128,128]{2,1,0:T(8,128)(2,1)S(1)} %collective-permute-done.1.refs_1_, ...), custom_call_target="tpu_custom_call" | custom-call | flops 9395240960 | bytes 5242880 | tf_op jit(solution)/shard_map/pallas_call | solution.py:410
  27.4 0.0 collective-permute-done.7.refs_1_
  27.5 0.0 collective-permute-done.8.refs_2_
  27.5 0.0 collective-permute-done.9.refs_3_
  27.5 2.1 %shard_map.69 = (bf16[8,2,128,128]{3,2,1,0:T(8,128)(2,1)S(1)}, f32[8,2,128,128]{3,2,1,0:T(8,128)S(1)}, f32[8,128]{1,0:T(8,128)S(1)}) custom-call(s32[1]{0:T(128)} %bitcast.place_ref, bf16[4,128,128]{2,1,0:T(8,128)(2,1)S(1)} %get-tuple-element.23.refs_0_, bf16[4,128,128]{2,1,0:T(8,128)(2,1)S(1)} %collective-permute-done.7.refs_1_, ...), custom_call_target="tpu_custom_call" | custom-call | flops 2684354560 | bytes 2097152 | tf_op jit(solution)/shard_map/pallas_call | solution.py:155
  29.6 2.6 %collective-permute-start.11 = (f32[8,128]{1,0:T(8,128)S(1)}, f32[8,128]{1,0:T(8,128)S(1)}, u32[]{:S(2)}, u32[]{:S(2)}) collective-permute-start(f32[8,128]{1,0:T(8,128)S(1)} %broadcast_select_fusion), channel_id=1, source_target_pairs={{0,2},{1,3},{2,0},{3,1},{4,6},{5,7},{6,4},{7,5},{8,10},{9,11},{10,... | collective-permute-start | bytes 12296 | tf_op jit(solution)/shard_map/ppermute | solution.py:575
  32.2 1.3 %collective-permute-start.12 = (f32[8,128]{1,0:T(8,128)S(1)}, f32[8,128]{1,0:T(8,128)S(1)}, u32[]{:S(2)}, u32[]{:S(2)}) collective-permute-start(f32[8,128]{1,0:T(8,128)S(1)} %broadcast_select_fusion), channel_id=1, source_target_pairs={{0,3},{1,2},{2,1},{3,0},{4,7},{5,6},{6,5},{7,4},{8,11},{9,10},{10,... | collective-permute-start | bytes 12296 | tf_op jit(solution)/shard_map/ppermute | solution.py:575
  33.6 0.2 collective-permute-start.10
  33.8 5.3 %shard_map.70 = f32[264,128]{1,0:T(8,128)S(1)} custom-call(bf16[8,2,128,128]{3,2,1,0:T(8,128)(2,1)S(1)} %get-tuple-element.29.x_ref, bf16[8,2,128,128]{3,2,1,0:T(8,128)(2,1)S(1)} %get-tuple-element.27.refs_4_.kv_ref, f32[8,2,128,128]{3,2,1,0:T(8,128)S(1)} %get-tuple-element.30.teacher_ref, f32[4,64,128]{2,1,0:T(8,128)S(1)} %get-tuple-element.65.refs_6_.mq_ref, ...), custom_call_target="tpu_custom_call" | custom-call | flops 6710886400 | bytes 3145728 | tf_op jit(solution)/shard_map/pallas_call | solution.py:370
  39.3 0.0 collective-permute-done.11
  39.3 0.0 collective-permute-done.12
  39.3 0.0 collective-permute-done.10
  39.3 0.1 constant_dynamic-update-slice_fusion
  39.4 11.1 %all-gather.2 = f16[4352,128]{1,0:T(8,128)(2,1)S(1)} all-gather(f16[544,128]{1,0:T(8,128)(2,1)S(1)} %pad.4), channel_id=2, replica_groups=mesh['ctx'=8,'head'=4] {'ctx'}, dimensions={0}, use_global_device_ids=true | all-gather | bytes 1253376 | tf_op jit(solution)/shard_map/all_gather | solution.py:587
  50.5 0.1 convert.22.gathered_ref
  50.7 1.5 %shard_map.71 = (f32[32,64,128]{2,1,0:T(8,128)}, f32[32,64,128]{2,1,0:T(8,128)}) custom-call(f32[8,544,128]{2,1,0:T(8,128)S(1)} %convert.22.gathered_ref), custom_call_target="tpu_custom_call" | custom-call | tf_op jit(solution)/shard_map/pallas_call | solution.py:528
  (28 shorter events, 0.5 us)
Async XLA Ops:
  0.6 2.3 %copy-start = (bf16[128,2,128]{2,1,0:T(2,128)(2,1)S(1)}, bf16[128,2,128]{2,1,0:T(2,128)(2,1)}, u32[]{:S(2)}) copy-start(bf16[128,2,128]{2,1,0:T(2,128)(2,1)} %param.7) | copy-start | bytes 196612
  0.6 2.3 %copy-start.1 = (bf16[128,2,128]{2,1,0:T(2,128)(2,1)S(1)}, bf16[128,2,128]{2,1,0:T(2,128)(2,1)}, u32[]{:S(2)}) copy-start(bf16[128,2,128]{2,1,0:T(2,128)(2,1)} %param.6) | copy-start | bytes 196612
  2.4 2.1 %collective-permute-start = (bf16[4,4,128,128]{3,2,1,0:T(8,128)(2,1)S(1)}, bf16[4,4,128,128]{3,2,1,0:T(8,128)(2,1)S(1)}, u32[]{:S(2)}, u32[]{:S(2)}) collective-permute-start(bf16[4,4,128,128]{3,2,1,0:T(8,128)(2,1)S(1)} %dynamic-slice_bitcast_fusion), channel_id=1, source_target_pairs={{0,4},{4,0},{8,12},{12,8},{16,20},{20,16},{24,28},{28,24},{1,5},{5... | collective-permute-start | bytes 1572872 | tf_op jit(solution)/shard_map/ppermute | solution.py:464
  4.5 12.3 %collective-permute-start.5 = (bf16[2,128,128]{2,1,0:T(8,128)(2,1)S(1)}, bf16[2,128,128]{2,1,0:T(8,128)(2,1)S(1)}, u32[]{:S(2)}, u32[]{:S(2)}) collective-permute-start(bf16[2,128,128]{2,1,0:T(8,128)(2,1)S(1)} %get-tuple-element.51), channel_id=1, source_target_pairs={{0,24},{4,28},{8,16},{12,20},{16,8},{20,12},{24,0},{28,4},{1,25},{... | collective-permute-start | bytes 196616 | tf_op jit(solution)/shard_map/ppermute | solution.py:459
  8.4 8.4 %collective-permute-start.4 = (bf16[2,128,128]{2,1,0:T(8,128)(2,1)S(1)}, bf16[2,128,128]{2,1,0:T(8,128)(2,1)S(1)}, u32[]{:S(2)}, u32[]{:S(2)}) collective-permute-start(bf16[2,128,128]{2,1,0:T(8,128)(2,1)S(1)} %get-tuple-element.52), channel_id=1, source_target_pairs={{0,16},{4,20},{8,24},{12,28},{16,0},{20,4},{24,8},{28,12},{1,17},{... | collective-permute-start | bytes 196616 | tf_op jit(solution)/shard_map/ppermute | solution.py:459
  8.9 7.9 %collective-permute-start.1 = (bf16[6,128,128]{2,1,0:T(8,128)(2,1)S(1)}, bf16[6,128,128]{2,1,0:T(8,128)(2,1)S(1)}, u32[]{:S(2)}, u32[]{:S(2)}) collective-permute-start(bf16[6,128,128]{2,1,0:T(8,128)(2,1)S(1)} %pad_maximum_fusion.1), channel_id=1, source_target_pairs={{0,8},{4,12},{8,0},{12,4},{16,24},{20,28},{24,16},{28,20},{1,9},{5... | collective-permute-start | bytes 589832 | tf_op jit(solution)/shard_map/ppermute | solution.py:459
  9.2 10.0 %collective-permute-start.2 = (bf16[4,128,128]{2,1,0:T(8,128)(2,1)S(1)}, bf16[4,128,128]{2,1,0:T(8,128)(2,1)S(1)}, u32[]{:S(2)}, u32[]{:S(2)}) collective-permute-start(bf16[4,128,128]{2,1,0:T(8,128)(2,1)S(1)} %pad_maximum_fusion.4), channel_id=1, source_target_pairs={{0,16},{4,20},{8,24},{12,28},{16,0},{20,4},{24,8},{28,12},{1,17},{... | collective-permute-start | bytes 393224 | tf_op jit(solution)/shard_map/ppermute | solution.py:459
  11.2 9.4 %collective-permute-start.3 = (bf16[4,128,128]{2,1,0:T(8,128)(2,1)S(1)}, bf16[4,128,128]{2,1,0:T(8,128)(2,1)S(1)}, u32[]{:S(2)}, u32[]{:S(2)}) collective-permute-start(bf16[4,128,128]{2,1,0:T(8,128)(2,1)S(1)} %pad_maximum_fusion.5), channel_id=1, source_target_pairs={{0,24},{4,28},{8,16},{12,20},{16,8},{20,12},{24,0},{28,4},{1,25},{... | collective-permute-start | bytes 393224 | tf_op jit(solution)/shard_map/ppermute | solution.py:459
  16.9 3.7 %collective-permute-start.6 = (bf16[4,2,128,128]{3,2,1,0:T(8,128)(2,1)S(1)}, bf16[4,2,128,128]{3,2,1,0:T(8,128)(2,1)S(1)}, u32[]{:S(2)}, u32[]{:S(2)}) collective-permute-start(bf16[4,2,128,128]{3,2,1,0:T(8,128)(2,1)S(1)} %pad_maximum_fusion.refs_4_), channel_id=1, source_target_pairs={{0,4},{4,0},{8,12},{12,8},{16,20},{20,16},{24,28},{28,24},{1,5},{5... | collective-permute-start | bytes 786440 | tf_op jit(solution)/shard_map/ppermute | solution.py:464
  17.0 10.4 %collective-permute-start.7 = (bf16[4,128,128]{2,1,0:T(8,128)(2,1)S(1)}, bf16[4,128,128]{2,1,0:T(8,128)(2,1)S(1)}, u32[]{:S(2)}, u32[]{:S(2)}) collective-permute-start(bf16[4,128,128]{2,1,0:T(8,128)(2,1)S(1)} %get-tuple-element.24), channel_id=1, source_target_pairs={{0,8},{4,12},{8,0},{12,4},{16,24},{20,28},{24,16},{28,20},{1,9},{5... | collective-permute-start | bytes 393224 | tf_op jit(solution)/shard_map/ppermute | solution.py:459
  17.8 9.7 %collective-permute-start.8 = (bf16[4,128,128]{2,1,0:T(8,128)(2,1)S(1)}, bf16[4,128,128]{2,1,0:T(8,128)(2,1)S(1)}, u32[]{:S(2)}, u32[]{:S(2)}) collective-permute-start(bf16[4,128,128]{2,1,0:T(8,128)(2,1)S(1)} %get-tuple-element.25), channel_id=1, source_target_pairs={{0,16},{4,20},{8,24},{12,28},{16,0},{20,4},{24,8},{28,12},{1,17},{... | collective-permute-start | bytes 393224 | tf_op jit(solution)/shard_map/ppermute | solution.py:459
  19.1 8.3 %collective-permute-start.9 = (bf16[4,128,128]{2,1,0:T(8,128)(2,1)S(1)}, bf16[4,128,128]{2,1,0:T(8,128)(2,1)S(1)}, u32[]{:S(2)}, u32[]{:S(2)}) collective-permute-start(bf16[4,128,128]{2,1,0:T(8,128)(2,1)S(1)} %get-tuple-element.26), channel_id=1, source_target_pairs={{0,24},{4,28},{8,16},{12,20},{16,8},{20,12},{24,0},{28,4},{1,25},{... | collective-permute-start | bytes 393224 | tf_op jit(solution)/shard_map/ppermute | solution.py:459
  29.6 9.7 %collective-permute-start.11 = (f32[8,128]{1,0:T(8,128)S(1)}, f32[8,128]{1,0:T(8,128)S(1)}, u32[]{:S(2)}, u32[]{:S(2)}) collective-permute-start(f32[8,128]{1,0:T(8,128)S(1)} %broadcast_select_fusion), channel_id=1, source_target_pairs={{0,2},{1,3},{2,0},{3,1},{4,6},{5,7},{6,4},{7,5},{8,10},{9,11},{10,... | collective-permute-start | bytes 12296 | tf_op jit(solution)/shard_map/ppermute | solution.py:575
  32.2 7.1 %collective-permute-start.12 = (f32[8,128]{1,0:T(8,128)S(1)}, f32[8,128]{1,0:T(8,128)S(1)}, u32[]{:S(2)}, u32[]{:S(2)}) collective-permute-start(f32[8,128]{1,0:T(8,128)S(1)} %broadcast_select_fusion), channel_id=1, source_target_pairs={{0,3},{1,2},{2,1},{3,0},{4,7},{5,6},{6,5},{7,4},{8,11},{9,10},{10,... | collective-permute-start | bytes 12296 | tf_op jit(solution)/shard_map/ppermute | solution.py:575
  33.6 5.7 %collective-permute-start.10 = (f32[8,128]{1,0:T(8,128)S(1)}, f32[8,128]{1,0:T(8,128)S(1)}, u32[]{:S(2)}, u32[]{:S(2)}) collective-permute-start(f32[8,128]{1,0:T(8,128)S(1)} %broadcast_select_fusion), channel_id=1, source_target_pairs={{0,1},{1,0},{2,3},{3,2},{4,5},{5,4},{6,7},{7,6},{8,9},{9,8},{10,11... | collective-permute-start | bytes 12296 | tf_op jit(solution)/shard_map/ppermute | solution.py:575

commit v7 on v6

--- a/solution.py
+++ b/solution.py
@@ -502,9 +502,13 @@
     return arrived, keys, source_of
 
 
-def unpack_kernel(heads, power_rows, tail_row, scale, gathered_ref, *out_refs):
+def unpack_kernel(heads, power_rows, tail_row, scale, gathered_ref, *refs):
+    *out_refs, held_ref, sems = refs
     places, _, dim = gathered_ref.shape
     features = out_refs[0].shape[1]
+    runs = sems.shape[1]
+    per = places // runs
+    copies = []
 
     def row(p, i):
         return gathered_ref[p, i : i + 1, :]
@@ -514,22 +518,35 @@
         near_one = row(p, tail_row + 1) + row(p, tail_row + 2) * (1.0 / 1024.0)
         energy = energy + near_one * jnp.exp2(row(p, tail_row))
     scale = scale / energy
-    for p in range(places):
-        for h in range(heads):
-            factor = jnp.exp2(row(p, power_rows[h])) * scale
-            for i, out_ref in enumerate(out_refs):
-                rows = pl.ds((i * heads + h) * features, features)
-                out_ref[p * heads + h] = gathered_ref[p, rows, :] * factor
+    for run in range(runs):
+        for p in range(run * per, (run + 1) * per):
+            for h in range(heads):
+                factor = jnp.exp2(row(p, power_rows[h])) * scale
+                for i in range(2):
+                    rows = pl.ds((i * heads + h) * features, features)
+                    held_ref[i, p * heads + h] = gathered_ref[p, rows, :] * factor
+        done = pl.ds(run * per * heads, per * heads)
+        for i, out_ref in enumerate(out_refs):
+            copy = pltpu.make_async_copy(held_ref.at[i, done], out_ref.at[done], sems.at[i, run])
+            copy.start()
+            copies.append(copy)
+    for copy in copies:
+        copy.wait()
 
 
 def unpack_call(gathered, heads, features, power_rows, tail_row, scale):
     places, _, dim = gathered.shape
+    runs = 4 if places % 4 == 0 else 1
     whole = pl.BlockSpec(memory_space=pltpu.VMEM)
     return pl.pallas_call(
         functools.partial(unpack_kernel, heads, power_rows, tail_row, scale),
         in_specs=[whole],
-        out_specs=[whole, whole],
+        out_specs=[pl.BlockSpec(memory_space=pl.ANY)] * 2,
         out_shape=[jax.ShapeDtypeStruct((places * heads, features, dim), F32)] * 2,
+        scratch_shapes=[
+            pltpu.VMEM((2, places * heads, features, dim), F32),
+            pltpu.SemaphoreType.DMA((2, runs)),
+        ],
         compiler_params=pltpu.CompilerParams(vmem_limit_bytes=VMEM_LIMIT),
     )(gathered)
 

time: 52.3 us -> 52.5 us (level)
  no operation moved by 1% of the time
where the time goes in v7:
time: 52.5 us; the launch traced here: 52.3 us
  starting transfers between devices  16.4 us (31%)
  Pallas kernels  15.7 us (30%)
  blocking collectives  11.1 us (21%)
  waiting for transfers between devices  4.33 us (8%)
  local copies, waits for them, and re-layouts  2.99 us (6%)
  between operations  1.27 us (2%)
    ppermute x8, starting transfers between devices, send(): lax.ppermute(a, 'ctx', [(i, target_of(i // cores, j) * cores + i % cores)...  11.6 us
    all_gather x1, blocking collectives, on_device(): lax.all_gather(jnp.pad(sent, ((0, -used % 16), (0, 0))), 'ctx').astype(F32)  11.1 us
    pallas_call x1, Pallas kernels, both_call(): pl.pallas_call(functools.partial(both_kernel, (places, cores, heads, True...  6.85 us
    pallas_call x1, Pallas kernels, student_call(): pl.pallas_call(functools.partial(student_kernel, start, heads), in_specs=...  5.31 us
    ppermute x3, starting transfers between devices, on_device(): lax.ppermute(energy, 'head', [(i, partner(i, k, planes)) for i in range(p...  4.18 us
    ppermute x8, waiting for transfers between devices, send(): lax.ppermute(a, 'ctx', [(i, target_of(i // cores, j) * cores + i % cores)...  4.15 us
    pallas_call x1, Pallas kernels, teacher_call(): pl.pallas_call(functools.partial(teacher_kernel, (places, cores, heads, w...  2.15 us
    transpose x1, local copies, waits for them, and re-layouts, exchange(): by_head.transpose(1, 0, 2).reshape(chips, cores, heads, tokens, dim)  1.66 us
  transfers between devices with their start and end apart: 13, of which 2 were waited for; matrix products, arithmetic and copies ran while one was open for 3% of the time, Pallas kernels for 23%

profile of v7, /device:TPU:0, one launch (start us, length us, event | category | flops | bytes accessed | tf_op | source)
XLA Modules:
  0.0 52.3 jit_solution(5550863798859212138)
XLA Ops:
  0.6 0.0 copy-start
  0.6 0.0 copy-start.1
  0.7 1.7 %copy.7 = bf16[32,128,128]{2,1,0:T(8,128)(2,1)S(1)} copy(bf16[32,128,128]{2,0,1:T(8,128)(2,1)} %bitcast.78) | data formatting | bytes 2097152 | tf_op jit(solution)/shard_map/transpose | solution.py:470
  2.4 0.5 collective-permute-start
  2.9 0.0 copy-done
  2.9 0.0 copy-done.1
  3.2 1.0 %dynamic-slice_bitcast_fusion.1 = (f32[4,64,128]{2,1,0:T(8,128)S(1)}, f32[4,64,128]{2,1,0:T(8,128)S(1)}) fusion(f32[32,128,64]{1,2,0:T(8,128)} %param.9, s32[]{:T(128)S(6)} %select_n.118, f32[32,128,64]{1,2,0:T(8,128)} %param.8), kind=kLoop, calls=%fused_computation.11 | loop fusion | bytes 524292 | tf_op jit(solution)/shard_map/dynamic_slice | solution.py:571
  4.2 0.1 dynamic-slice_bitcast_fusion.4
  4.3 0.2 collective-permute-done
  4.5 3.9 %collective-permute-start.5 = (bf16[2,128,128]{2,1,0:T(8,128)(2,1)S(1)}, bf16[2,128,128]{2,1,0:T(8,128)(2,1)S(1)}, u32[]{:S(2)}, u32[]{:S(2)}) collective-permute-start(bf16[2,128,128]{2,1,0:T(8,128)(2,1)S(1)} %get-tuple-element.51), channel_id=1, source_target_pairs={{0,24},{4,28},{8,16},{12,20},{16,8},{20,12},{24,0},{28,4},{1,25},{... | collective-permute-start | bytes 196616 | tf_op jit(solution)/shard_map/ppermute | solution.py:459
  8.4 0.5 collective-permute-start.4
  8.9 0.2 collective-permute-start.1
  9.2 2.0 %collective-permute-start.2 = (bf16[4,128,128]{2,1,0:T(8,128)(2,1)S(1)}, bf16[4,128,128]{2,1,0:T(8,128)(2,1)S(1)}, u32[]{:S(2)}, u32[]{:S(2)}) collective-permute-start(bf16[4,128,128]{2,1,0:T(8,128)(2,1)S(1)} %pad_maximum_fusion.4), channel_id=1, source_target_pairs={{0,16},{4,20},{8,24},{12,28},{16,0},{20,4},{24,8},{28,12},{1,17},{... | collective-permute-start | bytes 393224 | tf_op jit(solution)/shard_map/ppermute | solution.py:459
  11.2 1.5 %collective-permute-start.3 = (bf16[4,128,128]{2,1,0:T(8,128)(2,1)S(1)}, bf16[4,128,128]{2,1,0:T(8,128)(2,1)S(1)}, u32[]{:S(2)}, u32[]{:S(2)}) collective-permute-start(bf16[4,128,128]{2,1,0:T(8,128)(2,1)S(1)} %pad_maximum_fusion.5), channel_id=1, source_target_pairs={{0,24},{4,28},{8,16},{12,20},{16,8},{20,12},{24,0},{28,4},{1,25},{... | collective-permute-start | bytes 393224 | tf_op jit(solution)/shard_map/ppermute | solution.py:459
  12.7 4.1 %collective-permute-done.1.refs_1_ = bf16[6,128,128]{2,1,0:T(8,128)(2,1)S(1)} collective-permute-done((bf16[6,128,128]{2,1,0:T(8,128)(2,1)S(1)}, bf16[6,128,128]{2,1,0:T(8,128)(2,1)S(1)}, u32[]{:S(2)}, u32[]{:S(2)}) %collective-permute-start.1) | collective-permute-done | bytes 196640 | tf_op jit(solution)/shard_map/ppermute | solution.py:459
  16.8 0.0 collective-permute-done.5
  16.8 0.0 collective-permute-done.4
  16.9 0.1 collective-permute-start.6
  17.0 0.8 %collective-permute-start.7 = (bf16[4,128,128]{2,1,0:T(8,128)(2,1)S(1)}, bf16[4,128,128]{2,1,0:T(8,128)(2,1)S(1)}, u32[]{:S(2)}, u32[]{:S(2)}) collective-permute-start(bf16[4,128,128]{2,1,0:T(8,128)(2,1)S(1)} %get-tuple-element.24), channel_id=1, source_target_pairs={{0,8},{4,12},{8,0},{12,4},{16,24},{20,28},{24,16},{28,20},{1,9},{5... | collective-permute-start | bytes 393224 | tf_op jit(solution)/shard_map/ppermute | solution.py:459
  17.8 1.3 %collective-permute-start.8 = (bf16[4,128,128]{2,1,0:T(8,128)(2,1)S(1)}, bf16[4,128,128]{2,1,0:T(8,128)(2,1)S(1)}, u32[]{:S(2)}, u32[]{:S(2)}) collective-permute-start(bf16[4,128,128]{2,1,0:T(8,128)(2,1)S(1)} %get-tuple-element.25), channel_id=1, source_target_pairs={{0,16},{4,20},{8,24},{12,28},{16,0},{20,4},{24,8},{28,12},{1,17},{... | collective-permute-start | bytes 393224 | tf_op jit(solution)/shard_map/ppermute | solution.py:459
  19.1 0.0 collective-permute-done.2.refs_2_
  19.1 1.4 %collective-permute-start.9 = (bf16[4,128,128]{2,1,0:T(8,128)(2,1)S(1)}, bf16[4,128,128]{2,1,0:T(8,128)(2,1)S(1)}, u32[]{:S(2)}, u32[]{:S(2)}) collective-permute-start(bf16[4,128,128]{2,1,0:T(8,128)(2,1)S(1)} %get-tuple-element.26), channel_id=1, source_target_pairs={{0,24},{4,28},{8,16},{12,20},{16,8},{20,12},{24,0},{28,4},{1,25},{... | collective-permute-start | bytes 393224 | tf_op jit(solution)/shard_map/ppermute | solution.py:459
  20.6 0.0 collective-permute-done.3.refs_3_
  20.6 0.0 collective-permute-done.6.refs_5_
  20.6 6.8 %shard_map.68 = (bf16[8,2,128,128]{3,2,1,0:T(8,128)(2,1)S(1)}, f32[8,128]{1,0:T(8,128)S(1)}, f32[264,128]{1,0:T(8,128)S(1)}) custom-call(s32[1]{0:T(128)} %bitcast.place_ref, bf16[4,128,128]{2,1,0:T(8,128)(2,1)S(1)} %pad_maximum_fusion.2.refs_0_, bf16[6,128,128]{2,1,0:T(8,128)(2,1)S(1)} %collective-permute-done.1.refs_1_, ...), custom_call_target="tpu_custom_call" | custom-call | flops 9395240960 | bytes 5242880 | tf_op jit(solution)/shard_map/pallas_call | solution.py:410
  27.4 0.0 collective-permute-done.7.refs_1_
  27.5 0.0 collective-permute-done.8.refs_2_
  27.5 0.0 collective-permute-done.9.refs_3_
  27.5 2.1 %shard_map.69 = (bf16[8,2,128,128]{3,2,1,0:T(8,128)(2,1)S(1)}, f32[8,2,128,128]{3,2,1,0:T(8,128)S(1)}, f32[8,128]{1,0:T(8,128)S(1)}) custom-call(s32[1]{0:T(128)} %bitcast.place_ref, bf16[4,128,128]{2,1,0:T(8,128)(2,1)S(1)} %get-tuple-element.23.refs_0_, bf16[4,128,128]{2,1,0:T(8,128)(2,1)S(1)} %collective-permute-done.7.refs_1_, ...), custom_call_target="tpu_custom_call" | custom-call | flops 2684354560 | bytes 2097152 | tf_op jit(solution)/shard_map/pallas_call | solution.py:155
  29.6 2.6 %collective-permute-start.11 = (f32[8,128]{1,0:T(8,128)S(1)}, f32[8,128]{1,0:T(8,128)S(1)}, u32[]{:S(2)}, u32[]{:S(2)}) collective-permute-start(f32[8,128]{1,0:T(8,128)S(1)} %broadcast_select_fusion), channel_id=1, source_target_pairs={{0,2},{1,3},{2,0},{3,1},{4,6},{5,7},{6,4},{7,5},{8,10},{9,11},{10,... | collective-permute-start | bytes 12296 | tf_op jit(solution)/shard_map/ppermute | solution.py:592
  32.2 1.3 %collective-permute-start.12 = (f32[8,128]{1,0:T(8,128)S(1)}, f32[8,128]{1,0:T(8,128)S(1)}, u32[]{:S(2)}, u32[]{:S(2)}) collective-permute-start(f32[8,128]{1,0:T(8,128)S(1)} %broadcast_select_fusion), channel_id=1, source_target_pairs={{0,3},{1,2},{2,1},{3,0},{4,7},{5,6},{6,5},{7,4},{8,11},{9,10},{10,... | collective-permute-start | bytes 12296 | tf_op jit(solution)/shard_map/ppermute | solution.py:592
  33.6 0.2 collective-permute-start.10
  33.8 5.3 %shard_map.70 = f32[264,128]{1,0:T(8,128)S(1)} custom-call(bf16[8,2,128,128]{3,2,1,0:T(8,128)(2,1)S(1)} %get-tuple-element.29.x_ref, bf16[8,2,128,128]{3,2,1,0:T(8,128)(2,1)S(1)} %get-tuple-element.27.refs_4_.kv_ref, f32[8,2,128,128]{3,2,1,0:T(8,128)S(1)} %get-tuple-element.30.teacher_ref, f32[4,64,128]{2,1,0:T(8,128)S(1)} %get-tuple-element.65.refs_6_.mq_ref, ...), custom_call_target="tpu_custom_call" | custom-call | flops 6710886400 | bytes 3145728 | tf_op jit(solution)/shard_map/pallas_call | solution.py:370
  39.3 0.0 collective-permute-done.11
  39.3 0.0 collective-permute-done.12
  39.3 0.0 collective-permute-done.10
  39.3 0.1 constant_dynamic-update-slice_fusion
  39.4 11.1 %all-gather.2 = f16[4352,128]{1,0:T(8,128)(2,1)S(1)} all-gather(f16[544,128]{1,0:T(8,128)(2,1)S(1)} %pad.4), channel_id=2, replica_groups=mesh['ctx'=8,'head'=4] {'ctx'}, dimensions={0}, use_global_device_ids=true | all-gather | bytes 1253376 | tf_op jit(solution)/shard_map/all_gather | solution.py:604
  50.5 0.1 convert.22.gathered_ref
  50.7 1.4 %shard_map.71 = (f32[32,64,128]{2,1,0:T(8,128)}, f32[32,64,128]{2,1,0:T(8,128)}) custom-call(f32[8,544,128]{2,1,0:T(8,128)S(1)} %convert.22.gathered_ref), custom_call_target="tpu_custom_call" | custom-call | tf_op jit(solution)/shard_map/pallas_call | solution.py:541
  (28 shorter events, 0.5 us)
Async XLA Ops:
  0.6 2.3 %copy-start = (bf16[128,2,128]{2,1,0:T(2,128)(2,1)S(1)}, bf16[128,2,128]{2,1,0:T(2,128)(2,1)}, u32[]{:S(2)}) copy-start(bf16[128,2,128]{2,1,0:T(2,128)(2,1)} %param.7) | copy-start | bytes 196612
  0.6 2.3 %copy-start.1 = (bf16[128,2,128]{2,1,0:T(2,128)(2,1)S(1)}, bf16[128,2,128]{2,1,0:T(2,128)(2,1)}, u32[]{:S(2)}) copy-start(bf16[128,2,128]{2,1,0:T(2,128)(2,1)} %param.6) | copy-start | bytes 196612
  2.4 2.1 %collective-permute-start = (bf16[4,4,128,128]{3,2,1,0:T(8,128)(2,1)S(1)}, bf16[4,4,128,128]{3,2,1,0:T(8,128)(2,1)S(1)}, u32[]{:S(2)}, u32[]{:S(2)}) collective-permute-start(bf16[4,4,128,128]{3,2,1,0:T(8,128)(2,1)S(1)} %dynamic-slice_bitcast_fusion), channel_id=1, source_target_pairs={{0,4},{4,0},{8,12},{12,8},{16,20},{20,16},{24,28},{28,24},{1,5},{5... | collective-permute-start | bytes 1572872 | tf_op jit(solution)/shard_map/ppermute | solution.py:464
  4.5 12.3 %collective-permute-start.5 = (bf16[2,128,128]{2,1,0:T(8,128)(2,1)S(1)}, bf16[2,128,128]{2,1,0:T(8,128)(2,1)S(1)}, u32[]{:S(2)}, u32[]{:S(2)}) collective-permute-start(bf16[2,128,128]{2,1,0:T(8,128)(2,1)S(1)} %get-tuple-element.51), channel_id=1, source_target_pairs={{0,24},{4,28},{8,16},{12,20},{16,8},{20,12},{24,0},{28,4},{1,25},{... | collective-permute-start | bytes 196616 | tf_op jit(solution)/shard_map/ppermute | solution.py:459
  8.4 8.4 %collective-permute-start.4 = (bf16[2,128,128]{2,1,0:T(8,128)(2,1)S(1)}, bf16[2,128,128]{2,1,0:T(8,128)(2,1)S(1)}, u32[]{:S(2)}, u32[]{:S(2)}) collective-permute-start(bf16[2,128,128]{2,1,0:T(8,128)(2,1)S(1)} %get-tuple-element.52), channel_id=1, source_target_pairs={{0,16},{4,20},{8,24},{12,28},{16,0},{20,4},{24,8},{28,12},{1,17},{... | collective-permute-start | bytes 196616 | tf_op jit(solution)/shard_map/ppermute | solution.py:459
  8.9 7.9 %collective-permute-start.1 = (bf16[6,128,128]{2,1,0:T(8,128)(2,1)S(1)}, bf16[6,128,128]{2,1,0:T(8,128)(2,1)S(1)}, u32[]{:S(2)}, u32[]{:S(2)}) collective-permute-start(bf16[6,128,128]{2,1,0:T(8,128)(2,1)S(1)} %pad_maximum_fusion.1), channel_id=1, source_target_pairs={{0,8},{4,12},{8,0},{12,4},{16,24},{20,28},{24,16},{28,20},{1,9},{5... | collective-permute-start | bytes 589832 | tf_op jit(solution)/shard_map/ppermute | solution.py:459
  9.2 10.0 %collective-permute-start.2 = (bf16[4,128,128]{2,1,0:T(8,128)(2,1)S(1)}, bf16[4,128,128]{2,1,0:T(8,128)(2,1)S(1)}, u32[]{:S(2)}, u32[]{:S(2)}) collective-permute-start(bf16[4,128,128]{2,1,0:T(8,128)(2,1)S(1)} %pad_maximum_fusion.4), channel_id=1, source_target_pairs={{0,16},{4,20},{8,24},{12,28},{16,0},{20,4},{24,8},{28,12},{1,17},{... | collective-permute-start | bytes 393224 | tf_op jit(solution)/shard_map/ppermute | solution.py:459
  11.2 9.4 %collective-permute-start.3 = (bf16[4,128,128]{2,1,0:T(8,128)(2,1)S(1)}, bf16[4,128,128]{2,1,0:T(8,128)(2,1)S(1)}, u32[]{:S(2)}, u32[]{:S(2)}) collective-permute-start(bf16[4,128,128]{2,1,0:T(8,128)(2,1)S(1)} %pad_maximum_fusion.5), channel_id=1, source_target_pairs={{0,24},{4,28},{8,16},{12,20},{16,8},{20,12},{24,0},{28,4},{1,25},{... | collective-permute-start | bytes 393224 | tf_op jit(solution)/shard_map/ppermute | solution.py:459
  16.9 3.7 %collective-permute-start.6 = (bf16[4,2,128,128]{3,2,1,0:T(8,128)(2,1)S(1)}, bf16[4,2,128,128]{3,2,1,0:T(8,128)(2,1)S(1)}, u32[]{:S(2)}, u32[]{:S(2)}) collective-permute-start(bf16[4,2,128,128]{3,2,1,0:T(8,128)(2,1)S(1)} %pad_maximum_fusion.refs_4_), channel_id=1, source_target_pairs={{0,4},{4,0},{8,12},{12,8},{16,20},{20,16},{24,28},{28,24},{1,5},{5... | collective-permute-start | bytes 786440 | tf_op jit(solution)/shard_map/ppermute | solution.py:464
  17.0 10.4 %collective-permute-start.7 = (bf16[4,128,128]{2,1,0:T(8,128)(2,1)S(1)}, bf16[4,128,128]{2,1,0:T(8,128)(2,1)S(1)}, u32[]{:S(2)}, u32[]{:S(2)}) collective-permute-start(bf16[4,128,128]{2,1,0:T(8,128)(2,1)S(1)} %get-tuple-element.24), channel_id=1, source_target_pairs={{0,8},{4,12},{8,0},{12,4},{16,24},{20,28},{24,16},{28,20},{1,9},{5... | collective-permute-start | bytes 393224 | tf_op jit(solution)/shard_map/ppermute | solution.py:459
  17.8 9.7 %collective-permute-start.8 = (bf16[4,128,128]{2,1,0:T(8,128)(2,1)S(1)}, bf16[4,128,128]{2,1,0:T(8,128)(2,1)S(1)}, u32[]{:S(2)}, u32[]{:S(2)}) collective-permute-start(bf16[4,128,128]{2,1,0:T(8,128)(2,1)S(1)} %get-tuple-element.25), channel_id=1, source_target_pairs={{0,16},{4,20},{8,24},{12,28},{16,0},{20,4},{24,8},{28,12},{1,17},{... | collective-permute-start | bytes 393224 | tf_op jit(solution)/shard_map/ppermute | solution.py:459
  19.1 8.3 %collective-permute-start.9 = (bf16[4,128,128]{2,1,0:T(8,128)(2,1)S(1)}, bf16[4,128,128]{2,1,0:T(8,128)(2,1)S(1)}, u32[]{:S(2)}, u32[]{:S(2)}) collective-permute-start(bf16[4,128,128]{2,1,0:T(8,128)(2,1)S(1)} %get-tuple-element.26), channel_id=1, source_target_pairs={{0,24},{4,28},{8,16},{12,20},{16,8},{20,12},{24,0},{28,4},{1,25},{... | collective-permute-start | bytes 393224 | tf_op jit(solution)/shard_map/ppermute | solution.py:459
  29.6 9.7 %collective-permute-start.11 = (f32[8,128]{1,0:T(8,128)S(1)}, f32[8,128]{1,0:T(8,128)S(1)}, u32[]{:S(2)}, u32[]{:S(2)}) collective-permute-start(f32[8,128]{1,0:T(8,128)S(1)} %broadcast_select_fusion), channel_id=1, source_target_pairs={{0,2},{1,3},{2,0},{3,1},{4,6},{5,7},{6,4},{7,5},{8,10},{9,11},{10,... | collective-permute-start | bytes 12296 | tf_op jit(solution)/shard_map/ppermute | solution.py:592
  32.2 7.1 %collective-permute-start.12 = (f32[8,128]{1,0:T(8,128)S(1)}, f32[8,128]{1,0:T(8,128)S(1)}, u32[]{:S(2)}, u32[]{:S(2)}) collective-permute-start(f32[8,128]{1,0:T(8,128)S(1)} %broadcast_select_fusion), channel_id=1, source_target_pairs={{0,3},{1,2},{2,1},{3,0},{4,7},{5,6},{6,5},{7,4},{8,11},{9,10},{10,... | collective-permute-start | bytes 12296 | tf_op jit(solution)/shard_map/ppermute | solution.py:592
  33.6 5.7 %collective-permute-start.10 = (f32[8,128]{1,0:T(8,128)S(1)}, f32[8,128]{1,0:T(8,128)S(1)}, u32[]{:S(2)}, u32[]{:S(2)}) collective-permute-start(f32[8,128]{1,0:T(8,128)S(1)} %broadcast_select_fusion), channel_id=1, source_target_pairs={{0,1},{1,0},{2,3},{3,2},{4,5},{5,4},{6,7},{7,6},{8,9},{9,8},{10,11... | collective-permute-start | bytes 12296 | tf_op jit(solution)/shard_map/ppermute | solution.py:592

commit v8 on v7

--- a/solution.py
+++ b/solution.py
@@ -587,7 +587,8 @@
         rows = (stop - start) * features
         grads.append((result[:rows], result[rows : 2 * rows]))
         powers.append(result[2 * rows :])
-    energy = jnp.where(place * heads < query_heads, energy, 0.0)
+    if padding:
+        energy = jnp.where(place * heads < query_heads, energy, 0.0)
     shifted = [
         lax.ppermute(energy, "head", [(i, partner(i, k, planes)) for i in range(planes)])
         for k in range(1, planes)

time: 52.5 us -> 52.7 us (level)
  no operation moved by 1% of the time
where the time goes in v8:
time: 52.7 us; the launch traced here: 52.5 us
  starting transfers between devices  16.6 us (31%)
  Pallas kernels  15.7 us (30%)
  blocking collectives  11.1 us (21%)
  waiting for transfers between devices  4.33 us (8%)
  local copies, waits for them, and re-layouts  2.99 us (6%)
  between operations  1.27 us (2%)
    ppermute x8, starting transfers between devices, send(): lax.ppermute(a, 'ctx', [(i, target_of(i // cores, j) * cores + i % cores)...  11.6 us
    all_gather x1, blocking collectives, on_device(): lax.all_gather(jnp.pad(sent, ((0, -used % 16), (0, 0))), 'ctx').astype(F32)  11.1 us
    pallas_call x1, Pallas kernels, both_call(): pl.pallas_call(functools.partial(both_kernel, (places, cores, heads, True...  6.85 us
    pallas_call x1, Pallas kernels, student_call(): pl.pallas_call(functools.partial(student_kernel, start, heads), in_specs=...  5.3 us
    ppermute x3, starting transfers between devices, on_device(): lax.ppermute(energy, 'head', [(i, partner(i, k, planes)) for i in range(p...  4.39 us
    ppermute x8, waiting for transfers between devices, send(): lax.ppermute(a, 'ctx', [(i, target_of(i // cores, j) * cores + i % cores)...  4.15 us
    pallas_call x1, Pallas kernels, teacher_call(): pl.pallas_call(functools.partial(teacher_kernel, (places, cores, heads, w...  2.15 us
    transpose x1, local copies, waits for them, and re-layouts, exchange(): by_head.transpose(1, 0, 2).reshape(chips, cores, heads, tokens, dim)  1.66 us
  transfers between devices with their start and end apart: 13, of which 2 were waited for; matrix products, arithmetic and copies ran while one was open for 3% of the time, Pallas kernels for 23%

profile of v8, /device:TPU:0, one launch (start us, length us, event | category | flops | bytes accessed | tf_op | source)
XLA Modules:
  0.0 52.5 jit_solution(15067755033017234123)
XLA Ops:
  0.6 0.0 copy-start
  0.6 0.0 copy-start.1
  0.7 1.7 %copy.7 = bf16[32,128,128]{2,1,0:T(8,128)(2,1)S(1)} copy(bf16[32,128,128]{2,0,1:T(8,128)(2,1)} %bitcast.78) | data formatting | bytes 2097152 | tf_op jit(solution)/shard_map/transpose | solution.py:470
  2.4 0.5 collective-permute-start
  2.9 0.0 copy-done
  2.9 0.0 copy-done.1
  3.2 1.0 %dynamic-slice_bitcast_fusion.1 = (f32[4,64,128]{2,1,0:T(8,128)S(1)}, f32[4,64,128]{2,1,0:T(8,128)S(1)}) fusion(f32[32,128,64]{1,2,0:T(8,128)} %param.9, s32[]{:T(128)S(6)} %select_n.110, f32[32,128,64]{1,2,0:T(8,128)} %param.8), kind=kLoop, calls=%fused_computation.11 | loop fusion | bytes 524292 | tf_op jit(solution)/shard_map/dynamic_slice | solution.py:571
  4.2 0.1 dynamic-slice_bitcast_fusion.4
  4.3 0.2 collective-permute-done
  4.5 3.9 %collective-permute-start.5 = (bf16[2,128,128]{2,1,0:T(8,128)(2,1)S(1)}, bf16[2,128,128]{2,1,0:T(8,128)(2,1)S(1)}, u32[]{:S(2)}, u32[]{:S(2)}) collective-permute-start(bf16[2,128,128]{2,1,0:T(8,128)(2,1)S(1)} %get-tuple-element.51), channel_id=1, source_target_pairs={{0,24},{4,28},{8,16},{12,20},{16,8},{20,12},{24,0},{28,4},{1,25},{... | collective-permute-start | bytes 196616 | tf_op jit(solution)/shard_map/ppermute | solution.py:459
  8.4 0.5 collective-permute-start.4
  8.9 0.2 collective-permute-start.1
  9.2 2.0 %collective-permute-start.2 = (bf16[4,128,128]{2,1,0:T(8,128)(2,1)S(1)}, bf16[4,128,128]{2,1,0:T(8,128)(2,1)S(1)}, u32[]{:S(2)}, u32[]{:S(2)}) collective-permute-start(bf16[4,128,128]{2,1,0:T(8,128)(2,1)S(1)} %pad_maximum_fusion.4), channel_id=1, source_target_pairs={{0,16},{4,20},{8,24},{12,28},{16,0},{20,4},{24,8},{28,12},{1,17},{... | collective-permute-start | bytes 393224 | tf_op jit(solution)/shard_map/ppermute | solution.py:459
  11.2 1.5 %collective-permute-start.3 = (bf16[4,128,128]{2,1,0:T(8,128)(2,1)S(1)}, bf16[4,128,128]{2,1,0:T(8,128)(2,1)S(1)}, u32[]{:S(2)}, u32[]{:S(2)}) collective-permute-start(bf16[4,128,128]{2,1,0:T(8,128)(2,1)S(1)} %pad_maximum_fusion.5), channel_id=1, source_target_pairs={{0,24},{4,28},{8,16},{12,20},{16,8},{20,12},{24,0},{28,4},{1,25},{... | collective-permute-start | bytes 393224 | tf_op jit(solution)/shard_map/ppermute | solution.py:459
  12.7 4.1 %collective-permute-done.1.refs_1_ = bf16[6,128,128]{2,1,0:T(8,128)(2,1)S(1)} collective-permute-done((bf16[6,128,128]{2,1,0:T(8,128)(2,1)S(1)}, bf16[6,128,128]{2,1,0:T(8,128)(2,1)S(1)}, u32[]{:S(2)}, u32[]{:S(2)}) %collective-permute-start.1) | collective-permute-done | bytes 196640 | tf_op jit(solution)/shard_map/ppermute | solution.py:459
  16.8 0.0 collective-permute-done.5
  16.8 0.0 collective-permute-done.4
  16.9 0.1 collective-permute-start.6
  17.0 0.8 %collective-permute-start.7 = (bf16[4,128,128]{2,1,0:T(8,128)(2,1)S(1)}, bf16[4,128,128]{2,1,0:T(8,128)(2,1)S(1)}, u32[]{:S(2)}, u32[]{:S(2)}) collective-permute-start(bf16[4,128,128]{2,1,0:T(8,128)(2,1)S(1)} %get-tuple-element.24), channel_id=1, source_target_pairs={{0,8},{4,12},{8,0},{12,4},{16,24},{20,28},{24,16},{28,20},{1,9},{5... | collective-permute-start | bytes 393224 | tf_op jit(solution)/shard_map/ppermute | solution.py:459
  17.8 1.3 %collective-permute-start.8 = (bf16[4,128,128]{2,1,0:T(8,128)(2,1)S(1)}, bf16[4,128,128]{2,1,0:T(8,128)(2,1)S(1)}, u32[]{:S(2)}, u32[]{:S(2)}) collective-permute-start(bf16[4,128,128]{2,1,0:T(8,128)(2,1)S(1)} %get-tuple-element.25), channel_id=1, source_target_pairs={{0,16},{4,20},{8,24},{12,28},{16,0},{20,4},{24,8},{28,12},{1,17},{... | collective-permute-start | bytes 393224 | tf_op jit(solution)/shard_map/ppermute | solution.py:459
  19.1 0.0 collective-permute-done.2.refs_2_
  19.1 1.4 %collective-permute-start.9 = (bf16[4,128,128]{2,1,0:T(8,128)(2,1)S(1)}, bf16[4,128,128]{2,1,0:T(8,128)(2,1)S(1)}, u32[]{:S(2)}, u32[]{:S(2)}) collective-permute-start(bf16[4,128,128]{2,1,0:T(8,128)(2,1)S(1)} %get-tuple-element.26), channel_id=1, source_target_pairs={{0,24},{4,28},{8,16},{12,20},{16,8},{20,12},{24,0},{28,4},{1,25},{... | collective-permute-start | bytes 393224 | tf_op jit(solution)/shard_map/ppermute | solution.py:459
  20.6 0.0 collective-permute-done.3.refs_3_
  20.6 0.0 collective-permute-done.6.refs_5_
  20.6 6.8 %shard_map.68 = (bf16[8,2,128,128]{3,2,1,0:T(8,128)(2,1)S(1)}, f32[8,128]{1,0:T(8,128)S(1)}, f32[264,128]{1,0:T(8,128)S(1)}) custom-call(s32[1]{0:T(128)} %bitcast.place_ref, bf16[4,128,128]{2,1,0:T(8,128)(2,1)S(1)} %pad_maximum_fusion.2.refs_0_, bf16[6,128,128]{2,1,0:T(8,128)(2,1)S(1)} %collective-permute-done.1.refs_1_, ...), custom_call_target="tpu_custom_call" | custom-call | flops 9395240960 | bytes 5242880 | tf_op jit(solution)/shard_map/pallas_call | solution.py:410
  27.4 0.0 collective-permute-done.7.refs_1_
  27.5 0.0 collective-permute-done.8.refs_2_
  27.5 0.0 collective-permute-done.9.refs_3_
  27.5 2.1 %shard_map.69 = (bf16[8,2,128,128]{3,2,1,0:T(8,128)(2,1)S(1)}, f32[8,2,128,128]{3,2,1,0:T(8,128)S(1)}, f32[8,128]{1,0:T(8,128)S(1)}) custom-call(s32[1]{0:T(128)} %bitcast.place_ref, bf16[4,128,128]{2,1,0:T(8,128)(2,1)S(1)} %get-tuple-element.23.refs_0_, bf16[4,128,128]{2,1,0:T(8,128)(2,1)S(1)} %collective-permute-done.7.refs_1_, ...), custom_call_target="tpu_custom_call" | custom-call | flops 2684354560 | bytes 2097152 | tf_op jit(solution)/shard_map/pallas_call | solution.py:155
  29.6 3.6 %collective-permute-start.12 = (f32[8,128]{1,0:T(8,128)S(1)}, f32[8,128]{1,0:T(8,128)S(1)}, u32[]{:S(2)}, u32[]{:S(2)}) collective-permute-start(f32[8,128]{1,0:T(8,128)S(1)} %get-tuple-element.31), channel_id=1, source_target_pairs={{0,3},{1,2},{2,1},{3,0},{4,7},{5,6},{6,5},{7,4},{8,11},{9,10},{10,... | collective-permute-start | bytes 12296 | tf_op jit(solution)/shard_map/ppermute | solution.py:593
  33.2 0.0 collective-permute-start.11
  33.2 0.8 %collective-permute-start.10 = (f32[8,128]{1,0:T(8,128)S(1)}, f32[8,128]{1,0:T(8,128)S(1)}, u32[]{:S(2)}, u32[]{:S(2)}) collective-permute-start(f32[8,128]{1,0:T(8,128)S(1)} %get-tuple-element.31), channel_id=1, source_target_pairs={{0,1},{1,0},{2,3},{3,2},{4,5},{5,4},{6,7},{7,6},{8,9},{9,8},{10,11... | collective-permute-start | bytes 12296 | tf_op jit(solution)/shard_map/ppermute | solution.py:593
  34.1 5.3 %shard_map.70 = f32[264,128]{1,0:T(8,128)S(1)} custom-call(bf16[8,2,128,128]{3,2,1,0:T(8,128)(2,1)S(1)} %get-tuple-element.29.x_ref, bf16[8,2,128,128]{3,2,1,0:T(8,128)(2,1)S(1)} %get-tuple-element.27.refs_4_.kv_ref, f32[8,2,128,128]{3,2,1,0:T(8,128)S(1)} %get-tuple-element.30.teacher_ref, f32[4,64,128]{2,1,0:T(8,128)S(1)} %get-tuple-element.65.refs_6_.mq_ref, ...), custom_call_target="tpu_custom_call" | custom-call | flops 6710886400 | bytes 3145728 | tf_op jit(solution)/shard_map/pallas_call | solution.py:370
  39.5 0.0 collective-permute-done.12
  39.5 0.0 collective-permute-done.11
  39.5 0.0 collective-permute-done.10
  39.5 0.1 constant_dynamic-update-slice_fusion
  39.6 11.1 %all-gather.2 = f16[4352,128]{1,0:T(8,128)(2,1)S(1)} all-gather(f16[544,128]{1,0:T(8,128)(2,1)S(1)} %pad.4), channel_id=2, replica_groups=mesh['ctx'=8,'head'=4] {'ctx'}, dimensions={0}, use_global_device_ids=true | all-gather | bytes 1253376 | tf_op jit(solution)/shard_map/all_gather | solution.py:605
  50.7 0.1 convert.22.gathered_ref
  50.9 1.4 %shard_map.71 = (f32[32,64,128]{2,1,0:T(8,128)}, f32[32,64,128]{2,1,0:T(8,128)}) custom-call(f32[8,544,128]{2,1,0:T(8,128)S(1)} %convert.22.gathered_ref), custom_call_target="tpu_custom_call" | custom-call | tf_op jit(solution)/shard_map/pallas_call | solution.py:541
  (27 shorter events, 0.5 us)
Async XLA Ops:
  0.6 2.3 %copy-start = (bf16[128,2,128]{2,1,0:T(2,128)(2,1)S(1)}, bf16[128,2,128]{2,1,0:T(2,128)(2,1)}, u32[]{:S(2)}) copy-start(bf16[128,2,128]{2,1,0:T(2,128)(2,1)} %param.7) | copy-start | bytes 196612
  0.6 2.3 %copy-start.1 = (bf16[128,2,128]{2,1,0:T(2,128)(2,1)S(1)}, bf16[128,2,128]{2,1,0:T(2,128)(2,1)}, u32[]{:S(2)}) copy-start(bf16[128,2,128]{2,1,0:T(2,128)(2,1)} %param.6) | copy-start | bytes 196612
  2.4 2.1 %collective-permute-start = (bf16[4,4,128,128]{3,2,1,0:T(8,128)(2,1)S(1)}, bf16[4,4,128,128]{3,2,1,0:T(8,128)(2,1)S(1)}, u32[]{:S(2)}, u32[]{:S(2)}) collective-permute-start(bf16[4,4,128,128]{3,2,1,0:T(8,128)(2,1)S(1)} %dynamic-slice_bitcast_fusion), channel_id=1, source_target_pairs={{0,4},{4,0},{8,12},{12,8},{16,20},{20,16},{24,28},{28,24},{1,5},{5... | collective-permute-start | bytes 1572872 | tf_op jit(solution)/shard_map/ppermute | solution.py:464
  4.5 12.3 %collective-permute-start.5 = (bf16[2,128,128]{2,1,0:T(8,128)(2,1)S(1)}, bf16[2,128,128]{2,1,0:T(8,128)(2,1)S(1)}, u32[]{:S(2)}, u32[]{:S(2)}) collective-permute-start(bf16[2,128,128]{2,1,0:T(8,128)(2,1)S(1)} %get-tuple-element.51), channel_id=1, source_target_pairs={{0,24},{4,28},{8,16},{12,20},{16,8},{20,12},{24,0},{28,4},{1,25},{... | collective-permute-start | bytes 196616 | tf_op jit(solution)/shard_map/ppermute | solution.py:459
  8.4 8.4 %collective-permute-start.4 = (bf16[2,128,128]{2,1,0:T(8,128)(2,1)S(1)}, bf16[2,128,128]{2,1,0:T(8,128)(2,1)S(1)}, u32[]{:S(2)}, u32[]{:S(2)}) collective-permute-start(bf16[2,128,128]{2,1,0:T(8,128)(2,1)S(1)} %get-tuple-element.52), channel_id=1, source_target_pairs={{0,16},{4,20},{8,24},{12,28},{16,0},{20,4},{24,8},{28,12},{1,17},{... | collective-permute-start | bytes 196616 | tf_op jit(solution)/shard_map/ppermute | solution.py:459
  8.9 7.9 %collective-permute-start.1 = (bf16[6,128,128]{2,1,0:T(8,128)(2,1)S(1)}, bf16[6,128,128]{2,1,0:T(8,128)(2,1)S(1)}, u32[]{:S(2)}, u32[]{:S(2)}) collective-permute-start(bf16[6,128,128]{2,1,0:T(8,128)(2,1)S(1)} %pad_maximum_fusion.1), channel_id=1, source_target_pairs={{0,8},{4,12},{8,0},{12,4},{16,24},{20,28},{24,16},{28,20},{1,9},{5... | collective-permute-start | bytes 589832 | tf_op jit(solution)/shard_map/ppermute | solution.py:459
  9.2 10.0 %collective-permute-start.2 = (bf16[4,128,128]{2,1,0:T(8,128)(2,1)S(1)}, bf16[4,128,128]{2,1,0:T(8,128)(2,1)S(1)}, u32[]{:S(2)}, u32[]{:S(2)}) collective-permute-start(bf16[4,128,128]{2,1,0:T(8,128)(2,1)S(1)} %pad_maximum_fusion.4), channel_id=1, source_target_pairs={{0,16},{4,20},{8,24},{12,28},{16,0},{20,4},{24,8},{28,12},{1,17},{... | collective-permute-start | bytes 393224 | tf_op jit(solution)/shard_map/ppermute | solution.py:459
  11.2 9.4 %collective-permute-start.3 = (bf16[4,128,128]{2,1,0:T(8,128)(2,1)S(1)}, bf16[4,128,128]{2,1,0:T(8,128)(2,1)S(1)}, u32[]{:S(2)}, u32[]{:S(2)}) collective-permute-start(bf16[4,128,128]{2,1,0:T(8,128)(2,1)S(1)} %pad_maximum_fusion.5), channel_id=1, source_target_pairs={{0,24},{4,28},{8,16},{12,20},{16,8},{20,12},{24,0},{28,4},{1,25},{... | collective-permute-start | bytes 393224 | tf_op jit(solution)/shard_map/ppermute | solution.py:459
  16.9 3.7 %collective-permute-start.6 = (bf16[4,2,128,128]{3,2,1,0:T(8,128)(2,1)S(1)}, bf16[4,2,128,128]{3,2,1,0:T(8,128)(2,1)S(1)}, u32[]{:S(2)}, u32[]{:S(2)}) collective-permute-start(bf16[4,2,128,128]{3,2,1,0:T(8,128)(2,1)S(1)} %pad_maximum_fusion.refs_4_), channel_id=1, source_target_pairs={{0,4},{4,0},{8,12},{12,8},{16,20},{20,16},{24,28},{28,24},{1,5},{5... | collective-permute-start | bytes 786440 | tf_op jit(solution)/shard_map/ppermute | solution.py:464
  17.0 10.4 %collective-permute-start.7 = (bf16[4,128,128]{2,1,0:T(8,128)(2,1)S(1)}, bf16[4,128,128]{2,1,0:T(8,128)(2,1)S(1)}, u32[]{:S(2)}, u32[]{:S(2)}) collective-permute-start(bf16[4,128,128]{2,1,0:T(8,128)(2,1)S(1)} %get-tuple-element.24), channel_id=1, source_target_pairs={{0,8},{4,12},{8,0},{12,4},{16,24},{20,28},{24,16},{28,20},{1,9},{5... | collective-permute-start | bytes 393224 | tf_op jit(solution)/shard_map/ppermute | solution.py:459
  17.8 9.7 %collective-permute-start.8 = (bf16[4,128,128]{2,1,0:T(8,128)(2,1)S(1)}, bf16[4,128,128]{2,1,0:T(8,128)(2,1)S(1)}, u32[]{:S(2)}, u32[]{:S(2)}) collective-permute-start(bf16[4,128,128]{2,1,0:T(8,128)(2,1)S(1)} %get-tuple-element.25), channel_id=1, source_target_pairs={{0,16},{4,20},{8,24},{12,28},{16,0},{20,4},{24,8},{28,12},{1,17},{... | collective-permute-start | bytes 393224 | tf_op jit(solution)/shard_map/ppermute | solution.py:459
  19.1 8.3 %collective-permute-start.9 = (bf16[4,128,128]{2,1,0:T(8,128)(2,1)S(1)}, bf16[4,128,128]{2,1,0:T(8,128)(2,1)S(1)}, u32[]{:S(2)}, u32[]{:S(2)}) collective-permute-start(bf16[4,128,128]{2,1,0:T(8,128)(2,1)S(1)} %get-tuple-element.26), channel_id=1, source_target_pairs={{0,24},{4,28},{8,16},{12,20},{16,8},{20,12},{24,0},{28,4},{1,25},{... | collective-permute-start | bytes 393224 | tf_op jit(solution)/shard_map/ppermute | solution.py:459
  29.6 9.9 %collective-permute-start.12 = (f32[8,128]{1,0:T(8,128)S(1)}, f32[8,128]{1,0:T(8,128)S(1)}, u32[]{:S(2)}, u32[]{:S(2)}) collective-permute-start(f32[8,128]{1,0:T(8,128)S(1)} %get-tuple-element.31), channel_id=1, source_target_pairs={{0,3},{1,2},{2,1},{3,0},{4,7},{5,6},{6,5},{7,4},{8,11},{9,10},{10,... | collective-permute-start | bytes 12296 | tf_op jit(solution)/shard_map/ppermute | solution.py:593
  33.2 6.3 %collective-permute-start.11 = (f32[8,128]{1,0:T(8,128)S(1)}, f32[8,128]{1,0:T(8,128)S(1)}, u32[]{:S(2)}, u32[]{:S(2)}) collective-permute-start(f32[8,128]{1,0:T(8,128)S(1)} %get-tuple-element.31), channel_id=1, source_target_pairs={{0,2},{1,3},{2,0},{3,1},{4,6},{5,7},{6,4},{7,5},{8,10},{9,11},{10,... | collective-permute-start | bytes 12296 | tf_op jit(solution)/shard_map/ppermute | solution.py:593
  33.2 6.3 %collective-permute-start.10 = (f32[8,128]{1,0:T(8,128)S(1)}, f32[8,128]{1,0:T(8,128)S(1)}, u32[]{:S(2)}, u32[]{:S(2)}) collective-permute-start(f32[8,128]{1,0:T(8,128)S(1)} %get-tuple-element.31), channel_id=1, source_target_pairs={{0,1},{1,0},{2,3},{3,2},{4,5},{5,4},{6,7},{7,6},{8,9},{9,8},{10,11... | collective-permute-start | bytes 12296 | tf_op jit(solution)/shard_map/ppermute | solution.py:593
